TPU v7x, 512 devices: a whole 4x8x8 slice. The times are simulated.
512 devices in a mesh: dp: 16 (over y_hi, x, core), tp: 32 (over z, y_lo).
Axes of the slice: x: 4, y: 8 (y_hi: 2, y_lo: 4; y = y_hi * 4 + y_lo), z: 8, core: 2. Of those that a mesh axis runs over, the one named last changes fastest.
Arguments:
- queries: bfloat16 [512, 128, 576], P(('dp', 'tp')), may hold values from -600 to 600
- latent_cache: bfloat16 [512, 1792, 576], P(('dp', 'tp')), may hold values from -17 to 17
- new_latent: bfloat16 [512, 576], P(('dp', 'tp')), may hold values from -8 to 8
- lengths: int32 [512], P(('dp', 'tp')), may hold values from 112 to 1792, as said below
- order: int32 [512], replicated, may hold values from 0 to 511, each once
- value_up: bfloat16 [128, 512, 128], P('tp'), may hold values from -0.25 to 0.25
- out_proj: bfloat16 [16384, 7168], P('tp', 'dp'), may hold values from -0.046875 to 0.046875
- residual: bfloat16 [512, 7168], P('tp', 'dp'), may hold values from -8 to 8
- norm_gain: bfloat16 [7168], P('dp'), may hold values from 0.099609375 to 1.8984375
- gate_weight: bfloat16 [7168, 18432], P('dp', 'tp'), may hold values from -0.0625 to 0.0625
- up_weight: bfloat16 [7168, 18432], P('dp', 'tp'), may hold values from -0.0625 to 0.0625
- down_weight: bfloat16 [18432, 7168], P('tp', 'dp'), may hold values from -0.046875 to 0.046875
Outputs:
- layer_out: bfloat16 [512, 7168], P('tp', 'dp')
Inputs may be any that keep to these rules, and one draw needn't show every extreme that they name: `lengths`: at least 2; some row uses all 1792 positions.
All inputs are finite; a program needn't handle non-finite values.
Results may differ from a plain program's by a relative error of at most 0.013.
Values may be sent and summed in bfloat16 or wider, within the bound.
No kernel may reach another device: no remote copies, remote signals or barrier semaphores. Data moves between devices by JAX's collectives and lax.ppermute only.
A program may use at most 64 MiB of HBM per device.

v0:
```python
import jax
import jax.numpy as jnp
from jax import lax
from jax.sharding import PartitionSpec as P

D = 7168
LAT = 512
ROPE = 64
HD = 128


def local(
    queries,
    latent_cache,
    new_latent,
    lengths,
    order,
    value_up,
    out_proj,
    residual,
    norm_gain,
    gate_weight,
    up_weight,
    down_weight,
):
    factor = (HD + ROPE) ** (-0.5)
    positions = latent_cache.shape[1]
    scores = (
        jnp.einsum("rhc,rpc->rhp", queries, latent_cache, preferred_element_type=jnp.float32)
        * factor
    )
    places = jnp.arange(positions)
    scores = jnp.where(places[None, None, :] < lengths[:, None, None], scores, -jnp.inf)
    own_score = (
        jnp.einsum("rhc,rc->rh", queries, new_latent, preferred_element_type=jnp.float32) * factor
    )
    highest = jnp.maximum(jnp.max(scores, axis=2), own_score)
    expo = jnp.exp(scores - highest[:, :, None])
    own_expo = jnp.exp(own_score - highest)
    total = jnp.sum(expo, axis=2) + own_expo
    probs = (expo / total[:, :, None]).astype(jnp.bfloat16)
    own_prob = (own_expo / total).astype(jnp.bfloat16)
    summed = jnp.einsum(
        "rhp,rpl->rhl", probs, latent_cache[:, :, :LAT], preferred_element_type=jnp.float32
    )
    summed = summed + own_prob.astype(jnp.float32)[:, :, None] * new_latent[:, None, :LAT].astype(
        jnp.float32
    )
    latent_out = summed.astype(jnp.bfloat16)
    owned = lax.all_to_all(latent_out, "tp", split_axis=1, concat_axis=0, tiled=True)
    head_values = jnp.einsum("rhl,hlv->rhv", owned, value_up, preferred_element_type=jnp.float32)
    head_values = head_values.astype(jnp.bfloat16).reshape(owned.shape[0], -1)
    attn_terms = jnp.dot(
        lax.all_gather(head_values, "dp", axis=0, tiled=True),
        out_proj,
        preferred_element_type=jnp.float32,
    )
    attn_own = lax.psum_scatter(attn_terms, "tp", scatter_dimension=0, tiled=True)
    mid = (residual.astype(jnp.float32) + attn_own).astype(jnp.bfloat16)
    mid_all = lax.all_gather(mid, "tp", axis=0, tiled=True)
    mid_wide = mid_all.astype(jnp.float32)
    squares = jnp.sum(mid_wide * mid_wide, axis=1)
    meansq = lax.psum(squares, "dp") / D
    scaled = mid_wide * lax.rsqrt(meansq + 1e-06)[:, None] * norm_gain.astype(jnp.float32)[None, :]
    normed = scaled.astype(jnp.bfloat16)
    gate_term = jnp.dot(normed, gate_weight, preferred_element_type=jnp.float32)
    up_term = jnp.dot(normed, up_weight, preferred_element_type=jnp.float32)
    gate, upper = lax.psum((gate_term, up_term), "dp")
    hidden = (jax.nn.silu(gate) * upper).astype(jnp.bfloat16)
    ffn_terms = jnp.dot(hidden, down_weight, preferred_element_type=jnp.float32)
    ordered_terms = jnp.take(ffn_terms, order, axis=0)
    ffn_own = lax.psum_scatter(ordered_terms, "tp", scatter_dimension=0, tiled=True)
    own_count = ffn_own.shape[0]
    wanted = lax.dynamic_slice_in_dim(order, lax.axis_index("tp") * own_count, own_count)
    mid_rows = jnp.take(mid_wide, wanted, axis=0)
    return (mid_rows + ffn_own).astype(jnp.bfloat16)


def solution(mesh):
    placed = (
        P(("dp", "tp"), None, None),
        P(("dp", "tp"), None, None),
        P(("dp", "tp"), None),
        P(("dp", "tp")),
        P(),
        P("tp", None, None),
        P("tp", "dp"),
        P("tp", "dp"),
        P("dp"),
        P("dp", "tp"),
        P("dp", "tp"),
        P("tp", "dp"),
    )
    return jax.shard_map(
        local, mesh=mesh, in_specs=placed, out_specs=P("tp", "dp"), check_vma=False
    )
```

profile of v0, /device:TPU:6, one launch (start us, length us, event | category | flops | bytes accessed | tf_op | source)
XLA Modules:
  0.0 717.5 jit_solution(2948268740065855127)
XLA Ops:
  7.3 0.7 slice_convert_fusion
  8.0 2.4 fusion.28
  10.4 0.1 fusion.29
  10.6 0.3 fusion.16
  10.9 0.8 fusion.11
  11.6 0.2 copy.33
  11.9 0.5 broadcast.50
  12.4 1.4 reduce.6
  13.8 0.1 reshape.120
  13.9 24.5 %all_to_all.12 = bf16[32,2,1024]{2,1,0:T(2,128)(2,1)S(1)} all-to-all(bf16[32,2,1024]{2,1,0:T(2,128)(2,1)S(1)} %reshape.120), channel_id=1, replica_groups=mesh['dp'=16,'tp'=32] {'tp'}, dimensions={0} | all-to-all | bytes 262144 | tf_op jit(solution)/shard_map/all_to_all | solution.py:50
  38.4 0.1 reshape.121
  38.5 0.7 bitcast_reduce_fusion
  39.3 0.2 fusion.14
  39.5 24.4 %all_gather.6 = bf16[512,512]{1,0:T(8,128)(2,1)S(1)} all-gather(bf16[32,512]{1,0:T(8,128)(2,1)S(1)} %bitcast.55), channel_id=1, replica_groups=mesh['dp'=16,'tp'=32] {'dp'}, dimensions={0}, use_global_device_ids=true | all-gather | bytes 557056 | tf_op jit(solution)/shard_map/all_gather | solution.py:54
  63.9 1.5 fusion.30
  65.4 160.5 %reduce-scatter.3.cloned.1.call-done = f32[16,448]{1,0:T(8,128)} async-done(((f32[512,448]{1,0:T(8,128)}), f32[16,448]{1,0:T(8,128)}) %reduce-scatter.3.cloned.1.call-update) | async-done | bytes 28688 | tf_op jit(solution)/shard_map/reduce_scatter | solution.py:58
  225.9 0.8 add_convert_fusion.1
  226.7 77.9 %all_gather.7 = bf16[512,448]{1,0:T(8,128)(2,1)S(1)} all-gather(bf16[16,448]{1,0:T(8,128)(2,1)S(1)} %add_convert_fusion.1), channel_id=1, replica_groups=mesh['dp'=16,'tp'=32] {'tp'}, dimensions={0}, use_global_device_ids=true | all-gather | bytes 473088 | tf_op jit(solution)/shard_map/all_gather | solution.py:60
  304.6 0.2 multiply_reduce_fusion
  304.8 38.1 %psum.21 = f32[512]{0:T(512)S(1)} all-reduce(f32[512]{0:T(512)S(1)} %multiply_reduce_fusion), channel_id=1, replica_groups=mesh['dp'=16,'tp'=32] {'dp'}, use_global_device_ids=true, to_apply=%region_4.5 | all-reduce | flops 512 | bytes 4096 | tf_op jit(solution)/shard_map/psum | solution.py:63
  342.9 1.7 fusion.20
  344.6 1.7 fusion.21
  346.3 0.6 copy-done.7
  346.9 189.9 %all-reduce.3.cloned.1.call-done = (f32[512,576]{0,1:T(8,128)}, f32[512,576]{0,1:T(8,128)}) async-done(((f32[512,576]{0,1:T(8,128)}, f32[512,576]{0,1:T(8,128)}), (f32[512,576]{0,1:T(8,128)}, f32[512,576]{0,1:T(8,128)})) %all-reduce.3.cloned.1.call-update) | async-done | bytes 2359312 | tf_op jit(solution)/shard_map/psum | solution.py:68
  536.9 2.3 fusion.17
  539.2 1.6 gather_fusion.1
  540.8 1.1 broadcast_select_fusion
  541.9 0.1 compare_and_fusion.1
  542.0 0.1 convert_element_type.67
  542.2 0.6 gather_fusion
  542.7 166.8 %reduce-scatter.5.cloned.1.call-done = f32[16,448]{1,0:T(8,128)} async-done(((f32[512,448]{1,0:T(8,128)}), f32[16,448]{1,0:T(8,128)}) %reduce-scatter.5.cloned.1.call-update) | async-done | bytes 28688 | tf_op jit(solution)/shard_map/reduce_scatter | solution.py:72
  709.6 1.4 add_convert_fusion
  (37 shorter events, 0.3 us)
Async XLA Ops:
  6.5 336.4 %copy-start = (bf16[448,576]{1,0:T(8,128)(2,1)S(1)}, bf16[448,576]{1,0:T(8,128)(2,1)}, u32[]{:S(2)}) copy-start(bf16[448,576]{1,0:T(8,128)(2,1)} %param.22) | copy-start | bytes 1548292
  6.5 219.4 %reduce-scatter.3.cloned.1.call-start = ((), (), s32[]{:S(2)}) async-start(), calls=%async_computation.3 | async-start | bytes 1081344 | tf_op jit(solution)/shard_map/reduce_scatter | solution.py:58
  8.0 2.4 copy-start.2
  8.0 2.5 copy-start.8
  8.0 2.9 copy-start.1
  11.6 27.7 %copy-start.4 = (bf16[4,512,128]{2,1,0:T(8,128)(2,1)S(1)}, bf16[4,512,128]{2,1,0:T(8,128)(2,1)}, u32[]{:S(2)}) copy-start(bf16[4,512,128]{2,1,0:T(8,128)(2,1)} %param.17) | copy-start | bytes 1572868
  38.4 25.5 %copy-start.5 = (bf16[512,448]{0,1:T(8,128)(2,1)S(1)}, bf16[512,448]{0,1:T(8,128)(2,1)}, u32[]{:S(2)}) copy-start(bf16[512,448]{0,1:T(8,128)(2,1)} %param.18) | copy-start | bytes 1376260
  63.9 1.5 copy-start.9
  63.9 162.0 %copy-start.6 = (bf16[16,448]{1,0:T(8,128)(2,1)S(1)}, bf16[16,448]{1,0:T(8,128)(2,1)}, u32[]{:S(2)}) copy-start(bf16[16,448]{1,0:T(8,128)(2,1)} %param.19) | copy-start | bytes 43012
  65.4 471.5 %all-reduce.3.cloned.1.call-start = ((), (), s32[]{:S(2)}) async-start(), calls=%async_computation.5 | async-start | bytes 4718592 | tf_op jit(solution)/shard_map/psum | solution.py:68
  304.8 39.8 %copy-start.3 = (bf16[448,576]{1,0:T(8,128)(2,1)S(1)}, bf16[448,576]{1,0:T(8,128)(2,1)}, u32[]{:S(2)}) copy-start(bf16[448,576]{1,0:T(8,128)(2,1)} %param.21) | copy-start | bytes 1548292
  346.2 0.7 copy-start.7
  346.2 190.6 %copy-start.10 = (bf16[576,448]{0,1:T(8,128)(2,1)S(1)}, bf16[576,448]{0,1:T(8,128)(2,1)}, u32[]{:S(2)}) copy-start(bf16[576,448]{0,1:T(8,128)(2,1)} %param.23) | copy-start | bytes 1548292
  346.3 363.3 %reduce-scatter.5.cloned.1.call-start = ((), (), s32[]{:S(2)}) async-start(), calls=%async_computation.4 | async-start | bytes 1081344 | tf_op jit(solution)/shard_map/reduce_scatter | solution.py:72
Sparse Core Ops, SparseCore 0:
  65.5 160.3 reduce-scatter.2
  346.4 190.4 all-reduce.2
  542.1 167.4 reduce-scatter.4
where the time goes:
time: 718 us
  waiting for transfers between devices  517 us (72%)
  blocking collectives  165 us (23%)
  between operations  14 us (2%)
  matrix products  10.6 us (1%)
    psum x1, waiting for transfers between devices, local(): gate, upper = lax.psum((gate_term, up_term), 'dp')  190 us
    reduce_scatter x1, waiting for transfers between devices, local(): lax.psum_scatter(ordered_terms, 'tp', scatter_dimension=0, tiled=True)  167 us
    reduce_scatter x1, waiting for transfers between devices, local(): lax.psum_scatter(attn_terms, 'tp', scatter_dimension=0, tiled=True)  160 us
    all_gather x1, blocking collectives, local(): mid_all = lax.all_gather(mid, 'tp', axis=0, tiled=True)  77.9 us
    psum x1, blocking collectives, local(): meansq = lax.psum(squares, 'dp') / D  38.1 us
    all_to_all x1, blocking collectives, local(): lax.all_to_all(latent_out, 'tp', split_axis=1, concat_axis=0, tiled=True)  24.5 us
    all_gather x1, blocking collectives, local(): lax.all_gather(head_values, 'dp', axis=0, tiled=True)  24.4 us
  transfers between devices with their start and end apart: 3, of which 3 were waited for; matrix products, arithmetic and copies ran while one was open for 0% of the time, Pallas kernels for 0%

commit v1 on v0

v1 whole, which is shorter than its diff:
```python
import jax
import jax.numpy as jnp
from jax import lax
from jax.experimental import pallas as pl
from jax.experimental.pallas import tpu as pltpu
from jax.sharding import PartitionSpec as P

D = 7168
LAT = 512
ROPE = 64
HD = 128
BF = jnp.bfloat16
F32 = jnp.float32


NT = (((1,), (1,)), ((), ()))
VMEM = pl.BlockSpec(memory_space=pltpu.VMEM)
SMEM = pl.BlockSpec(memory_space=pltpu.SMEM)


def call(kernel, out, specs, flops):
    return pl.pallas_call(
        kernel,
        out_shape=out,
        in_specs=specs,
        out_specs=VMEM,
        compiler_params=pltpu.CompilerParams(vmem_limit_bytes=24 * 2**20),
        cost_estimate=pl.CostEstimate(flops=flops, bytes_accessed=2**21, transcendentals=0),
    )


def attn_kernel(first_ref, heads_ref, w1_ref, w2_ref, res_ref, out_ref):
    weights = jnp.concatenate([w1_ref[...], w2_ref[...]], axis=0)
    terms = lax.dot_general(heads_ref[...], weights, NT, preferred_element_type=F32)
    rows, count = heads_ref.shape[0], res_ref.shape[0]
    at_row = lax.broadcasted_iota(jnp.int32, (rows, count), 0)
    at_res = lax.broadcasted_iota(jnp.int32, (rows, count), 1)
    here = jnp.where(at_row == at_res + first_ref[0], 1.0, 0.0).astype(BF)
    terms = terms + jnp.dot(here, res_ref[...], preferred_element_type=F32)
    out_ref[...] = terms.astype(BF)


def ff_kernel(mid_ref, gain_ref, g1_ref, g2_ref, u1_ref, u2_ref, out_ref):
    wide = mid_ref[...].astype(F32)
    squares = jnp.sum(wide * wide, axis=1, keepdims=True)
    high = squares.astype(BF).astype(F32)
    gained = (wide * gain_ref[...].astype(F32)).astype(BF)
    ff = g1_ref.shape[1]
    parts, rows, block = out_ref.shape[0], out_ref.shape[1], out_ref.shape[2] // 2
    for k, (a_ref, b_ref, extra) in enumerate(
        ((g1_ref, g2_ref, high), (u1_ref, u2_ref, squares - high))
    ):
        weights = jnp.concatenate([a_ref[...], b_ref[...]], axis=0)
        term = jnp.dot(gained, weights, preferred_element_type=F32)
        pad = jnp.broadcast_to(extra, (extra.shape[0], block - ff))
        term = jnp.concatenate([term, pad], axis=1)
        for q in range(parts):
            part = term[q * rows : (q + 1) * rows].astype(BF)
            out_ref[q, :, k * block : (k + 1) * block] = part


def down_kernel(order_ref, spots_ref, hidden_ref, w_ref, out_ref):
    pick = jnp.where(order_ref[...] == spots_ref[...], 1.0, 0.0).astype(BF)
    hidden = jnp.dot(pick, hidden_ref[...], preferred_element_type=F32).astype(BF)
    terms = lax.dot_general(hidden, w_ref[...], NT, preferred_element_type=F32)
    out_ref[...] = terms.astype(BF)


def exchange(array, axis, groups):
    return lax.all_to_all(
        array, axis, split_axis=0, concat_axis=0, axis_index_groups=groups, tiled=True
    )


def sum_scatter(terms, axis, count, groups=None):
    return add_blocks(exchange(terms, axis, groups), count)


def add_blocks(got, count):
    got = got.reshape((count, got.shape[0] // count) + got.shape[1:])
    return jnp.sum(got.astype(F32), axis=0)


def gather_rows(rows, axis, count, groups=None):
    copies = jnp.broadcast_to(rows[None], (count,) + rows.shape)
    got = exchange(copies, axis, groups)
    return got.reshape((count * rows.shape[0],) + rows.shape[1:])


def local(
    queries,
    latent_cache,
    new_latent,
    lengths,
    order,
    value_up,
    out_proj,
    residual,
    norm_gain,
    gate_weight,
    up_weight,
    down_weight,
    n_dp,
    n_tp,
):
    core = lax.rem(lax.axis_index("dp"), 2)
    swap = [(i, i ^ 1) for i in range(n_dp)]
    n_x = n_dp // 4
    tp = lax.axis_index("tp")

    def at(y, x, c):
        return (y * n_x + x) * 2 + c

    xs, two = range(n_x), range(2)
    along_x = [[at(y, x, c) for x in xs] for y in two for c in two]
    same_y = [[at(y, x, c) for x in xs for c in two] for y in two]
    across_y = [(i, (i + n_dp // 2) % n_dp) for i in range(n_dp)]
    out_proj2 = lax.ppermute(out_proj, "dp", swap)
    norm_gain2 = lax.ppermute(norm_gain, "dp", swap)
    residual2 = lax.ppermute(residual, "dp", swap)
    factor = (HD + ROPE) ** (-0.5)
    positions = latent_cache.shape[1]
    scores = (
        jnp.einsum("rhc,rpc->rhp", queries, latent_cache, preferred_element_type=jnp.float32)
        * factor
    )
    places = jnp.arange(positions)
    scores = jnp.where(places[None, None, :] < lengths[:, None, None], scores, -jnp.inf)
    own_score = (
        jnp.einsum("rhc,rc->rh", queries, new_latent, preferred_element_type=jnp.float32) * factor
    )
    highest = jnp.maximum(jnp.max(scores, axis=2), own_score)
    expo = jnp.exp(scores - highest[:, :, None])
    own_expo = jnp.exp(own_score - highest)
    total = jnp.sum(expo, axis=2) + own_expo
    probs = (expo / total[:, :, None]).astype(jnp.bfloat16)
    own_prob = (own_expo / total).astype(jnp.bfloat16)
    summed = jnp.einsum(
        "rhp,rpl->rhl", probs, latent_cache[:, :, :LAT], preferred_element_type=jnp.float32
    )
    summed = summed + own_prob.astype(jnp.float32)[:, :, None] * new_latent[:, None, :LAT].astype(
        jnp.float32
    )
    latent_out = summed.astype(jnp.bfloat16)
    both_y = [
        [at(y, x, c) * n_tp + j for y in two for j in range(n_tp)] for x in xs for c in two
    ]
    copies = jnp.broadcast_to(latent_out, (2,) + latent_out.shape[1:])
    copies = copies.reshape((2 * n_tp, -1, LAT))
    owned = exchange(copies, ("dp", "tp"), both_y)
    head_values = jnp.einsum("rhl,hlv->rhv", owned, value_up, preferred_element_type=jnp.float32)
    head_values = head_values.astype(jnp.bfloat16).reshape(owned.shape[0], -1)
    heads_set = gather_rows(head_values, "dp", n_x, along_x)
    places = jnp.arange(n_dp // 2 * n_tp)
    set_dp = (places // n_tp % 2 * n_x + places // (2 * n_tp)) * 2
    set_rows = set_dp * n_tp + places % n_tp
    count = residual.shape[0]
    res_row = tp * count
    res_dp = lax.div(res_row, n_tp)
    res_x, res_y = lax.rem(lax.div(res_dp, 2), n_x), lax.div(res_dp, 2 * n_x)
    first = (res_x * 2 + res_y) * n_tp + lax.rem(res_row, n_tp)
    first = jnp.where(lax.rem(res_dp, 2) == core, first, -count).reshape(1)
    res_pair = jnp.concatenate([residual, residual2], axis=1)
    attn_terms = call(
        attn_kernel,
        jax.ShapeDtypeStruct((heads_set.shape[0], res_pair.shape[1]), BF),
        [SMEM] + [VMEM] * 4,
        2 * heads_set.size * res_pair.shape[1],
    )(first, heads_set, out_proj.T, out_proj2.T, res_pair)
    width = residual.shape[1]
    attn_terms, gate_weight, up_weight = lax.optimization_barrier(
        (attn_terms, gate_weight, up_weight)
    )
    got = exchange(attn_terms, "tp", None)
    gate_weight2 = lax.ppermute(gate_weight, "dp", swap)
    up_weight2 = lax.ppermute(up_weight, "dp", swap)
    got, gate_weight2, up_weight2 = lax.optimization_barrier((got, gate_weight2, up_weight2))
    mid = add_blocks(got, n_tp).astype(BF)
    mid_set = gather_rows(mid, "tp", n_tp)
    mid_here, mid_there = mid_set[:, :width], mid_set[:, width:]
    gain = jnp.concatenate([norm_gain, norm_gain2])[None, :]
    ff = gate_weight.shape[1]
    block = (ff + 127) // 128 * 128
    terms = call(
        ff_kernel,
        jax.ShapeDtypeStruct((n_x, mid_set.shape[0] // n_x, 2 * block), BF),
        [VMEM] * 6,
        4 * mid_set.size * ff,
    )(mid_set, gain, gate_weight, gate_weight2, up_weight, up_weight2)
    terms, mid_there = lax.optimization_barrier((terms, mid_there))
    got = exchange(terms, "dp", along_x).reshape(-1, 2 * block)
    mid_rest = lax.ppermute(mid_there, "dp", swap)
    got, mid_rest = lax.optimization_barrier((got, mid_rest))
    sums = add_blocks(got, n_x)
    sums = sums + lax.ppermute(sums.astype(BF), "dp", across_y).astype(F32)
    meansq = (sums[:, ff] + sums[:, block + ff]) / D
    scale = lax.rsqrt(meansq + 1e-06)[:, None]
    gate = sums[:, :ff] * scale
    upper = sums[:, block : block + ff] * scale
    hidden = (jax.nn.silu(gate) * upper).astype(BF)
    hidden = gather_rows(hidden, "dp", n_x * 2, same_y)
    rows = hidden.shape[0]
    spots = jnp.arange(rows)
    spot_dp = at(spots // n_tp % 2, spots // (4 * n_tp), spots // (2 * n_tp) % 2)
    spot_rows = spot_dp * n_tp + spots % n_tp
    ffn_terms = call(
        down_kernel,
        jax.ShapeDtypeStruct((rows, down_weight.shape[1]), BF),
        [VMEM] * 4,
        2 * rows * ff * (rows + down_weight.shape[1]),
    )(order[:, None], spot_rows[None, :].astype(jnp.int32), hidden, down_weight.T)
    ffn_own = sum_scatter(ffn_terms, "tp", n_tp)
    own_count = ffn_own.shape[0]
    wanted = lax.dynamic_slice_in_dim(order, tp * own_count, own_count)
    pick1 = (wanted[:, None] == (set_rows + core * n_tp)[None, :]).astype(BF)
    pick2 = (wanted[:, None] == (set_rows + (1 - core) * n_tp)[None, :]).astype(BF)
    mid_rows = jnp.dot(pick1, mid_here, preferred_element_type=F32) + jnp.dot(
        pick2, mid_rest, preferred_element_type=F32
    )
    return (mid_rows + ffn_own).astype(BF)


def solution(mesh):
    n_dp, n_tp = mesh.shape["dp"], mesh.shape["tp"]

    def run(*args):
        return local(*args, n_dp=n_dp, n_tp=n_tp)

    placed = (
        P(("dp", "tp"), None, None),
        P(("dp", "tp"), None, None),
        P(("dp", "tp"), None),
        P(("dp", "tp")),
        P(),
        P("tp", None, None),
        P("tp", "dp"),
        P("tp", "dp"),
        P("dp"),
        P("dp", "tp"),
        P("dp", "tp"),
        P("tp", "dp"),
    )
    return jax.shard_map(
        run, mesh=mesh, in_specs=placed, out_specs=P("tp", "dp"), check_vma=False
    )
```

time: 718 us -> 161 us (0.22)
  waiting for transfers between devices: 517 us -> 80.9 us
  blocking collectives: 165 us -> 0 us
  starting transfers between devices: 0.09 us -> 61.5 us
  between operations: 14 us -> 1.06 us
    reduce_scatter x2 -> x0, waiting for transfers between devices: 327 us -> none  [the longest x1 167 us: local(): lax.psum_scatter(ordered_terms, 'tp', scatter_dimension=0, tiled=True)]
    psum x1 -> x0, waiting for transfers between devices: 190 us -> none  [local(): gate, upper = lax.psum((gate_term, up_term), 'dp')]
    all_gather x2 -> x0, blocking collectives: 102 us -> none  [the longest x1 77.9 us: local(): mid_all = lax.all_gather(mid, 'tp', axis=0, tiled=True)]
    all_to_all x0 -> x7, waiting for transfers between devices: none -> 65.9 us  [exchange(): lax.all_to_all(array, axis, split_axis=0, concat_axis=0, axis_index_group...]
    all_to_all x0 -> x7, starting transfers between devices: none -> 45.2 us  [exchange(): lax.all_to_all(array, axis, split_axis=0, concat_axis=0, axis_index_group...]
    psum x1 -> x0, blocking collectives: 38.1 us -> none  [local(): meansq = lax.psum(squares, 'dp') / D]
    all_to_all x1 -> x0, blocking collectives: 24.5 us -> none  [local(): lax.all_to_all(latent_out, 'tp', split_axis=1, concat_axis=0, tiled=True)]
    ppermute x0 -> x7, starting transfers between devices: none -> 16.3 us  [the longest x1 4.31 us: local(): sums = sums + lax.ppermute(sums.astype(BF), 'dp', across_y).astype(F32)]
  transfers between devices with their start and end apart: 3 -> 14, of which waited for: 3 -> 12; matrix products, arithmetic and copies ran while one was open for 0% -> 1% of each run, Pallas kernels for 0% -> 0%
where the time goes in v1:
time: 161 us; the launch traced here: 158 us
  waiting for transfers between devices  80.9 us (50%)
  starting transfers between devices  61.5 us (38%)
  Pallas kernels  4.96 us (3%)
  matrix products  4.51 us (3%)
  local copies, waits for them, and re-layouts  3.63 us (2%)
  other arithmetic  1.82 us (1%)
    all_to_all x7, waiting for transfers between devices, exchange(): lax.all_to_all(array, axis, split_axis=0, concat_axis=0, axis_index_group...  65.9 us
    all_to_all x7, starting transfers between devices, exchange(): lax.all_to_all(array, axis, split_axis=0, concat_axis=0, axis_index_group...  45.2 us
    ppermute x1, waiting for transfers between devices, local(): sums = sums + lax.ppermute(sums.astype(BF), 'dp', across_y).astype(F32)  9.78 us
    ppermute x1, starting transfers between devices, local(): sums = sums + lax.ppermute(sums.astype(BF), 'dp', across_y).astype(F32)  4.31 us
  transfers between devices with their start and end apart: 14, of which 12 were waited for; matrix products, arithmetic and copies ran while one was open for 1% of the time, Pallas kernels for 0%

profile of v1, /device:TPU:6, one launch (start us, length us, event | category | flops | bytes accessed | tf_op | source)
XLA Modules:
  0.0 158.4 jit_solution(16569891601223602394)
XLA Ops:
  1.4 2.4 %fusion.54 = (f32[128]{0:T(128)S(1)}, f32[128,1792]{1,0:T(8,128)S(1)}) fusion(bf16[1,1792,576]{1,2,0:T(8,128)(2,1)} %param.13, bf16[1,128,576]{1,2,0:T(8,128)(2,1)} %param.12, pred[1792]{0:T(1024)(128)(4,1)S(1)} %iota_compare_fusion), kind=kOutput, calls=%fused_computation.100 | convolution fusion | flops 264929152 | bytes 3131648 | tf_op jit(solution)/shard_map/rhc,rpc->rhp/dot_general | solution.py:124
  5.9 16.6 %all-to-all-start = ((bf16[64,4,512]{2,1,0:T(4,128)(2,1)}), bf16[64,4,512]{2,1,0:T(4,128)(2,1)S(1)}, u32[]{:S(2)}, u32[]{:S(2)}) async-start(bf16[64,4,512]{2,1,0:T(4,128)(2,1)} %reshape.342), calls=%async_computation | async-start | bytes 524288 | tf_op jit(solution)/shard_map/all_to_all | solution.py:70
  22.5 1.9 %collective-permute-start = (bf16[512,448]{0,1:T(8,128)(2,1)S(1)}, bf16[512,448]{0,1:T(8,128)(2,1)S(1)}, u32[]{:S(2)}, u32[]{:S(2)}) collective-permute-start(bf16[512,448]{0,1:T(8,128)(2,1)S(1)} %copy-done.3), channel_id=1, source_target_pairs={{0,32},{32,0},{64,96},{96,64},{128,160},{160,128},{192,224},{224,1... | collective-permute-start | bytes 1376264 | tf_op jit(solution)/shard_map/ppermute | solution.py:118
  24.4 13.1 %all-to-all-done = bf16[64,4,512]{2,1,0:T(4,128)(2,1)S(1)} async-done(((bf16[64,4,512]{2,1,0:T(4,128)(2,1)}), bf16[64,4,512]{2,1,0:T(4,128)(2,1)S(1)}, u32[]{:S(2)}, u32[]{:S(2)}) %all-to-all-start) | async-done | bytes 262176 | tf_op jit(solution)/shard_map/all_to_all | solution.py:70
  38.5 4.8 %all-to-all-start.1 = ((bf16[4,64,512]{2,1,0:T(8,128)(2,1)}), bf16[4,64,512]{2,1,0:T(8,128)(2,1)S(1)}, u32[]{:S(2)}, u32[]{:S(2)}) async-start(bf16[4,64,512]{2,1,0:T(8,128)(2,1)} %broadcast_in_dim.30), calls=%async_computation.1 | async-start | bytes 524288 | tf_op jit(solution)/shard_map/all_to_all | solution.py:70
  43.3 1.9 %collective-permute-start.1 = (bf16[16,448]{1,0:T(8,128)(2,1)S(1)}, bf16[16,448]{1,0:T(8,128)(2,1)S(1)}, u32[]{:S(2)}, u32[]{:S(2)}) collective-permute-start(bf16[16,448]{1,0:T(8,128)(2,1)S(1)} %copy-done.7), channel_id=1, source_target_pairs={{0,32},{32,0},{64,96},{96,64},{128,160},{160,128},{192,224},{224,1... | collective-permute-start | bytes 43016 | tf_op jit(solution)/shard_map/ppermute | solution.py:120
  45.2 1.1 collective-permute-done.1
  46.4 1.5 all-to-all-done.1
  47.9 1.3 shard_map.118
  49.2 3.9 %all-to-all-start.2 = ((bf16[32,8,896]{2,1,0:T(8,128)(2,1)}), bf16[32,8,896]{2,1,0:T(8,128)(2,1)S(1)}, u32[]{:S(2)}, u32[]{:S(2)}) async-start(bf16[32,8,896]{2,1,0:T(8,128)(2,1)} %bitcast.11), calls=%async_computation.2 | async-start | bytes 917504 | tf_op jit(solution)/shard_map/all_to_all | solution.py:70
  53.1 1.9 %collective-permute-start.2 = (bf16[448,576]{1,0:T(8,128)(2,1)S(1)}, bf16[448,576]{1,0:T(8,128)(2,1)S(1)}, u32[]{:S(2)}, u32[]{:S(2)}) collective-permute-start(bf16[448,576]{1,0:T(8,128)(2,1)S(1)} %copy-done.1), channel_id=1, source_target_pairs={{0,32},{32,0},{64,96},{96,64},{128,160},{160,128},{192,224},{224,1... | collective-permute-start | bytes 1548296 | tf_op jit(solution)/shard_map/ppermute | solution.py:175
  55.1 2.4 %collective-permute-start.3 = (bf16[448,576]{1,0:T(8,128)(2,1)S(1)}, bf16[448,576]{1,0:T(8,128)(2,1)S(1)}, u32[]{:S(2)}, u32[]{:S(2)}) collective-permute-start(bf16[448,576]{1,0:T(8,128)(2,1)S(1)} %copy-done.2), channel_id=1, source_target_pairs={{0,32},{32,0},{64,96},{96,64},{128,160},{160,128},{192,224},{224,1... | collective-permute-start | bytes 1548296 | tf_op jit(solution)/shard_map/ppermute | solution.py:176
  57.5 1.6 collective-permute-done.3.u2_ref
  59.1 9.2 %all-to-all-done.2 = bf16[32,8,896]{2,1,0:T(8,128)(2,1)S(1)} async-done(((bf16[32,8,896]{2,1,0:T(8,128)(2,1)}), bf16[32,8,896]{2,1,0:T(8,128)(2,1)S(1)}, u32[]{:S(2)}, u32[]{:S(2)}) %all-to-all-start.2) | async-done | bytes 458784 | tf_op jit(solution)/shard_map/all_to_all | solution.py:70
  68.3 0.8 broadcast_in_dim.31
  69.1 4.7 %all-to-all-start.3 = ((bf16[32,8,896]{2,1,0:T(8,128)(2,1)}), bf16[32,8,896]{2,1,0:T(8,128)(2,1)S(1)}, u32[]{:S(2)}, u32[]{:S(2)}) async-start(bf16[32,8,896]{2,1,0:T(8,128)(2,1)} %broadcast_in_dim.31), calls=%async_computation.3 | async-start | bytes 917504 | tf_op jit(solution)/shard_map/all_to_all | solution.py:70
  73.9 1.9 %collective-permute-start.4 = (bf16[448]{0:T(512)(128)(2,1)S(1)}, bf16[448]{0:T(512)(128)(2,1)S(1)}, u32[]{:S(2)}, u32[]{:S(2)}) collective-permute-start(bf16[448]{0:T(512)(128)(2,1)S(1)} %copy-done.10), channel_id=1, source_target_pairs={{0,32},{32,0},{64,96},{96,64},{128,160},{160,128},{192,224},{224,1... | collective-permute-start | bytes 2696 | tf_op jit(solution)/shard_map/ppermute | solution.py:119
  75.8 1.1 collective-permute-done.4
  77.0 12.6 %all-to-all-done.3 = bf16[32,8,896]{2,1,0:T(8,128)(2,1)S(1)} async-done(((bf16[32,8,896]{2,1,0:T(8,128)(2,1)}), bf16[32,8,896]{2,1,0:T(8,128)(2,1)S(1)}, u32[]{:S(2)}, u32[]{:S(2)}) %all-to-all-start.3) | async-done | bytes 458784 | tf_op jit(solution)/shard_map/all_to_all | solution.py:70
  89.8 1.8 %shard_map.119 = bf16[4,64,1280]{2,1,0:T(8,128)(2,1)} custom-call(bf16[256,896]{1,0:T(8,128)(2,1)S(1)} %bitcast.58, bf16[1,896]{1,0:T(2,128)(2,1)S(1)} %broadcast_in_dim.32.gain_ref, bf16[448,576]{1,0:T(8,128)(2,1)S(1)} %copy-done.1, bf16[448,576]{1,0:T(8,128)(2,1)S(1)} %collective-permute-done.2.g2_ref, bf16[448,576]{1,0:T(8,128)(2,1)S(1)} %copy-done.2, ...), custom_call_target="tpu_custom_call" | custom-call | flops 528482304 | bytes 2097152 | tf_op jit(solution)/shard_map/pallas_call | solution.py:184
  91.6 4.8 %all-to-all-start.4 = ((bf16[4,64,1280]{2,1,0:T(8,128)(2,1)}), bf16[4,64,1280]{2,1,0:T(8,128)(2,1)S(1)}, u32[]{:S(2)}, u32[]{:S(2)}) async-start(bf16[4,64,1280]{2,1,0:T(8,128)(2,1)} %shard_map.119), calls=%async_computation.4 | async-start | bytes 1310720 | tf_op jit(solution)/shard_map/all_to_all | solution.py:70
  96.4 1.9 %collective-permute-start.5 = (bf16[256,448]{1,0:T(8,128)(2,1)S(1)}, bf16[256,448]{1,0:T(8,128)(2,1)S(1)}, u32[]{:S(2)}, u32[]{:S(2)}) collective-permute-start(bf16[256,448]{1,0:T(8,128)(2,1)S(1)} %slice.33), channel_id=1, source_target_pairs={{0,32},{32,0},{64,96},{96,64},{128,160},{160,128},{192,224},{224,1... | collective-permute-start | bytes 688136 | tf_op jit(solution)/shard_map/ppermute | solution.py:192
  98.3 1.5 collective-permute-done.5
  99.8 3.3 %all-to-all-done.4 = bf16[4,64,1280]{2,1,0:T(8,128)(2,1)S(1)} async-done(((bf16[4,64,1280]{2,1,0:T(8,128)(2,1)}), bf16[4,64,1280]{2,1,0:T(8,128)(2,1)S(1)}, u32[]{:S(2)}, u32[]{:S(2)}) %all-to-all-start.4) | async-done | bytes 655392 | tf_op jit(solution)/shard_map/all_to_all | solution.py:70
  103.2 4.3 %collective-permute-start.6 = (bf16[64,1280]{1,0:T(8,128)(2,1)S(1)}, bf16[64,1280]{1,0:T(8,128)(2,1)S(1)}, u32[]{:S(2)}, u32[]{:S(2)}) collective-permute-start(bf16[64,1280]{1,0:T(8,128)(2,1)S(1)} %convert_element_type.68), channel_id=1, source_target_pairs={{0,256},{32,288},{64,320},{96,352},{128,384},{160,416},{192,448},{... | collective-permute-start | bytes 491528 | tf_op jit(solution)/shard_map/ppermute | solution.py:195
  107.5 9.8 %collective-permute-done.6 = bf16[64,1280]{1,0:T(8,128)(2,1)S(1)} collective-permute-done((bf16[64,1280]{1,0:T(8,128)(2,1)S(1)}, bf16[64,1280]{1,0:T(8,128)(2,1)S(1)}, u32[]{:S(2)}, u32[]{:S(2)}) %collective-permute-start.6) | collective-permute-done | bytes 163872 | tf_op jit(solution)/shard_map/ppermute | solution.py:195
  117.7 0.9 broadcast_in_dim.34
  118.6 4.5 %all-to-all-start.5 = ((bf16[8,64,576]{2,1,0:T(8,128)(2,1)}), bf16[8,64,576]{2,1,0:T(8,128)(2,1)S(1)}, u32[]{:S(2)}, u32[]{:S(2)}) async-start(bf16[8,64,576]{2,1,0:T(8,128)(2,1)} %broadcast_in_dim.34), calls=%async_computation.5 | async-start | bytes 1310720 | tf_op jit(solution)/shard_map/all_to_all | solution.py:70
  123.3 9.5 %all-to-all-done.5 = bf16[8,64,576]{2,1,0:T(8,128)(2,1)S(1)} async-done(((bf16[8,64,576]{2,1,0:T(8,128)(2,1)}), bf16[8,64,576]{2,1,0:T(8,128)(2,1)S(1)}, u32[]{:S(2)}, u32[]{:S(2)}) %all-to-all-start.5) | async-done | bytes 589856 | tf_op jit(solution)/shard_map/all_to_all | solution.py:70
  132.8 1.8 %shard_map.120 = bf16[512,448]{1,0:T(8,128)(2,1)} custom-call(s32[512,1]{1,0:T(8,128)S(1)} %copy.23.order_ref, s32[1,512]{1,0:T(1,128)S(1)} %fusion.36.spots_ref, bf16[512,576]{1,0:T(8,128)(2,1)S(1)} %bitcast.61, bf16[448,576]{1,0:T(8,128)(2,1)S(1)} %bitcast.64), custom_call_target="tpu_custom_call" | custom-call | flops 566231040 | bytes 2097152 | tf_op jit(solution)/shard_map/pallas_call | solution.py:206
  134.6 5.9 %all-to-all-start.6 = ((bf16[32,16,448]{2,1,0:T(8,128)(2,1)}), bf16[32,16,448]{2,1,0:T(8,128)(2,1)S(1)}, u32[]{:S(2)}, u32[]{:S(2)}) async-start(bf16[32,16,448]{2,1,0:T(8,128)(2,1)} %bitcast.20), calls=%async_computation.6 | async-start | bytes 1048576 | tf_op jit(solution)/shard_map/all_to_all | solution.py:70
  140.8 16.7 %all-to-all-done.6 = bf16[32,16,448]{2,1,0:T(8,128)(2,1)S(1)} async-done(((bf16[32,16,448]{2,1,0:T(8,128)(2,1)}), bf16[32,16,448]{2,1,0:T(8,128)(2,1)S(1)}, u32[]{:S(2)}, u32[]{:S(2)}) %all-to-all-start.6) | async-done | bytes 458784 | tf_op jit(solution)/shard_map/all_to_all | solution.py:70
  (53 shorter events, 5.8 us)
Async XLA Ops:
  0.0 37.5 %copy-start = (bf16[4,512,128]{2,1,0:T(8,128)(2,1)S(1)}, bf16[4,512,128]{2,1,0:T(8,128)(2,1)}, u32[]{:S(2)}) copy-start(bf16[4,512,128]{2,1,0:T(8,128)(2,1)} %param.17) | copy-start | bytes 1572868
  0.0 3.9 %copy-start.8 = (bf16[1,576]{1,0:T(2,128)(2,1)S(1)}, bf16[1,576]{1,0:T(2,128)(2,1)}, u32[]{:S(2)}) copy-start(bf16[1,576]{1,0:T(2,128)(2,1)} %param.14) | copy-start | bytes 3460
  0.0 3.9 %copy-start.6 = (bf16[1,128,576]{1,2,0:T(8,128)(2,1)S(1)}, bf16[1,128,576]{1,2,0:T(8,128)(2,1)}, u32[]{:S(2)}) copy-start(bf16[1,128,576]{1,2,0:T(8,128)(2,1)} %param.12) | copy-start | bytes 442372
  1.4 2.9 %copy-start.5 = (bf16[1,1792,576]{1,2,0:T(8,128)(2,1)S(1)}, bf16[1,1792,576]{1,2,0:T(8,128)(2,1)}, u32[]{:S(2)}) copy-start(bf16[1,1792,576]{1,2,0:T(8,128)(2,1)} %param.13) | copy-start | bytes 6193156
  4.3 18.2 %copy-start.3 = (bf16[512,448]{0,1:T(8,128)(2,1)S(1)}, bf16[512,448]{0,1:T(8,128)(2,1)}, u32[]{:S(2)}) copy-start(bf16[512,448]{0,1:T(8,128)(2,1)} %param.18) | copy-start | bytes 1376260
  5.1 38.2 %copy-start.7 = (bf16[16,448]{1,0:T(8,128)(2,1)S(1)}, bf16[16,448]{1,0:T(8,128)(2,1)}, u32[]{:S(2)}) copy-start(bf16[16,448]{1,0:T(8,128)(2,1)} %param.19) | copy-start | bytes 43012
  5.9 31.6 %all-to-all-start = ((bf16[64,4,512]{2,1,0:T(4,128)(2,1)}), bf16[64,4,512]{2,1,0:T(4,128)(2,1)S(1)}, u32[]{:S(2)}, u32[]{:S(2)}) async-start(bf16[64,4,512]{2,1,0:T(4,128)(2,1)} %reshape.342), calls=%async_computation | async-start | bytes 524288 | tf_op jit(solution)/shard_map/all_to_all | solution.py:70
  22.5 23.9 %collective-permute-start = (bf16[512,448]{0,1:T(8,128)(2,1)S(1)}, bf16[512,448]{0,1:T(8,128)(2,1)S(1)}, u32[]{:S(2)}, u32[]{:S(2)}) collective-permute-start(bf16[512,448]{0,1:T(8,128)(2,1)S(1)} %copy-done.3), channel_id=1, source_target_pairs={{0,32},{32,0},{64,96},{96,64},{128,160},{160,128},{192,224},{224,1... | collective-permute-start | bytes 1376264 | tf_op jit(solution)/shard_map/ppermute | solution.py:118
  37.8 15.4 %copy-start.1 = (bf16[448,576]{1,0:T(8,128)(2,1)S(1)}, bf16[448,576]{1,0:T(8,128)(2,1)}, u32[]{:S(2)}) copy-start(bf16[448,576]{1,0:T(8,128)(2,1)} %g1_ref) | copy-start | bytes 1548292
  37.8 17.3 %copy-start.2 = (bf16[448,576]{1,0:T(8,128)(2,1)S(1)}, bf16[448,576]{1,0:T(8,128)(2,1)}, u32[]{:S(2)}) copy-start(bf16[448,576]{1,0:T(8,128)(2,1)} %u1_ref) | copy-start | bytes 1548292
  38.5 9.4 %all-to-all-start.1 = ((bf16[4,64,512]{2,1,0:T(8,128)(2,1)}), bf16[4,64,512]{2,1,0:T(8,128)(2,1)S(1)}, u32[]{:S(2)}, u32[]{:S(2)}) async-start(bf16[4,64,512]{2,1,0:T(8,128)(2,1)} %broadcast_in_dim.30), calls=%async_computation.1 | async-start | bytes 524288 | tf_op jit(solution)/shard_map/all_to_all | solution.py:70
  43.3 3.1 %collective-permute-start.1 = (bf16[16,448]{1,0:T(8,128)(2,1)S(1)}, bf16[16,448]{1,0:T(8,128)(2,1)S(1)}, u32[]{:S(2)}, u32[]{:S(2)}) collective-permute-start(bf16[16,448]{1,0:T(8,128)(2,1)S(1)} %copy-done.7), channel_id=1, source_target_pairs={{0,32},{32,0},{64,96},{96,64},{128,160},{160,128},{192,224},{224,1... | collective-permute-start | bytes 43016 | tf_op jit(solution)/shard_map/ppermute | solution.py:120
  47.9 26.0 %copy-start.10 = (bf16[448]{0:T(512)(128)(2,1)S(1)}, bf16[448]{0:T(512)(128)(2,1)}, u32[]{:S(2)}) copy-start(bf16[448]{0:T(512)(128)(2,1)} %param.20) | copy-start | bytes 2692
  49.2 19.0 %all-to-all-start.2 = ((bf16[32,8,896]{2,1,0:T(8,128)(2,1)}), bf16[32,8,896]{2,1,0:T(8,128)(2,1)S(1)}, u32[]{:S(2)}, u32[]{:S(2)}) async-start(bf16[32,8,896]{2,1,0:T(8,128)(2,1)} %bitcast.11), calls=%async_computation.2 | async-start | bytes 917504 | tf_op jit(solution)/shard_map/all_to_all | solution.py:70
  53.1 4.4 %collective-permute-start.2 = (bf16[448,576]{1,0:T(8,128)(2,1)S(1)}, bf16[448,576]{1,0:T(8,128)(2,1)S(1)}, u32[]{:S(2)}, u32[]{:S(2)}) collective-permute-start(bf16[448,576]{1,0:T(8,128)(2,1)S(1)} %copy-done.1), channel_id=1, source_target_pairs={{0,32},{32,0},{64,96},{96,64},{128,160},{160,128},{192,224},{224,1... | collective-permute-start | bytes 1548296 | tf_op jit(solution)/shard_map/ppermute | solution.py:175
  55.1 4.0 %collective-permute-start.3 = (bf16[448,576]{1,0:T(8,128)(2,1)S(1)}, bf16[448,576]{1,0:T(8,128)(2,1)S(1)}, u32[]{:S(2)}, u32[]{:S(2)}) collective-permute-start(bf16[448,576]{1,0:T(8,128)(2,1)S(1)} %copy-done.2), channel_id=1, source_target_pairs={{0,32},{32,0},{64,96},{96,64},{128,160},{160,128},{192,224},{224,1... | collective-permute-start | bytes 1548296 | tf_op jit(solution)/shard_map/ppermute | solution.py:176
  69.1 20.5 %all-to-all-start.3 = ((bf16[32,8,896]{2,1,0:T(8,128)(2,1)}), bf16[32,8,896]{2,1,0:T(8,128)(2,1)S(1)}, u32[]{:S(2)}, u32[]{:S(2)}) async-start(bf16[32,8,896]{2,1,0:T(8,128)(2,1)} %broadcast_in_dim.31), calls=%async_computation.3 | async-start | bytes 917504 | tf_op jit(solution)/shard_map/all_to_all | solution.py:70
  73.9 3.0 %collective-permute-start.4 = (bf16[448]{0:T(512)(128)(2,1)S(1)}, bf16[448]{0:T(512)(128)(2,1)S(1)}, u32[]{:S(2)}, u32[]{:S(2)}) collective-permute-start(bf16[448]{0:T(512)(128)(2,1)S(1)} %copy-done.10), channel_id=1, source_target_pairs={{0,32},{32,0},{64,96},{96,64},{128,160},{160,128},{192,224},{224,1... | collective-permute-start | bytes 2696 | tf_op jit(solution)/shard_map/ppermute | solution.py:119
  91.6 11.5 %all-to-all-start.4 = ((bf16[4,64,1280]{2,1,0:T(8,128)(2,1)}), bf16[4,64,1280]{2,1,0:T(8,128)(2,1)S(1)}, u32[]{:S(2)}, u32[]{:S(2)}) async-start(bf16[4,64,1280]{2,1,0:T(8,128)(2,1)} %shard_map.119), calls=%async_computation.4 | async-start | bytes 1310720 | tf_op jit(solution)/shard_map/all_to_all | solution.py:70
  96.4 3.4 %collective-permute-start.5 = (bf16[256,448]{1,0:T(8,128)(2,1)S(1)}, bf16[256,448]{1,0:T(8,128)(2,1)S(1)}, u32[]{:S(2)}, u32[]{:S(2)}) collective-permute-start(bf16[256,448]{1,0:T(8,128)(2,1)S(1)} %slice.33), channel_id=1, source_target_pairs={{0,32},{32,0},{64,96},{96,64},{128,160},{160,128},{192,224},{224,1... | collective-permute-start | bytes 688136 | tf_op jit(solution)/shard_map/ppermute | solution.py:192
  103.2 20.0 %copy-start.9 = (s32[512]{0:T(512)S(1)}, s32[512]{0:T(512)}, u32[]{:S(2)}) copy-start(s32[512]{0:T(512)} %param.16) | copy-start | bytes 6148
  103.2 29.6 %copy-start.4 = (bf16[576,448]{0,1:T(8,128)(2,1)S(1)}, bf16[576,448]{0,1:T(8,128)(2,1)}, u32[]{:S(2)}) copy-start(bf16[576,448]{0,1:T(8,128)(2,1)} %param.23) | copy-start | bytes 1548292
  103.2 14.1 %collective-permute-start.6 = (bf16[64,1280]{1,0:T(8,128)(2,1)S(1)}, bf16[64,1280]{1,0:T(8,128)(2,1)S(1)}, u32[]{:S(2)}, u32[]{:S(2)}) collective-permute-start(bf16[64,1280]{1,0:T(8,128)(2,1)S(1)} %convert_element_type.68), channel_id=1, source_target_pairs={{0,256},{32,288},{64,320},{96,352},{128,384},{160,416},{192,448},{... | collective-permute-start | bytes 491528 | tf_op jit(solution)/shard_map/ppermute | solution.py:195
  118.6 14.2 %all-to-all-start.5 = ((bf16[8,64,576]{2,1,0:T(8,128)(2,1)}), bf16[8,64,576]{2,1,0:T(8,128)(2,1)S(1)}, u32[]{:S(2)}, u32[]{:S(2)}) async-start(bf16[8,64,576]{2,1,0:T(8,128)(2,1)} %broadcast_in_dim.34), calls=%async_computation.5 | async-start | bytes 1310720 | tf_op jit(solution)/shard_map/all_to_all | solution.py:70
  134.6 22.9 %all-to-all-start.6 = ((bf16[32,16,448]{2,1,0:T(8,128)(2,1)}), bf16[32,16,448]{2,1,0:T(8,128)(2,1)S(1)}, u32[]{:S(2)}, u32[]{:S(2)}) async-start(bf16[32,16,448]{2,1,0:T(8,128)(2,1)} %bitcast.20), calls=%async_computation.6 | async-start | bytes 1048576 | tf_op jit(solution)/shard_map/all_to_all | solution.py:70

commit v2 on v1

--- a/solution.py
+++ b/solution.py
@@ -59,11 +59,71 @@
             out_ref[q, :, k * block : (k + 1) * block] = part
 
 
-def down_kernel(order_ref, spots_ref, hidden_ref, w_ref, out_ref):
-    pick = jnp.where(order_ref[...] == spots_ref[...], 1.0, 0.0).astype(BF)
-    hidden = jnp.dot(pick, hidden_ref[...], preferred_element_type=F32).astype(BF)
-    terms = lax.dot_general(hidden, w_ref[...], NT, preferred_element_type=F32)
-    out_ref[...] = terms.astype(BF)
+def down_kernel(pick_ref, hidden_ref, w_ref, out_ref):
+    half = out_ref.shape[0]
+    hidden = hidden_ref[...]
+    parts = []
+    for k in range(2):
+        pick = pick_ref[k * half : (k + 1) * half]
+        rows = jnp.dot(pick, hidden, preferred_element_type=F32).astype(BF)
+        parts.append(lax.dot_general(rows, w_ref[...], NT, preferred_element_type=F32))
+    out_ref[...] = jnp.concatenate(parts, axis=1).astype(BF)
+
+
+def mid_kernel(got_ref, out_ref):
+    total = got_ref[0].astype(F32)
+    for k in range(1, got_ref.shape[0]):
+        total = total + got_ref[k].astype(F32)
+    total = total.astype(BF)
+    for k in range(out_ref.shape[0]):
+        out_ref[k] = total
+
+
+def hidden_kernel(mine_ref, theirs_ref, out_ref):
+    sums = mine_ref[...] + theirs_ref[...].astype(F32)
+    ff, block = out_ref.shape[2], sums.shape[1] // 2
+    meansq = (sums[:, ff : ff + 1] + sums[:, block + ff : block + ff + 1]) / D
+    scale = lax.rsqrt(meansq + 1e-06)
+    gate = sums[:, :ff] * scale
+    upper = sums[:, block : block + ff] * scale
+    hidden = (gate / (1.0 + jnp.exp(-gate)) * upper).astype(BF)
+    for q in range(out_ref.shape[0]):
+        out_ref[q] = hidden
+
+
+def attend_kernel(length_ref, queries_ref, new_ref, cache_ref, out_ref, held, sems):
+    positions, piece = cache_ref.shape[1], 512
+    copies = []
+    for k, start in enumerate(range(0, positions, piece)):
+        at = (slice(None), pl.ds(start, min(piece, positions - start)))
+        copies.append(pltpu.make_async_copy(cache_ref.at[at], held.at[at], sems.at[k]))
+        copies[-1].start()
+    factor = (HD + ROPE) ** (-0.5)
+    queries = queries_ref[...].T
+    new = new_ref[...].astype(F32)
+    own = jnp.sum(queries.astype(F32) * new, axis=1, keepdims=True) * factor
+    scores, highest = [], own
+    for k, start in enumerate(range(0, positions, piece)):
+        size = min(piece, positions - start)
+        copies[k].wait()
+        part = jnp.dot(queries, held[:, start : start + size], preferred_element_type=F32)
+        place = lax.broadcasted_iota(jnp.int32, (1, size), 1) + start
+        part = jnp.where(place < length_ref[0], part * factor, -jnp.inf)
+        scores.append(part)
+        highest = jnp.maximum(highest, jnp.max(part, axis=1, keepdims=True))
+    total = jnp.exp(own - highest)
+    expos = [jnp.exp(part - highest) for part in scores]
+    for expo in expos:
+        total = total + jnp.sum(expo, axis=1, keepdims=True)
+    share = 1.0 / total
+    own = (jnp.exp(own - highest) * share).astype(BF).astype(F32)
+    probs = jnp.concatenate([(expo * share).astype(BF) for expo in expos], axis=1)
+    latent = lax.dot_general(probs, held[:LAT, :], NT, preferred_element_type=F32)
+    latent = latent + own * new[:, :LAT]
+    count, heads = out_ref.shape[0] // 2, out_ref.shape[1]
+    latent = latent.reshape(count, heads, LAT).astype(BF)
+    out_ref[:count] = latent
+    out_ref[count:] = latent
 
 
 def exchange(array, axis, groups):
@@ -118,35 +178,21 @@
     out_proj2 = lax.ppermute(out_proj, "dp", swap)
     norm_gain2 = lax.ppermute(norm_gain, "dp", swap)
     residual2 = lax.ppermute(residual, "dp", swap)
-    factor = (HD + ROPE) ** (-0.5)
     positions = latent_cache.shape[1]
-    scores = (
-        jnp.einsum("rhc,rpc->rhp", queries, latent_cache, preferred_element_type=jnp.float32)
-        * factor
-    )
-    places = jnp.arange(positions)
-    scores = jnp.where(places[None, None, :] < lengths[:, None, None], scores, -jnp.inf)
-    own_score = (
-        jnp.einsum("rhc,rc->rh", queries, new_latent, preferred_element_type=jnp.float32) * factor
-    )
-    highest = jnp.maximum(jnp.max(scores, axis=2), own_score)
-    expo = jnp.exp(scores - highest[:, :, None])
-    own_expo = jnp.exp(own_score - highest)
-    total = jnp.sum(expo, axis=2) + own_expo
-    probs = (expo / total[:, :, None]).astype(jnp.bfloat16)
-    own_prob = (own_expo / total).astype(jnp.bfloat16)
-    summed = jnp.einsum(
-        "rhp,rpl->rhl", probs, latent_cache[:, :, :LAT], preferred_element_type=jnp.float32
-    )
-    summed = summed + own_prob.astype(jnp.float32)[:, :, None] * new_latent[:, None, :LAT].astype(
-        jnp.float32
-    )
-    latent_out = summed.astype(jnp.bfloat16)
+    copies = pl.pallas_call(
+        attend_kernel,
+        out_shape=jax.ShapeDtypeStruct((2 * n_tp, queries.shape[1] // n_tp, LAT), BF),
+        in_specs=[SMEM, VMEM, VMEM, pl.BlockSpec(memory_space=pl.ANY)],
+        out_specs=VMEM,
+        scratch_shapes=[
+            pltpu.VMEM((LAT + ROPE, positions), BF),
+            pltpu.SemaphoreType.DMA(((positions + 511) // 512,)),
+        ],
+        compiler_params=pltpu.CompilerParams(vmem_limit_bytes=24 * 2**20),
+    )(lengths, queries[0].T, new_latent, latent_cache[0].T)
     both_y = [
         [at(y, x, c) * n_tp + j for y in two for j in range(n_tp)] for x in xs for c in two
     ]
-    copies = jnp.broadcast_to(latent_out, (2,) + latent_out.shape[1:])
-    copies = copies.reshape((2 * n_tp, -1, LAT))
     owned = exchange(copies, ("dp", "tp"), both_y)
     head_values = jnp.einsum("rhl,hlv->rhv", owned, value_up, preferred_element_type=jnp.float32)
     head_values = head_values.astype(jnp.bfloat16).reshape(owned.shape[0], -1)
@@ -175,8 +221,9 @@
     gate_weight2 = lax.ppermute(gate_weight, "dp", swap)
     up_weight2 = lax.ppermute(up_weight, "dp", swap)
     got, gate_weight2, up_weight2 = lax.optimization_barrier((got, gate_weight2, up_weight2))
-    mid = add_blocks(got, n_tp).astype(BF)
-    mid_set = gather_rows(mid, "tp", n_tp)
+    got = got.reshape(n_tp, -1, got.shape[1])
+    copies = call(mid_kernel, jax.ShapeDtypeStruct(got.shape, BF), [VMEM], got.size)(got)
+    mid_set = exchange(copies, "tp", None).reshape(-1, got.shape[2])
     mid_here, mid_there = mid_set[:, :width], mid_set[:, width:]
     gain = jnp.concatenate([norm_gain, norm_gain2])[None, :]
     ff = gate_weight.shape[1]
@@ -192,25 +239,32 @@
     mid_rest = lax.ppermute(mid_there, "dp", swap)
     got, mid_rest = lax.optimization_barrier((got, mid_rest))
     sums = add_blocks(got, n_x)
-    sums = sums + lax.ppermute(sums.astype(BF), "dp", across_y).astype(F32)
-    meansq = (sums[:, ff] + sums[:, block + ff]) / D
-    scale = lax.rsqrt(meansq + 1e-06)[:, None]
-    gate = sums[:, :ff] * scale
-    upper = sums[:, block : block + ff] * scale
-    hidden = (jax.nn.silu(gate) * upper).astype(BF)
-    hidden = gather_rows(hidden, "dp", n_x * 2, same_y)
+    theirs = lax.ppermute(sums.astype(BF), "dp", across_y)
+    copies = call(
+        hidden_kernel,
+        jax.ShapeDtypeStruct((n_x * 2, sums.shape[0], ff), BF),
+        [VMEM] * 2,
+        8 * sums.size,
+    )(sums, theirs)
+    copies, order = lax.optimization_barrier((copies, order))
+    hidden = exchange(copies, "dp", same_y).reshape(-1, ff)
     rows = hidden.shape[0]
     spots = jnp.arange(rows)
     spot_dp = at(spots // n_tp % 2, spots // (4 * n_tp), spots // (2 * n_tp) % 2)
     spot_rows = spot_dp * n_tp + spots % n_tp
+    own_count = rows // n_tp
+    listed = order.reshape(n_tp, 2, own_count // 2).swapaxes(0, 1).reshape(rows)
+    pick = (listed[:, None] == spot_rows[None, :]).astype(BF)
+    hidden, pick = lax.optimization_barrier((hidden, pick))
+    width = down_weight.shape[1]
     ffn_terms = call(
         down_kernel,
-        jax.ShapeDtypeStruct((rows, down_weight.shape[1]), BF),
-        [VMEM] * 4,
-        2 * rows * ff * (rows + down_weight.shape[1]),
-    )(order[:, None], spot_rows[None, :].astype(jnp.int32), hidden, down_weight.T)
+        jax.ShapeDtypeStruct((rows // 2, 2 * width), BF),
+        [VMEM] * 3,
+        2 * rows * ff * (rows + width),
+    )(pick, hidden, down_weight.T)
     ffn_own = sum_scatter(ffn_terms, "tp", n_tp)
-    own_count = ffn_own.shape[0]
+    ffn_own = jnp.concatenate([ffn_own[:, :width], ffn_own[:, width:]], axis=0)
     wanted = lax.dynamic_slice_in_dim(order, tp * own_count, own_count)
     pick1 = (wanted[:, None] == (set_rows + core * n_tp)[None, :]).astype(BF)
     pick2 = (wanted[:, None] == (set_rows + (1 - core) * n_tp)[None, :]).astype(BF)

time: 161 us -> 161 us (level)
  Pallas kernels: 4.96 us -> 10.2 us
  matrix products: 4.51 us -> 1.2 us
    pallas_call x1 -> x4, Pallas kernels: 1.81 us -> 7 us  [the longest x1 3.28 us: local(): pl.pallas_call(attend_kernel, out_shape=jax.ShapeDtypeStruct((2 * n_tp, q...]
    dot_general x3 -> x0, matrix products: 3.32 us -> none  [the longest x1 2.43 us: local(): jnp.einsum('rhc,rpc->rhp', queries, latent_cache, preferred_element_type=...]
    unnamed x22, local copies, waits for them, and re-layouts: 0.06 us -> 3.2 us
    broadcast_in_dim x4 -> x2, local copies, waits for them, and re-layouts: 2.43 us -> 0.73 us  [gather_rows(): copies = jnp.broadcast_to(rows[None], (count,) + rows.shape)]
where the time goes in v2:
time: 161 us; the launch traced here: 158 us
  waiting for transfers between devices  79.5 us (49%)
  starting transfers between devices  61.5 us (38%)
  Pallas kernels  10.2 us (6%)
  local copies, waits for them, and re-layouts  4.43 us (3%)
    all_to_all x7, waiting for transfers between devices, exchange(): lax.all_to_all(array, axis, split_axis=0, concat_axis=0, axis_index_group...  64.3 us
    all_to_all x7, starting transfers between devices, exchange(): lax.all_to_all(array, axis, split_axis=0, concat_axis=0, axis_index_group...  45.1 us
    ppermute x1, waiting for transfers between devices, local(): theirs = lax.ppermute(sums.astype(BF), 'dp', across_y)  9.91 us
    ppermute x1, starting transfers between devices, local(): theirs = lax.ppermute(sums.astype(BF), 'dp', across_y)  4.3 us
    pallas_call x1, Pallas kernels, local(): pl.pallas_call(attend_kernel, out_shape=jax.ShapeDtypeStruct((2 * n_tp, q...  3.28 us
  transfers between devices with their start and end apart: 14, of which 12 were waited for; matrix products, arithmetic and copies ran while one was open for 1% of the time, Pallas kernels for 0%

profile of v2, /device:TPU:6, one launch (start us, length us, event | category | flops | bytes accessed | tf_op | source)
XLA Modules:
  0.0 158.3 jit_solution(12845557821031997121)
XLA Ops:
  0.7 1.6 copy-done.1
  3.9 3.3 %shard_map.118 = bf16[64,4,512]{2,1,0:T(4,128)(2,1)} custom-call(s32[1]{0:T(128)S(6)} %copy.22.length_ref, bf16[576,128]{1,0:T(8,128)(2,1)S(1)} %bitcast.38, bf16[1,576]{1,0:T(2,128)(2,1)S(1)} %copy-done.7, bf16[576,1792]{1,0:T(8,128)(2,1)S(1)} %bitcast.33), custom_call_target="tpu_custom_call" | custom-call | tf_op jit(solution)/shard_map/pallas_call | solution.py:182
  7.2 16.6 %all-to-all-start = ((bf16[64,4,512]{2,1,0:T(4,128)(2,1)}), bf16[64,4,512]{2,1,0:T(4,128)(2,1)S(1)}, u32[]{:S(2)}, u32[]{:S(2)}) async-start(bf16[64,4,512]{2,1,0:T(4,128)(2,1)} %shard_map.118), calls=%async_computation | async-start | bytes 524288 | tf_op jit(solution)/shard_map/all_to_all | solution.py:130
  23.8 1.9 %collective-permute-start = (bf16[512,448]{0,1:T(8,128)(2,1)S(1)}, bf16[512,448]{0,1:T(8,128)(2,1)S(1)}, u32[]{:S(2)}, u32[]{:S(2)}) collective-permute-start(bf16[512,448]{0,1:T(8,128)(2,1)S(1)} %copy-done.5), channel_id=1, source_target_pairs={{0,32},{32,0},{64,96},{96,64},{128,160},{160,128},{192,224},{224,1... | collective-permute-start | bytes 1376264 | tf_op jit(solution)/shard_map/ppermute | solution.py:178
  25.7 13.1 %all-to-all-done = bf16[64,4,512]{2,1,0:T(4,128)(2,1)S(1)} async-done(((bf16[64,4,512]{2,1,0:T(4,128)(2,1)}), bf16[64,4,512]{2,1,0:T(4,128)(2,1)S(1)}, u32[]{:S(2)}, u32[]{:S(2)}) %all-to-all-start) | async-done | bytes 262176 | tf_op jit(solution)/shard_map/all_to_all | solution.py:130
  39.8 4.8 %all-to-all-start.1 = ((bf16[4,64,512]{2,1,0:T(8,128)(2,1)}), bf16[4,64,512]{2,1,0:T(8,128)(2,1)S(1)}, u32[]{:S(2)}, u32[]{:S(2)}) async-start(bf16[4,64,512]{2,1,0:T(8,128)(2,1)} %broadcast_in_dim.7), calls=%async_computation.1 | async-start | bytes 524288 | tf_op jit(solution)/shard_map/all_to_all | solution.py:130
  44.6 1.9 %collective-permute-start.1 = (bf16[16,448]{1,0:T(8,128)(2,1)S(1)}, bf16[16,448]{1,0:T(8,128)(2,1)S(1)}, u32[]{:S(2)}, u32[]{:S(2)}) collective-permute-start(bf16[16,448]{1,0:T(8,128)(2,1)S(1)} %copy-done.8), channel_id=1, source_target_pairs={{0,32},{32,0},{64,96},{96,64},{128,160},{160,128},{192,224},{224,1... | collective-permute-start | bytes 43016 | tf_op jit(solution)/shard_map/ppermute | solution.py:180
  46.6 1.1 collective-permute-done.1
  47.8 1.5 all-to-all-done.1
  49.2 1.3 shard_map.119
  50.5 3.9 %all-to-all-start.2 = ((bf16[32,8,896]{2,1,0:T(8,128)(2,1)}), bf16[32,8,896]{2,1,0:T(8,128)(2,1)S(1)}, u32[]{:S(2)}, u32[]{:S(2)}) async-start(bf16[32,8,896]{2,1,0:T(8,128)(2,1)} %bitcast.9), calls=%async_computation.2 | async-start | bytes 917504 | tf_op jit(solution)/shard_map/all_to_all | solution.py:130
  54.4 1.9 %collective-permute-start.2 = (bf16[448,576]{1,0:T(8,128)(2,1)S(1)}, bf16[448,576]{1,0:T(8,128)(2,1)S(1)}, u32[]{:S(2)}, u32[]{:S(2)}) collective-permute-start(bf16[448,576]{1,0:T(8,128)(2,1)S(1)} %copy-done.2), channel_id=1, source_target_pairs={{0,32},{32,0},{64,96},{96,64},{128,160},{160,128},{192,224},{224,1... | collective-permute-start | bytes 1548296 | tf_op jit(solution)/shard_map/ppermute | solution.py:221
  56.4 2.4 %collective-permute-start.3 = (bf16[448,576]{1,0:T(8,128)(2,1)S(1)}, bf16[448,576]{1,0:T(8,128)(2,1)S(1)}, u32[]{:S(2)}, u32[]{:S(2)}) collective-permute-start(bf16[448,576]{1,0:T(8,128)(2,1)S(1)} %copy-done.3), channel_id=1, source_target_pairs={{0,32},{32,0},{64,96},{96,64},{128,160},{160,128},{192,224},{224,1... | collective-permute-start | bytes 1548296 | tf_op jit(solution)/shard_map/ppermute | solution.py:222
  58.8 1.6 collective-permute-done.3.u2_ref
  60.4 9.2 %all-to-all-done.2 = bf16[32,8,896]{2,1,0:T(8,128)(2,1)S(1)} async-done(((bf16[32,8,896]{2,1,0:T(8,128)(2,1)}), bf16[32,8,896]{2,1,0:T(8,128)(2,1)S(1)}, u32[]{:S(2)}, u32[]{:S(2)}) %all-to-all-start.2) | async-done | bytes 458784 | tf_op jit(solution)/shard_map/all_to_all | solution.py:130
  70.5 4.7 %all-to-all-start.3 = ((bf16[32,8,896]{2,1,0:T(8,128)(2,1)}), bf16[32,8,896]{2,1,0:T(8,128)(2,1)S(1)}, u32[]{:S(2)}, u32[]{:S(2)}) async-start(bf16[32,8,896]{2,1,0:T(8,128)(2,1)} %shard_map.120), calls=%async_computation.3 | async-start | bytes 917504 | tf_op jit(solution)/shard_map/all_to_all | solution.py:130
  75.2 1.9 %collective-permute-start.4 = (bf16[448]{0:T(512)(128)(2,1)S(1)}, bf16[448]{0:T(512)(128)(2,1)S(1)}, u32[]{:S(2)}, u32[]{:S(2)}) collective-permute-start(bf16[448]{0:T(512)(128)(2,1)S(1)} %copy-done.10), channel_id=1, source_target_pairs={{0,32},{32,0},{64,96},{96,64},{128,160},{160,128},{192,224},{224,1... | collective-permute-start | bytes 2696 | tf_op jit(solution)/shard_map/ppermute | solution.py:179
  77.1 1.1 collective-permute-done.4
  78.3 12.6 %all-to-all-done.3 = bf16[32,8,896]{2,1,0:T(8,128)(2,1)S(1)} async-done(((bf16[32,8,896]{2,1,0:T(8,128)(2,1)}), bf16[32,8,896]{2,1,0:T(8,128)(2,1)S(1)}, u32[]{:S(2)}, u32[]{:S(2)}) %all-to-all-start.3) | async-done | bytes 458784 | tf_op jit(solution)/shard_map/all_to_all | solution.py:130
  91.1 1.8 %shard_map.121 = bf16[4,64,1280]{2,1,0:T(8,128)(2,1)} custom-call(bf16[256,896]{1,0:T(8,128)(2,1)S(1)} %bitcast.30, bf16[1,896]{1,0:T(2,128)(2,1)S(1)} %broadcast_in_dim.8.gain_ref, bf16[448,576]{1,0:T(8,128)(2,1)S(1)} %copy-done.2, bf16[448,576]{1,0:T(8,128)(2,1)S(1)} %collective-permute-done.2.g2_ref, bf16[448,576]{1,0:T(8,128)(2,1)S(1)} %copy-done.3, ...), custom_call_target="tpu_custom_call" | custom-call | flops 528482304 | bytes 2097152 | tf_op jit(solution)/shard_map/pallas_call | solution.py:231
  92.9 4.8 %all-to-all-start.4 = ((bf16[4,64,1280]{2,1,0:T(8,128)(2,1)}), bf16[4,64,1280]{2,1,0:T(8,128)(2,1)S(1)}, u32[]{:S(2)}, u32[]{:S(2)}) async-start(bf16[4,64,1280]{2,1,0:T(8,128)(2,1)} %shard_map.121), calls=%async_computation.4 | async-start | bytes 1310720 | tf_op jit(solution)/shard_map/all_to_all | solution.py:130
  97.7 2.0 %collective-permute-start.5 = (bf16[256,448]{1,0:T(8,128)(2,1)S(1)}, bf16[256,448]{1,0:T(8,128)(2,1)S(1)}, u32[]{:S(2)}, u32[]{:S(2)}) collective-permute-start(bf16[256,448]{1,0:T(8,128)(2,1)S(1)} %slice.16), channel_id=1, source_target_pairs={{0,32},{32,0},{64,96},{96,64},{128,160},{160,128},{192,224},{224,1... | collective-permute-start | bytes 688136 | tf_op jit(solution)/shard_map/ppermute | solution.py:239
  99.7 1.5 collective-permute-done.5
  101.2 3.2 %all-to-all-done.4 = bf16[4,64,1280]{2,1,0:T(8,128)(2,1)S(1)} async-done(((bf16[4,64,1280]{2,1,0:T(8,128)(2,1)}), bf16[4,64,1280]{2,1,0:T(8,128)(2,1)S(1)}, u32[]{:S(2)}, u32[]{:S(2)}) %all-to-all-start.4) | async-done | bytes 655392 | tf_op jit(solution)/shard_map/all_to_all | solution.py:130
  104.5 4.3 %collective-permute-start.6 = (bf16[64,1280]{1,0:T(8,128)(2,1)S(1)}, bf16[64,1280]{1,0:T(8,128)(2,1)S(1)}, u32[]{:S(2)}, u32[]{:S(2)}) collective-permute-start(bf16[64,1280]{1,0:T(8,128)(2,1)S(1)} %convert_element_type.30), channel_id=1, source_target_pairs={{0,256},{32,288},{64,320},{96,352},{128,384},{160,416},{192,448},{... | collective-permute-start | bytes 491528 | tf_op jit(solution)/shard_map/ppermute | solution.py:242
  108.8 9.9 %collective-permute-done.6.theirs_ref = bf16[64,1280]{1,0:T(8,128)(2,1)S(1)} collective-permute-done((bf16[64,1280]{1,0:T(8,128)(2,1)S(1)}, bf16[64,1280]{1,0:T(8,128)(2,1)S(1)}, u32[]{:S(2)}, u32[]{:S(2)}) %collective-permute-start.6) | collective-permute-done | bytes 163872 | tf_op jit(solution)/shard_map/ppermute | solution.py:242
  118.7 1.0 shard_map.122
  119.8 4.5 %all-to-all-start.5 = ((bf16[8,64,576]{2,1,0:T(8,128)(2,1)}), bf16[8,64,576]{2,1,0:T(8,128)(2,1)S(1)}, u32[]{:S(2)}, u32[]{:S(2)}) async-start(bf16[8,64,576]{2,1,0:T(8,128)(2,1)} %shard_map.122), calls=%async_computation.5 | async-start | bytes 1310720 | tf_op jit(solution)/shard_map/all_to_all | solution.py:130
  124.7 9.3 %all-to-all-done.5 = bf16[8,64,576]{2,1,0:T(8,128)(2,1)S(1)} async-done(((bf16[8,64,576]{2,1,0:T(8,128)(2,1)}), bf16[8,64,576]{2,1,0:T(8,128)(2,1)S(1)}, u32[]{:S(2)}, u32[]{:S(2)}) %all-to-all-start.5) | async-done | bytes 589856 | tf_op jit(solution)/shard_map/all_to_all | solution.py:130
  134.0 1.8 %shard_map.123 = bf16[256,896]{1,0:T(8,128)(2,1)} custom-call(bf16[512,512]{1,0:T(8,128)(2,1)S(1)} %compare_convert_fusion.pick_ref, bf16[512,576]{1,0:T(8,128)(2,1)S(1)} %bitcast.32, bf16[448,576]{1,0:T(8,128)(2,1)S(1)} %bitcast.35), custom_call_target="tpu_custom_call" | custom-call | flops 566231040 | bytes 2097152 | tf_op jit(solution)/shard_map/pallas_call | solution.py:260
  135.8 5.8 %all-to-all-start.6 = ((bf16[32,8,896]{2,1,0:T(8,128)(2,1)}), bf16[32,8,896]{2,1,0:T(8,128)(2,1)S(1)}, u32[]{:S(2)}, u32[]{:S(2)}) async-start(bf16[32,8,896]{2,1,0:T(8,128)(2,1)} %bitcast.18), calls=%async_computation.6 | async-start | bytes 917504 | tf_op jit(solution)/shard_map/all_to_all | solution.py:130
  141.9 15.5 %all-to-all-done.6 = bf16[32,8,896]{2,1,0:T(8,128)(2,1)S(1)} async-done(((bf16[32,8,896]{2,1,0:T(8,128)(2,1)}), bf16[32,8,896]{2,1,0:T(8,128)(2,1)S(1)}, u32[]{:S(2)}, u32[]{:S(2)}) %all-to-all-start.6) | async-done | bytes 458784 | tf_op jit(solution)/shard_map/all_to_all | solution.py:130
  (45 shorter events, 5.5 us)
Async XLA Ops:
  0.0 38.8 %copy-start = (bf16[4,512,128]{2,1,0:T(8,128)(2,1)S(1)}, bf16[4,512,128]{2,1,0:T(8,128)(2,1)}, u32[]{:S(2)}) copy-start(bf16[4,512,128]{2,1,0:T(8,128)(2,1)} %param.17) | copy-start | bytes 1572868
  0.7 1.6 copy-start.1
  2.3 0.9 copy-start.6
  3.2 0.7 copy-start.7
  3.9 19.9 %copy-start.5 = (bf16[512,448]{0,1:T(8,128)(2,1)S(1)}, bf16[512,448]{0,1:T(8,128)(2,1)}, u32[]{:S(2)}) copy-start(bf16[512,448]{0,1:T(8,128)(2,1)} %param.18) | copy-start | bytes 1376260
  3.9 40.7 %copy-start.8 = (bf16[16,448]{1,0:T(8,128)(2,1)S(1)}, bf16[16,448]{1,0:T(8,128)(2,1)}, u32[]{:S(2)}) copy-start(bf16[16,448]{1,0:T(8,128)(2,1)} %param.19) | copy-start | bytes 43012
  7.2 31.6 %all-to-all-start = ((bf16[64,4,512]{2,1,0:T(4,128)(2,1)}), bf16[64,4,512]{2,1,0:T(4,128)(2,1)S(1)}, u32[]{:S(2)}, u32[]{:S(2)}) async-start(bf16[64,4,512]{2,1,0:T(4,128)(2,1)} %shard_map.118), calls=%async_computation | async-start | bytes 524288 | tf_op jit(solution)/shard_map/all_to_all | solution.py:130
  23.8 24.0 %collective-permute-start = (bf16[512,448]{0,1:T(8,128)(2,1)S(1)}, bf16[512,448]{0,1:T(8,128)(2,1)S(1)}, u32[]{:S(2)}, u32[]{:S(2)}) collective-permute-start(bf16[512,448]{0,1:T(8,128)(2,1)S(1)} %copy-done.5), channel_id=1, source_target_pairs={{0,32},{32,0},{64,96},{96,64},{128,160},{160,128},{192,224},{224,1... | collective-permute-start | bytes 1376264 | tf_op jit(solution)/shard_map/ppermute | solution.py:178
  39.1 15.4 %copy-start.2 = (bf16[448,576]{1,0:T(8,128)(2,1)S(1)}, bf16[448,576]{1,0:T(8,128)(2,1)}, u32[]{:S(2)}) copy-start(bf16[448,576]{1,0:T(8,128)(2,1)} %g1_ref) | copy-start | bytes 1548292
  39.1 17.3 %copy-start.3 = (bf16[448,576]{1,0:T(8,128)(2,1)S(1)}, bf16[448,576]{1,0:T(8,128)(2,1)}, u32[]{:S(2)}) copy-start(bf16[448,576]{1,0:T(8,128)(2,1)} %u1_ref) | copy-start | bytes 1548292
  39.8 9.4 %all-to-all-start.1 = ((bf16[4,64,512]{2,1,0:T(8,128)(2,1)}), bf16[4,64,512]{2,1,0:T(8,128)(2,1)S(1)}, u32[]{:S(2)}, u32[]{:S(2)}) async-start(bf16[4,64,512]{2,1,0:T(8,128)(2,1)} %broadcast_in_dim.7), calls=%async_computation.1 | async-start | bytes 524288 | tf_op jit(solution)/shard_map/all_to_all | solution.py:130
  44.6 3.1 %collective-permute-start.1 = (bf16[16,448]{1,0:T(8,128)(2,1)S(1)}, bf16[16,448]{1,0:T(8,128)(2,1)S(1)}, u32[]{:S(2)}, u32[]{:S(2)}) collective-permute-start(bf16[16,448]{1,0:T(8,128)(2,1)S(1)} %copy-done.8), channel_id=1, source_target_pairs={{0,32},{32,0},{64,96},{96,64},{128,160},{160,128},{192,224},{224,1... | collective-permute-start | bytes 43016 | tf_op jit(solution)/shard_map/ppermute | solution.py:180
  49.2 26.0 %copy-start.10 = (bf16[448]{0:T(512)(128)(2,1)S(1)}, bf16[448]{0:T(512)(128)(2,1)}, u32[]{:S(2)}) copy-start(bf16[448]{0:T(512)(128)(2,1)} %param.20) | copy-start | bytes 2692
  50.5 19.0 %all-to-all-start.2 = ((bf16[32,8,896]{2,1,0:T(8,128)(2,1)}), bf16[32,8,896]{2,1,0:T(8,128)(2,1)S(1)}, u32[]{:S(2)}, u32[]{:S(2)}) async-start(bf16[32,8,896]{2,1,0:T(8,128)(2,1)} %bitcast.9), calls=%async_computation.2 | async-start | bytes 917504 | tf_op jit(solution)/shard_map/all_to_all | solution.py:130
  54.4 4.4 %collective-permute-start.2 = (bf16[448,576]{1,0:T(8,128)(2,1)S(1)}, bf16[448,576]{1,0:T(8,128)(2,1)S(1)}, u32[]{:S(2)}, u32[]{:S(2)}) collective-permute-start(bf16[448,576]{1,0:T(8,128)(2,1)S(1)} %copy-done.2), channel_id=1, source_target_pairs={{0,32},{32,0},{64,96},{96,64},{128,160},{160,128},{192,224},{224,1... | collective-permute-start | bytes 1548296 | tf_op jit(solution)/shard_map/ppermute | solution.py:221
  56.4 4.0 %collective-permute-start.3 = (bf16[448,576]{1,0:T(8,128)(2,1)S(1)}, bf16[448,576]{1,0:T(8,128)(2,1)S(1)}, u32[]{:S(2)}, u32[]{:S(2)}) collective-permute-start(bf16[448,576]{1,0:T(8,128)(2,1)S(1)} %copy-done.3), channel_id=1, source_target_pairs={{0,32},{32,0},{64,96},{96,64},{128,160},{160,128},{192,224},{224,1... | collective-permute-start | bytes 1548296 | tf_op jit(solution)/shard_map/ppermute | solution.py:222
  70.5 20.5 %all-to-all-start.3 = ((bf16[32,8,896]{2,1,0:T(8,128)(2,1)}), bf16[32,8,896]{2,1,0:T(8,128)(2,1)S(1)}, u32[]{:S(2)}, u32[]{:S(2)}) async-start(bf16[32,8,896]{2,1,0:T(8,128)(2,1)} %shard_map.120), calls=%async_computation.3 | async-start | bytes 917504 | tf_op jit(solution)/shard_map/all_to_all | solution.py:130
  75.2 3.0 %collective-permute-start.4 = (bf16[448]{0:T(512)(128)(2,1)S(1)}, bf16[448]{0:T(512)(128)(2,1)S(1)}, u32[]{:S(2)}, u32[]{:S(2)}) collective-permute-start(bf16[448]{0:T(512)(128)(2,1)S(1)} %copy-done.10), channel_id=1, source_target_pairs={{0,32},{32,0},{64,96},{96,64},{128,160},{160,128},{192,224},{224,1... | collective-permute-start | bytes 2696 | tf_op jit(solution)/shard_map/ppermute | solution.py:179
  92.9 11.5 %all-to-all-start.4 = ((bf16[4,64,1280]{2,1,0:T(8,128)(2,1)}), bf16[4,64,1280]{2,1,0:T(8,128)(2,1)S(1)}, u32[]{:S(2)}, u32[]{:S(2)}) async-start(bf16[4,64,1280]{2,1,0:T(8,128)(2,1)} %shard_map.121), calls=%async_computation.4 | async-start | bytes 1310720 | tf_op jit(solution)/shard_map/all_to_all | solution.py:130
  97.7 26.6 %copy-start.9 = (s32[512]{0:T(512)S(1)}, s32[512]{0:T(512)}, u32[]{:S(2)}) copy-start(s32[512]{0:T(512)} %param.16) | copy-start | bytes 6148
  97.7 3.5 %collective-permute-start.5 = (bf16[256,448]{1,0:T(8,128)(2,1)S(1)}, bf16[256,448]{1,0:T(8,128)(2,1)S(1)}, u32[]{:S(2)}, u32[]{:S(2)}) collective-permute-start(bf16[256,448]{1,0:T(8,128)(2,1)S(1)} %slice.16), channel_id=1, source_target_pairs={{0,32},{32,0},{64,96},{96,64},{128,160},{160,128},{192,224},{224,1... | collective-permute-start | bytes 688136 | tf_op jit(solution)/shard_map/ppermute | solution.py:239
  104.4 29.5 %copy-start.4 = (bf16[576,448]{0,1:T(8,128)(2,1)S(1)}, bf16[576,448]{0,1:T(8,128)(2,1)}, u32[]{:S(2)}) copy-start(bf16[576,448]{0,1:T(8,128)(2,1)} %param.23) | copy-start | bytes 1548292
  104.5 14.2 %collective-permute-start.6 = (bf16[64,1280]{1,0:T(8,128)(2,1)S(1)}, bf16[64,1280]{1,0:T(8,128)(2,1)S(1)}, u32[]{:S(2)}, u32[]{:S(2)}) collective-permute-start(bf16[64,1280]{1,0:T(8,128)(2,1)S(1)} %convert_element_type.30), channel_id=1, source_target_pairs={{0,256},{32,288},{64,320},{96,352},{128,384},{160,416},{192,448},{... | collective-permute-start | bytes 491528 | tf_op jit(solution)/shard_map/ppermute | solution.py:242
  119.8 14.2 %all-to-all-start.5 = ((bf16[8,64,576]{2,1,0:T(8,128)(2,1)}), bf16[8,64,576]{2,1,0:T(8,128)(2,1)S(1)}, u32[]{:S(2)}, u32[]{:S(2)}) async-start(bf16[8,64,576]{2,1,0:T(8,128)(2,1)} %shard_map.122), calls=%async_computation.5 | async-start | bytes 1310720 | tf_op jit(solution)/shard_map/all_to_all | solution.py:130
  135.8 21.6 %all-to-all-start.6 = ((bf16[32,8,896]{2,1,0:T(8,128)(2,1)}), bf16[32,8,896]{2,1,0:T(8,128)(2,1)S(1)}, u32[]{:S(2)}, u32[]{:S(2)}) async-start(bf16[32,8,896]{2,1,0:T(8,128)(2,1)} %bitcast.18), calls=%async_computation.6 | async-start | bytes 917504 | tf_op jit(solution)/shard_map/all_to_all | solution.py:130

commit v3 on v2

--- a/solution.py
+++ b/solution.py
@@ -6,6 +6,7 @@
 from jax.sharding import PartitionSpec as P
 
 D = 7168
+LANES = 128
 LAT = 512
 ROPE = 64
 HD = 128
@@ -45,23 +46,42 @@
     squares = jnp.sum(wide * wide, axis=1, keepdims=True)
     high = squares.astype(BF).astype(F32)
     gained = (wide * gain_ref[...].astype(F32)).astype(BF)
-    ff = g1_ref.shape[1]
-    parts, rows, block = out_ref.shape[0], out_ref.shape[1], out_ref.shape[2] // 2
-    for k, (a_ref, b_ref, extra) in enumerate(
-        ((g1_ref, g2_ref, high), (u1_ref, u2_ref, squares - high))
-    ):
+    terms = []
+    for a_ref, b_ref in ((g1_ref, g2_ref), (u1_ref, u2_ref)):
         weights = jnp.concatenate([a_ref[...], b_ref[...]], axis=0)
-        term = jnp.dot(gained, weights, preferred_element_type=F32)
-        pad = jnp.broadcast_to(extra, (extra.shape[0], block - ff))
-        term = jnp.concatenate([term, pad], axis=1)
-        for q in range(parts):
-            part = term[q * rows : (q + 1) * rows].astype(BF)
-            out_ref[q, :, k * block : (k + 1) * block] = part
+        terms.append(jnp.dot(gained, weights, preferred_element_type=F32))
+    terms = jnp.concatenate(terms, axis=1)
+    parts, tiles = out_ref.shape[0], terms.shape[1] // LANES
+    rows = terms.shape[0] // parts
+    for q in range(parts):
+        mine = slice(q * rows, (q + 1) * rows)
+        pack(out_ref, q, terms[mine], high[mine], (squares - high)[mine])
+
+
+def pack(out_ref, q, terms, high, low):
+    rows, tiles = terms.shape[0], terms.shape[1] // LANES
+    for t in range(tiles):
+        tile = terms[:, t * LANES : (t + 1) * LANES]
+        out_ref[q, t * rows : (t + 1) * rows, :] = tile.astype(BF)
+    lane = lax.broadcasted_iota(jnp.int32, (16, LANES), 1)
+    extra = jnp.zeros((16, LANES), F32)
+    for g in range(rows // 16):
+        mine = slice(16 * g, 16 * g + 16)
+        extra = jnp.where(lane == 2 * g, high[mine], extra)
+        extra = jnp.where(lane == 2 * g + 1, low[mine], extra)
+    out_ref[q, tiles * rows : tiles * rows + 16, :] = extra.astype(BF)
 
 
 def down_kernel(pick_ref, hidden_ref, w_ref, out_ref):
     half = out_ref.shape[0]
-    hidden = hidden_ref[...]
+    whole, rows = w_ref.shape[1] // LANES, 64
+    blocks = []
+    for q in range(hidden_ref.shape[0]):
+        tiles = [hidden_ref[q, t * rows : (t + 1) * rows, :] for t in range(whole)]
+        rest = hidden_ref[q, whole * rows :, :]
+        rest = jnp.concatenate([rest[:, : LANES // 2], rest[:, LANES // 2 :]], axis=0)
+        blocks.append(jnp.concatenate(tiles + [rest], axis=1))
+    hidden = jnp.concatenate(blocks, axis=0)
     parts = []
     for k in range(2):
         pick = pick_ref[k * half : (k + 1) * half]
@@ -81,23 +101,46 @@
 
 def hidden_kernel(mine_ref, theirs_ref, out_ref):
     sums = mine_ref[...] + theirs_ref[...].astype(F32)
-    ff, block = out_ref.shape[2], sums.shape[1] // 2
-    meansq = (sums[:, ff : ff + 1] + sums[:, block + ff : block + ff + 1]) / D
-    scale = lax.rsqrt(meansq + 1e-06)
-    gate = sums[:, :ff] * scale
-    upper = sums[:, block : block + ff] * scale
+    tiles = sums.shape[0] // 64
+    rows = 64
+    extra = sums[tiles * rows :]
+    squares = jnp.concatenate(
+        [
+            extra[:, 2 * g : 2 * g + 1] + extra[:, 2 * g + 1 : 2 * g + 2]
+            for g in range(rows // 16)
+        ],
+        axis=0,
+    )
+    scale = lax.rsqrt(squares / D + 1e-06)
+    both = jnp.concatenate([sums[t * rows : (t + 1) * rows] for t in range(tiles)], axis=1)
+    ff = both.shape[1] // 2
+    gate = both[:, :ff] * scale
+    upper = both[:, ff:] * scale
     hidden = (gate / (1.0 + jnp.exp(-gate)) * upper).astype(BF)
+    whole = ff // LANES
+    rest = hidden[:, whole * LANES :]
+    rest = jnp.concatenate([rest[: rows // 2], rest[rows // 2 :]], axis=1)
     for q in range(out_ref.shape[0]):
-        out_ref[q] = hidden
-
-
-def attend_kernel(length_ref, queries_ref, new_ref, cache_ref, out_ref, held, sems):
-    positions, piece = cache_ref.shape[1], 512
+        for t in range(whole):
+            tile = hidden[:, t * LANES : (t + 1) * LANES]
+            out_ref[q, t * rows : (t + 1) * rows, :] = tile
+        out_ref[q, whole * rows :, :] = rest
+
+
+def attend_kernel(length_ref, queries_hbm, new_hbm, cache_hbm, out_ref, *scratch):
+    held, queries_ref, new_ref, sems = scratch
+    positions, piece = held.shape[1], 512
+    first = pltpu.make_async_copy(queries_hbm, queries_ref, sems.at[0])
+    second = pltpu.make_async_copy(new_hbm, new_ref, sems.at[1])
+    first.start()
+    second.start()
     copies = []
     for k, start in enumerate(range(0, positions, piece)):
         at = (slice(None), pl.ds(start, min(piece, positions - start)))
-        copies.append(pltpu.make_async_copy(cache_ref.at[at], held.at[at], sems.at[k]))
+        copies.append(pltpu.make_async_copy(cache_hbm.at[at], held.at[at], sems.at[k + 2]))
         copies[-1].start()
+    first.wait()
+    second.wait()
     factor = (HD + ROPE) ** (-0.5)
     queries = queries_ref[...].T
     new = new_ref[...].astype(F32)
@@ -182,13 +225,15 @@
     copies = pl.pallas_call(
         attend_kernel,
         out_shape=jax.ShapeDtypeStruct((2 * n_tp, queries.shape[1] // n_tp, LAT), BF),
-        in_specs=[SMEM, VMEM, VMEM, pl.BlockSpec(memory_space=pl.ANY)],
+        in_specs=[SMEM] + [pl.BlockSpec(memory_space=pltpu.HBM)] * 3,
         out_specs=VMEM,
         scratch_shapes=[
             pltpu.VMEM((LAT + ROPE, positions), BF),
-            pltpu.SemaphoreType.DMA(((positions + 511) // 512,)),
+            pltpu.VMEM((LAT + ROPE, queries.shape[1]), BF),
+            pltpu.VMEM((1, LAT + ROPE), BF),
+            pltpu.SemaphoreType.DMA(((positions + 511) // 512 + 2,)),
         ],
-        compiler_params=pltpu.CompilerParams(vmem_limit_bytes=24 * 2**20),
+        compiler_params=pltpu.CompilerParams(vmem_limit_bytes=63 * 2**20 + 15 * 2**16),
     )(lengths, queries[0].T, new_latent, latent_cache[0].T)
     both_y = [
         [at(y, x, c) * n_tp + j for y in two for j in range(n_tp)] for x in xs for c in two
@@ -227,28 +272,28 @@
     mid_here, mid_there = mid_set[:, :width], mid_set[:, width:]
     gain = jnp.concatenate([norm_gain, norm_gain2])[None, :]
     ff = gate_weight.shape[1]
-    block = (ff + 127) // 128 * 128
+    tall = mid_set.shape[0] // n_x * (2 * ff // LANES) + 16
     terms = call(
         ff_kernel,
-        jax.ShapeDtypeStruct((n_x, mid_set.shape[0] // n_x, 2 * block), BF),
+        jax.ShapeDtypeStruct((n_x, tall, LANES), BF),
         [VMEM] * 6,
         4 * mid_set.size * ff,
     )(mid_set, gain, gate_weight, gate_weight2, up_weight, up_weight2)
     terms, mid_there = lax.optimization_barrier((terms, mid_there))
-    got = exchange(terms, "dp", along_x).reshape(-1, 2 * block)
+    got = exchange(terms, "dp", along_x).reshape(-1, LANES)
     mid_rest = lax.ppermute(mid_there, "dp", swap)
     got, mid_rest = lax.optimization_barrier((got, mid_rest))
     sums = add_blocks(got, n_x)
     theirs = lax.ppermute(sums.astype(BF), "dp", across_y)
     copies = call(
         hidden_kernel,
-        jax.ShapeDtypeStruct((n_x * 2, sums.shape[0], ff), BF),
+        jax.ShapeDtypeStruct((n_x * 2, 2 * n_tp * ff // LANES, LANES), BF),
         [VMEM] * 2,
         8 * sums.size,
     )(sums, theirs)
     copies, order = lax.optimization_barrier((copies, order))
-    hidden = exchange(copies, "dp", same_y).reshape(-1, ff)
-    rows = hidden.shape[0]
+    hidden = exchange(copies, "dp", same_y)
+    rows = n_dp * n_tp
     spots = jnp.arange(rows)
     spot_dp = at(spots // n_tp % 2, spots // (4 * n_tp), spots // (2 * n_tp) % 2)
     spot_rows = spot_dp * n_tp + spots % n_tp

time: 161 us -> 158 us (0.981)
  local copies, waits for them, and re-layouts: 4.43 us -> 1.27 us
  waiting for transfers between devices: 79.5 us -> 76.7 us
    unnamed x22 -> x14, local copies, waits for them, and re-layouts: 3.2 us -> 0.04 us
    ppermute x1, waiting for transfers between devices: 9.91 us -> 8.05 us  [local(): theirs = lax.ppermute(sums.astype(BF), 'dp', across_y)]
  transfers between devices with their start and end apart: 14 -> 14, of which waited for: 12 -> 12; matrix products, arithmetic and copies ran while one was open for 1% -> 2% of each run, Pallas kernels for 0% -> 0%
where the time goes in v3:
time: 158 us; the launch traced here: 156 us
  waiting for transfers between devices  76.7 us (49%)
  starting transfers between devices  62.9 us (40%)
  Pallas kernels  11.2 us (7%)
  matrix products  2.24 us (1%)
    all_to_all x7, waiting for transfers between devices, exchange(): lax.all_to_all(array, axis, split_axis=0, concat_axis=0, axis_index_group...  63.3 us
    all_to_all x7, starting transfers between devices, exchange(): lax.all_to_all(array, axis, split_axis=0, concat_axis=0, axis_index_group...  46.5 us
    ppermute x1, waiting for transfers between devices, local(): theirs = lax.ppermute(sums.astype(BF), 'dp', across_y)  8.05 us
    ppermute x1, starting transfers between devices, local(): theirs = lax.ppermute(sums.astype(BF), 'dp', across_y)  4.3 us
    pallas_call x1, Pallas kernels, local(): pl.pallas_call(attend_kernel, out_shape=jax.ShapeDtypeStruct((2 * n_tp, q...  4.14 us
  transfers between devices with their start and end apart: 14, of which 12 were waited for; matrix products, arithmetic and copies ran while one was open for 2% of the time, Pallas kernels for 0%

profile of v3, /device:TPU:6, one launch (start us, length us, event | category | flops | bytes accessed | tf_op | source)
XLA Modules:
  0.0 155.8 jit_solution(2393029281615350729)
XLA Ops:
  0.7 4.1 %shard_map.118 = bf16[64,4,512]{2,1,0:T(4,128)(2,1)} custom-call(s32[1]{0:T(128)S(6)} %copy.22.length_ref, bf16[576,128]{1,0:T(8,128)(2,1)} %bitcast.37, bf16[1,576]{1,0:T(2,128)(2,1)} %new_hbm.1, bf16[576,1792]{1,0:T(8,128)(2,1)} %bitcast.35), custom_call_target="tpu_custom_call" | custom-call | tf_op jit(solution)/shard_map/pallas_call | solution.py:225
  4.8 16.7 %all-to-all-start = ((bf16[64,4,512]{2,1,0:T(4,128)(2,1)}), bf16[64,4,512]{2,1,0:T(4,128)(2,1)S(1)}, u32[]{:S(2)}, u32[]{:S(2)}) async-start(bf16[64,4,512]{2,1,0:T(4,128)(2,1)} %shard_map.118), calls=%async_computation | async-start | bytes 524288 | tf_op jit(solution)/shard_map/all_to_all | solution.py:173
  21.5 1.9 %collective-permute-start = (bf16[512,448]{0,1:T(8,128)(2,1)}, bf16[512,448]{0,1:T(8,128)(2,1)S(1)}, u32[]{:S(2)}, u32[]{:S(2)}) collective-permute-start(bf16[512,448]{0,1:T(8,128)(2,1)} %param.18), channel_id=1, source_target_pairs={{0,32},{32,0},{64,96},{96,64},{128,160},{160,128},{192,224},{224,1... | collective-permute-start | bytes 1376264 | tf_op jit(solution)/shard_map/ppermute | solution.py:221
  23.5 13.1 %all-to-all-done = bf16[64,4,512]{2,1,0:T(4,128)(2,1)S(1)} async-done(((bf16[64,4,512]{2,1,0:T(4,128)(2,1)}), bf16[64,4,512]{2,1,0:T(4,128)(2,1)S(1)}, u32[]{:S(2)}, u32[]{:S(2)}) %all-to-all-start) | async-done | bytes 262176 | tf_op jit(solution)/shard_map/all_to_all | solution.py:173
  36.6 1.3 fusion
  38.6 4.8 %all-to-all-start.1 = ((bf16[4,64,512]{2,1,0:T(8,128)(2,1)}), bf16[4,64,512]{2,1,0:T(8,128)(2,1)S(1)}, u32[]{:S(2)}, u32[]{:S(2)}) async-start(bf16[4,64,512]{2,1,0:T(8,128)(2,1)} %broadcast_in_dim.7), calls=%async_computation.1 | async-start | bytes 524288 | tf_op jit(solution)/shard_map/all_to_all | solution.py:173
  43.4 1.9 %collective-permute-start.1 = (bf16[16,448]{1,0:T(8,128)(2,1)S(1)}, bf16[16,448]{1,0:T(8,128)(2,1)S(1)}, u32[]{:S(2)}, u32[]{:S(2)}) collective-permute-start(bf16[16,448]{1,0:T(8,128)(2,1)S(1)} %copy-done.4), channel_id=1, source_target_pairs={{0,32},{32,0},{64,96},{96,64},{128,160},{160,128},{192,224},{224,1... | collective-permute-start | bytes 43016 | tf_op jit(solution)/shard_map/ppermute | solution.py:223
  45.4 1.1 collective-permute-done.1
  46.6 1.5 all-to-all-done.1
  48.0 1.3 shard_map.119
  49.3 3.9 %all-to-all-start.2 = ((bf16[32,8,896]{2,1,0:T(8,128)(2,1)}), bf16[32,8,896]{2,1,0:T(8,128)(2,1)S(1)}, u32[]{:S(2)}, u32[]{:S(2)}) async-start(bf16[32,8,896]{2,1,0:T(8,128)(2,1)} %bitcast.9), calls=%async_computation.2 | async-start | bytes 917504 | tf_op jit(solution)/shard_map/all_to_all | solution.py:173
  53.2 1.9 %collective-permute-start.2 = (bf16[448,576]{1,0:T(8,128)(2,1)S(1)}, bf16[448,576]{1,0:T(8,128)(2,1)S(1)}, u32[]{:S(2)}, u32[]{:S(2)}) collective-permute-start(bf16[448,576]{1,0:T(8,128)(2,1)S(1)} %copy-done), channel_id=1, source_target_pairs={{0,32},{32,0},{64,96},{96,64},{128,160},{160,128},{192,224},{224,1... | collective-permute-start | bytes 1548296 | tf_op jit(solution)/shard_map/ppermute | solution.py:266
  55.2 2.4 %collective-permute-start.3 = (bf16[448,576]{1,0:T(8,128)(2,1)S(1)}, bf16[448,576]{1,0:T(8,128)(2,1)S(1)}, u32[]{:S(2)}, u32[]{:S(2)}) collective-permute-start(bf16[448,576]{1,0:T(8,128)(2,1)S(1)} %copy-done.1), channel_id=1, source_target_pairs={{0,32},{32,0},{64,96},{96,64},{128,160},{160,128},{192,224},{224,1... | collective-permute-start | bytes 1548296 | tf_op jit(solution)/shard_map/ppermute | solution.py:267
  57.6 1.6 %collective-permute-done.3.u2_ref = bf16[448,576]{1,0:T(8,128)(2,1)S(1)} collective-permute-done((bf16[448,576]{1,0:T(8,128)(2,1)S(1)}, bf16[448,576]{1,0:T(8,128)(2,1)S(1)}, u32[]{:S(2)}, u32[]{:S(2)}) %collective-permute-start.3) | collective-permute-done | bytes 516128 | tf_op jit(solution)/shard_map/ppermute | solution.py:267
  59.2 9.2 %all-to-all-done.2 = bf16[32,8,896]{2,1,0:T(8,128)(2,1)S(1)} async-done(((bf16[32,8,896]{2,1,0:T(8,128)(2,1)}), bf16[32,8,896]{2,1,0:T(8,128)(2,1)S(1)}, u32[]{:S(2)}, u32[]{:S(2)}) %all-to-all-start.2) | async-done | bytes 458784 | tf_op jit(solution)/shard_map/all_to_all | solution.py:173
  69.2 4.7 %all-to-all-start.3 = ((bf16[32,8,896]{2,1,0:T(8,128)(2,1)}), bf16[32,8,896]{2,1,0:T(8,128)(2,1)S(1)}, u32[]{:S(2)}, u32[]{:S(2)}) async-start(bf16[32,8,896]{2,1,0:T(8,128)(2,1)} %shard_map.120), calls=%async_computation.3 | async-start | bytes 917504 | tf_op jit(solution)/shard_map/all_to_all | solution.py:173
  74.0 1.9 %collective-permute-start.4 = (bf16[448]{0:T(512)(128)(2,1)S(1)}, bf16[448]{0:T(512)(128)(2,1)S(1)}, u32[]{:S(2)}, u32[]{:S(2)}) collective-permute-start(bf16[448]{0:T(512)(128)(2,1)S(1)} %copy-done.6), channel_id=1, source_target_pairs={{0,32},{32,0},{64,96},{96,64},{128,160},{160,128},{192,224},{224,1... | collective-permute-start | bytes 2696 | tf_op jit(solution)/shard_map/ppermute | solution.py:222
  75.9 1.1 collective-permute-done.4
  77.1 12.6 %all-to-all-done.3 = bf16[32,8,896]{2,1,0:T(8,128)(2,1)S(1)} async-done(((bf16[32,8,896]{2,1,0:T(8,128)(2,1)}), bf16[32,8,896]{2,1,0:T(8,128)(2,1)S(1)}, u32[]{:S(2)}, u32[]{:S(2)}) %all-to-all-start.3) | async-done | bytes 458784 | tf_op jit(solution)/shard_map/all_to_all | solution.py:173
  89.9 1.9 %shard_map.121 = bf16[4,592,128]{2,1,0:T(8,128)(2,1)} custom-call(bf16[256,896]{1,0:T(8,128)(2,1)S(1)} %bitcast.29, bf16[1,896]{1,0:T(2,128)(2,1)S(1)} %broadcast_in_dim.8.gain_ref, bf16[448,576]{1,0:T(8,128)(2,1)S(1)} %copy-done, bf16[448,576]{1,0:T(8,128)(2,1)S(1)} %collective-permute-done.2.g2_ref, bf16[448,576]{1,0:T(8,128)(2,1)S(1)} %copy-done.1, ...), custom_call_target="tpu_custom_call" | custom-call | flops 528482304 | bytes 2097152 | tf_op jit(solution)/shard_map/pallas_call | solution.py:276
  91.7 4.8 %all-to-all-start.4 = ((bf16[4,592,128]{2,1,0:T(8,128)(2,1)}), bf16[4,592,128]{2,1,0:T(8,128)(2,1)S(1)}, u32[]{:S(2)}, u32[]{:S(2)}) async-start(bf16[4,592,128]{2,1,0:T(8,128)(2,1)} %shard_map.121), calls=%async_computation.4 | async-start | bytes 1212416 | tf_op jit(solution)/shard_map/all_to_all | solution.py:173
  96.5 2.0 %collective-permute-start.5 = (bf16[256,448]{1,0:T(8,128)(2,1)S(1)}, bf16[256,448]{1,0:T(8,128)(2,1)S(1)}, u32[]{:S(2)}, u32[]{:S(2)}) collective-permute-start(bf16[256,448]{1,0:T(8,128)(2,1)S(1)} %slice.16), channel_id=1, source_target_pairs={{0,32},{32,0},{64,96},{96,64},{128,160},{160,128},{192,224},{224,1... | collective-permute-start | bytes 688136 | tf_op jit(solution)/shard_map/ppermute | solution.py:284
  98.6 1.5 collective-permute-done.5
  100.1 2.9 %all-to-all-done.4 = bf16[4,592,128]{2,1,0:T(8,128)(2,1)S(1)} async-done(((bf16[4,592,128]{2,1,0:T(8,128)(2,1)}), bf16[4,592,128]{2,1,0:T(8,128)(2,1)S(1)}, u32[]{:S(2)}, u32[]{:S(2)}) %all-to-all-start.4) | async-done | bytes 606240 | tf_op jit(solution)/shard_map/all_to_all | solution.py:173
  103.1 4.3 %collective-permute-start.6 = (bf16[592,128]{1,0:T(8,128)(2,1)S(1)}, bf16[592,128]{1,0:T(8,128)(2,1)S(1)}, u32[]{:S(2)}, u32[]{:S(2)}) collective-permute-start(bf16[592,128]{1,0:T(8,128)(2,1)S(1)} %convert_element_type.30), channel_id=1, source_target_pairs={{0,256},{32,288},{64,320},{96,352},{128,384},{160,416},{192,448},{... | collective-permute-start | bytes 454664 | tf_op jit(solution)/shard_map/ppermute | solution.py:287
  107.4 8.0 %collective-permute-done.6.theirs_ref = bf16[592,128]{1,0:T(8,128)(2,1)S(1)} collective-permute-done((bf16[592,128]{1,0:T(8,128)(2,1)S(1)}, bf16[592,128]{1,0:T(8,128)(2,1)S(1)}, u32[]{:S(2)}, u32[]{:S(2)}) %collective-permute-start.6) | collective-permute-done | bytes 151584 | tf_op jit(solution)/shard_map/ppermute | solution.py:287
  115.4 1.2 shard_map.122
  116.6 6.0 %all-to-all-start.5 = ((bf16[8,288,128]{2,1,0:T(8,128)(2,1)}), bf16[8,288,128]{2,1,0:T(8,128)(2,1)S(1)}, u32[]{:S(2)}, u32[]{:S(2)}) async-start(bf16[8,288,128]{2,1,0:T(8,128)(2,1)} %shard_map.122), calls=%async_computation.5 | async-start | bytes 1179648 | tf_op jit(solution)/shard_map/all_to_all | solution.py:173
  123.0 8.6 %all-to-all-done.5.hidden_ref = bf16[8,288,128]{2,1,0:T(8,128)(2,1)S(1)} async-done(((bf16[8,288,128]{2,1,0:T(8,128)(2,1)}), bf16[8,288,128]{2,1,0:T(8,128)(2,1)S(1)}, u32[]{:S(2)}, u32[]{:S(2)}) %all-to-all-start.5) | async-done | bytes 589856 | tf_op jit(solution)/shard_map/all_to_all | solution.py:173
  131.6 1.8 %shard_map.123 = bf16[256,896]{1,0:T(8,128)(2,1)} custom-call(bf16[512,512]{1,0:T(8,128)(2,1)S(1)} %compare_convert_fusion.pick_ref, bf16[8,288,128]{2,1,0:T(8,128)(2,1)S(1)} %all-to-all-done.5.hidden_ref, bf16[448,576]{1,0:T(8,128)(2,1)S(1)} %bitcast.32), custom_call_target="tpu_custom_call" | custom-call | flops 566231040 | bytes 2097152 | tf_op jit(solution)/shard_map/pallas_call | solution.py:305
  133.4 5.6 %all-to-all-start.6 = ((bf16[32,8,896]{2,1,0:T(8,128)(2,1)}), bf16[32,8,896]{2,1,0:T(8,128)(2,1)S(1)}, u32[]{:S(2)}, u32[]{:S(2)}) async-start(bf16[32,8,896]{2,1,0:T(8,128)(2,1)} %bitcast.17), calls=%async_computation.6 | async-start | bytes 917504 | tf_op jit(solution)/shard_map/all_to_all | solution.py:173
  139.3 15.5 %all-to-all-done.6 = bf16[32,8,896]{2,1,0:T(8,128)(2,1)S(1)} async-done(((bf16[32,8,896]{2,1,0:T(8,128)(2,1)}), bf16[32,8,896]{2,1,0:T(8,128)(2,1)S(1)}, u32[]{:S(2)}, u32[]{:S(2)}) %all-to-all-start.6) | async-done | bytes 458784 | tf_op jit(solution)/shard_map/all_to_all | solution.py:173
  (37 shorter events, 3.6 us)
Async XLA Ops:
  4.8 38.6 %copy-start.4 = (bf16[16,448]{1,0:T(8,128)(2,1)S(1)}, bf16[16,448]{1,0:T(8,128)(2,1)}, u32[]{:S(2)}) copy-start(bf16[16,448]{1,0:T(8,128)(2,1)} %param.19) | copy-start | bytes 43012
  4.8 43.2 %copy-start.3 = (bf16[512,448]{0,1:T(8,128)(2,1)S(1)}, bf16[512,448]{0,1:T(8,128)(2,1)}, u32[]{:S(2)}) copy-start(bf16[512,448]{0,1:T(8,128)(2,1)} %param.18) | copy-start | bytes 1376260
  4.8 31.8 %all-to-all-start = ((bf16[64,4,512]{2,1,0:T(4,128)(2,1)}), bf16[64,4,512]{2,1,0:T(4,128)(2,1)S(1)}, u32[]{:S(2)}, u32[]{:S(2)}) async-start(bf16[64,4,512]{2,1,0:T(4,128)(2,1)} %shard_map.118), calls=%async_computation | async-start | bytes 524288 | tf_op jit(solution)/shard_map/all_to_all | solution.py:173
  21.5 25.0 %collective-permute-start = (bf16[512,448]{0,1:T(8,128)(2,1)}, bf16[512,448]{0,1:T(8,128)(2,1)S(1)}, u32[]{:S(2)}, u32[]{:S(2)}) collective-permute-start(bf16[512,448]{0,1:T(8,128)(2,1)} %param.18), channel_id=1, source_target_pairs={{0,32},{32,0},{64,96},{96,64},{128,160},{160,128},{192,224},{224,1... | collective-permute-start | bytes 1376264 | tf_op jit(solution)/shard_map/ppermute | solution.py:221
  37.9 15.4 %copy-start = (bf16[448,576]{1,0:T(8,128)(2,1)S(1)}, bf16[448,576]{1,0:T(8,128)(2,1)}, u32[]{:S(2)}) copy-start(bf16[448,576]{1,0:T(8,128)(2,1)} %g1_ref) | copy-start | bytes 1548292
  37.9 17.3 %copy-start.1 = (bf16[448,576]{1,0:T(8,128)(2,1)S(1)}, bf16[448,576]{1,0:T(8,128)(2,1)}, u32[]{:S(2)}) copy-start(bf16[448,576]{1,0:T(8,128)(2,1)} %u1_ref) | copy-start | bytes 1548292
  38.6 9.4 %all-to-all-start.1 = ((bf16[4,64,512]{2,1,0:T(8,128)(2,1)}), bf16[4,64,512]{2,1,0:T(8,128)(2,1)S(1)}, u32[]{:S(2)}, u32[]{:S(2)}) async-start(bf16[4,64,512]{2,1,0:T(8,128)(2,1)} %broadcast_in_dim.7), calls=%async_computation.1 | async-start | bytes 524288 | tf_op jit(solution)/shard_map/all_to_all | solution.py:173
  43.4 3.1 %collective-permute-start.1 = (bf16[16,448]{1,0:T(8,128)(2,1)S(1)}, bf16[16,448]{1,0:T(8,128)(2,1)S(1)}, u32[]{:S(2)}, u32[]{:S(2)}) collective-permute-start(bf16[16,448]{1,0:T(8,128)(2,1)S(1)} %copy-done.4), channel_id=1, source_target_pairs={{0,32},{32,0},{64,96},{96,64},{128,160},{160,128},{192,224},{224,1... | collective-permute-start | bytes 43016 | tf_op jit(solution)/shard_map/ppermute | solution.py:223
  48.0 26.0 %copy-start.6 = (bf16[448]{0:T(512)(128)(2,1)S(1)}, bf16[448]{0:T(512)(128)(2,1)}, u32[]{:S(2)}) copy-start(bf16[448]{0:T(512)(128)(2,1)} %param.20) | copy-start | bytes 2692
  49.3 19.0 %all-to-all-start.2 = ((bf16[32,8,896]{2,1,0:T(8,128)(2,1)}), bf16[32,8,896]{2,1,0:T(8,128)(2,1)S(1)}, u32[]{:S(2)}, u32[]{:S(2)}) async-start(bf16[32,8,896]{2,1,0:T(8,128)(2,1)} %bitcast.9), calls=%async_computation.2 | async-start | bytes 917504 | tf_op jit(solution)/shard_map/all_to_all | solution.py:173
  53.2 4.4 %collective-permute-start.2 = (bf16[448,576]{1,0:T(8,128)(2,1)S(1)}, bf16[448,576]{1,0:T(8,128)(2,1)S(1)}, u32[]{:S(2)}, u32[]{:S(2)}) collective-permute-start(bf16[448,576]{1,0:T(8,128)(2,1)S(1)} %copy-done), channel_id=1, source_target_pairs={{0,32},{32,0},{64,96},{96,64},{128,160},{160,128},{192,224},{224,1... | collective-permute-start | bytes 1548296 | tf_op jit(solution)/shard_map/ppermute | solution.py:266
  55.2 4.0 %collective-permute-start.3 = (bf16[448,576]{1,0:T(8,128)(2,1)S(1)}, bf16[448,576]{1,0:T(8,128)(2,1)S(1)}, u32[]{:S(2)}, u32[]{:S(2)}) collective-permute-start(bf16[448,576]{1,0:T(8,128)(2,1)S(1)} %copy-done.1), channel_id=1, source_target_pairs={{0,32},{32,0},{64,96},{96,64},{128,160},{160,128},{192,224},{224,1... | collective-permute-start | bytes 1548296 | tf_op jit(solution)/shard_map/ppermute | solution.py:267
  69.2 20.5 %all-to-all-start.3 = ((bf16[32,8,896]{2,1,0:T(8,128)(2,1)}), bf16[32,8,896]{2,1,0:T(8,128)(2,1)S(1)}, u32[]{:S(2)}, u32[]{:S(2)}) async-start(bf16[32,8,896]{2,1,0:T(8,128)(2,1)} %shard_map.120), calls=%async_computation.3 | async-start | bytes 917504 | tf_op jit(solution)/shard_map/all_to_all | solution.py:173
  74.0 3.0 %collective-permute-start.4 = (bf16[448]{0:T(512)(128)(2,1)S(1)}, bf16[448]{0:T(512)(128)(2,1)S(1)}, u32[]{:S(2)}, u32[]{:S(2)}) collective-permute-start(bf16[448]{0:T(512)(128)(2,1)S(1)} %copy-done.6), channel_id=1, source_target_pairs={{0,32},{32,0},{64,96},{96,64},{128,160},{160,128},{192,224},{224,1... | collective-permute-start | bytes 2696 | tf_op jit(solution)/shard_map/ppermute | solution.py:222
  91.7 11.3 %all-to-all-start.4 = ((bf16[4,592,128]{2,1,0:T(8,128)(2,1)}), bf16[4,592,128]{2,1,0:T(8,128)(2,1)S(1)}, u32[]{:S(2)}, u32[]{:S(2)}) async-start(bf16[4,592,128]{2,1,0:T(8,128)(2,1)} %shard_map.121), calls=%async_computation.4 | async-start | bytes 1212416 | tf_op jit(solution)/shard_map/all_to_all | solution.py:173
  96.5 26.1 %copy-start.5 = (s32[512]{0:T(512)S(1)}, s32[512]{0:T(512)}, u32[]{:S(2)}) copy-start(s32[512]{0:T(512)} %param.16) | copy-start | bytes 6148
  96.5 3.5 %collective-permute-start.5 = (bf16[256,448]{1,0:T(8,128)(2,1)S(1)}, bf16[256,448]{1,0:T(8,128)(2,1)S(1)}, u32[]{:S(2)}, u32[]{:S(2)}) collective-permute-start(bf16[256,448]{1,0:T(8,128)(2,1)S(1)} %slice.16), channel_id=1, source_target_pairs={{0,32},{32,0},{64,96},{96,64},{128,160},{160,128},{192,224},{224,1... | collective-permute-start | bytes 688136 | tf_op jit(solution)/shard_map/ppermute | solution.py:284
  103.0 28.6 %copy-start.2 = (bf16[576,448]{0,1:T(8,128)(2,1)S(1)}, bf16[576,448]{0,1:T(8,128)(2,1)}, u32[]{:S(2)}) copy-start(bf16[576,448]{0,1:T(8,128)(2,1)} %param.23) | copy-start | bytes 1548292
  103.1 12.4 %collective-permute-start.6 = (bf16[592,128]{1,0:T(8,128)(2,1)S(1)}, bf16[592,128]{1,0:T(8,128)(2,1)S(1)}, u32[]{:S(2)}, u32[]{:S(2)}) collective-permute-start(bf16[592,128]{1,0:T(8,128)(2,1)S(1)} %convert_element_type.30), channel_id=1, source_target_pairs={{0,256},{32,288},{64,320},{96,352},{128,384},{160,416},{192,448},{... | collective-permute-start | bytes 454664 | tf_op jit(solution)/shard_map/ppermute | solution.py:287
  116.6 14.9 %all-to-all-start.5 = ((bf16[8,288,128]{2,1,0:T(8,128)(2,1)}), bf16[8,288,128]{2,1,0:T(8,128)(2,1)S(1)}, u32[]{:S(2)}, u32[]{:S(2)}) async-start(bf16[8,288,128]{2,1,0:T(8,128)(2,1)} %shard_map.122), calls=%async_computation.5 | async-start | bytes 1179648 | tf_op jit(solution)/shard_map/all_to_all | solution.py:173
  133.4 21.4 %all-to-all-start.6 = ((bf16[32,8,896]{2,1,0:T(8,128)(2,1)}), bf16[32,8,896]{2,1,0:T(8,128)(2,1)S(1)}, u32[]{:S(2)}, u32[]{:S(2)}) async-start(bf16[32,8,896]{2,1,0:T(8,128)(2,1)} %bitcast.17), calls=%async_computation.6 | async-start | bytes 917504 | tf_op jit(solution)/shard_map/all_to_all | solution.py:173

commit v4 on v3

--- a/solution.py
+++ b/solution.py
@@ -28,6 +28,23 @@
         compiler_params=pltpu.CompilerParams(vmem_limit_bytes=24 * 2**20),
         cost_estimate=pl.CostEstimate(flops=flops, bytes_accessed=2**21, transcendentals=0),
     )
+
+
+def value_kernel(owned_ref, w_ref, out_ref):
+    rows, heads, lat = owned_ref.shape
+    size = w_ref.shape[1] // heads
+    owned = owned_ref[...].reshape(rows * heads, lat)
+    full = jnp.dot(owned, w_ref[...], preferred_element_type=F32)
+    shape = (rows * heads, heads * size)
+    head = lax.rem(lax.broadcasted_iota(jnp.int32, shape, 0), heads)
+    block = lax.div(lax.broadcasted_iota(jnp.int32, shape, 1), size)
+    full = jnp.where(head == block, full, 0.0).astype(BF)
+    at_row = lax.broadcasted_iota(jnp.int32, (rows, rows * heads), 0)
+    source = lax.div(lax.broadcasted_iota(jnp.int32, (rows, rows * heads), 1), heads)
+    join = jnp.where(at_row == source, 1.0, 0.0).astype(BF)
+    values = jnp.dot(join, full, preferred_element_type=F32).astype(BF)
+    for q in range(out_ref.shape[0]):
+        out_ref[q] = values
 
 
 def attn_kernel(first_ref, heads_ref, w1_ref, w2_ref, res_ref, out_ref):
@@ -238,10 +255,18 @@
     both_y = [
         [at(y, x, c) * n_tp + j for y in two for j in range(n_tp)] for x in xs for c in two
     ]
+    heads, _, size = value_up.shape
+    copies, value_up = lax.optimization_barrier((copies, value_up))
     owned = exchange(copies, ("dp", "tp"), both_y)
-    head_values = jnp.einsum("rhl,hlv->rhv", owned, value_up, preferred_element_type=jnp.float32)
-    head_values = head_values.astype(jnp.bfloat16).reshape(owned.shape[0], -1)
-    heads_set = gather_rows(head_values, "dp", n_x, along_x)
+    maps = value_up.transpose(1, 0, 2).reshape(LAT, heads * size)
+    owned, maps = lax.optimization_barrier((owned, maps))
+    copies = call(
+        value_kernel,
+        jax.ShapeDtypeStruct((n_x, owned.shape[0], heads * size), BF),
+        [VMEM] * 2,
+        2 * owned.size * heads * size,
+    )(owned, maps)
+    heads_set = exchange(copies, "dp", along_x).reshape(-1, heads * size)
     places = jnp.arange(n_dp // 2 * n_tp)
     set_dp = (places // n_tp % 2 * n_x + places // (2 * n_tp)) * 2
     set_rows = set_dp * n_tp + places % n_tp

time: 158 us -> 157 us (level)
  transfers between devices with their start and end apart: 14 -> 14, of which waited for: 12 -> 12; matrix products, arithmetic and copies ran while one was open for 2% -> 1% of each run, Pallas kernels for 0% -> 1%
where the time goes in v4:
time: 157 us; the launch traced here: 155 us
  waiting for transfers between devices  75.5 us (48%)
  starting transfers between devices  62.9 us (40%)
  Pallas kernels  12.3 us (8%)
  local copies, waits for them, and re-layouts  1.64 us (1%)
    all_to_all x7, waiting for transfers between devices, exchange(): lax.all_to_all(array, axis, split_axis=0, concat_axis=0, axis_index_group...  62.2 us
    all_to_all x7, starting transfers between devices, exchange(): lax.all_to_all(array, axis, split_axis=0, concat_axis=0, axis_index_group...  46.5 us
    ppermute x1, waiting for transfers between devices, local(): theirs = lax.ppermute(sums.astype(BF), 'dp', across_y)  8.04 us
    ppermute x1, starting transfers between devices, local(): theirs = lax.ppermute(sums.astype(BF), 'dp', across_y)  4.3 us
    pallas_call x1, Pallas kernels, local(): pl.pallas_call(attend_kernel, out_shape=jax.ShapeDtypeStruct((2 * n_tp, q...  4.14 us
  transfers between devices with their start and end apart: 14, of which 12 were waited for; matrix products, arithmetic and copies ran while one was open for 1% of the time, Pallas kernels for 1%

profile of v4, /device:TPU:6, one launch (start us, length us, event | category | flops | bytes accessed | tf_op | source)
XLA Modules:
  0.0 154.9 jit_solution(2375051533978312331)
XLA Ops:
  0.7 4.1 %shard_map.118 = bf16[64,4,512]{2,1,0:T(4,128)(2,1)} custom-call(s32[1]{0:T(128)S(6)} %copy.18.length_ref, bf16[576,128]{1,0:T(8,128)(2,1)} %bitcast.35, bf16[1,576]{1,0:T(2,128)(2,1)} %new_hbm.1, bf16[576,1792]{1,0:T(8,128)(2,1)} %bitcast.34), custom_call_target="tpu_custom_call" | custom-call | tf_op jit(solution)/shard_map/pallas_call | solution.py:242
  4.8 16.7 %all-to-all-start = ((bf16[64,4,512]{2,1,0:T(4,128)(2,1)}), bf16[64,4,512]{2,1,0:T(4,128)(2,1)S(1)}, u32[]{:S(2)}, u32[]{:S(2)}) async-start(bf16[64,4,512]{2,1,0:T(4,128)(2,1)} %shard_map.118), calls=%async_computation | async-start | bytes 524288 | tf_op jit(solution)/shard_map/all_to_all | solution.py:190
  21.5 1.9 %collective-permute-start = (bf16[512,448]{0,1:T(8,128)(2,1)}, bf16[512,448]{0,1:T(8,128)(2,1)S(1)}, u32[]{:S(2)}, u32[]{:S(2)}) collective-permute-start(bf16[512,448]{0,1:T(8,128)(2,1)} %param.18), channel_id=1, source_target_pairs={{0,32},{32,0},{64,96},{96,64},{128,160},{160,128},{192,224},{224,1... | collective-permute-start | bytes 1376264 | tf_op jit(solution)/shard_map/ppermute | solution.py:238
  24.6 12.0 %all-to-all-done.owned_ref = bf16[64,4,512]{2,1,0:T(4,128)(2,1)S(1)} async-done(((bf16[64,4,512]{2,1,0:T(4,128)(2,1)}), bf16[64,4,512]{2,1,0:T(4,128)(2,1)S(1)}, u32[]{:S(2)}, u32[]{:S(2)}) %all-to-all-start) | async-done | bytes 262176 | tf_op jit(solution)/shard_map/all_to_all | solution.py:190
  36.6 1.1 shard_map.119
  37.7 4.8 %all-to-all-start.1 = ((bf16[4,64,512]{2,1,0:T(8,128)(2,1)}), bf16[4,64,512]{2,1,0:T(8,128)(2,1)S(1)}, u32[]{:S(2)}, u32[]{:S(2)}) async-start(bf16[4,64,512]{2,1,0:T(8,128)(2,1)} %shard_map.119), calls=%async_computation.1 | async-start | bytes 524288 | tf_op jit(solution)/shard_map/all_to_all | solution.py:190
  42.5 1.9 %collective-permute-start.1 = (bf16[16,448]{1,0:T(8,128)(2,1)S(1)}, bf16[16,448]{1,0:T(8,128)(2,1)S(1)}, u32[]{:S(2)}, u32[]{:S(2)}) collective-permute-start(bf16[16,448]{1,0:T(8,128)(2,1)S(1)} %copy-done.4), channel_id=1, source_target_pairs={{0,32},{32,0},{64,96},{96,64},{128,160},{160,128},{192,224},{224,1... | collective-permute-start | bytes 43016 | tf_op jit(solution)/shard_map/ppermute | solution.py:240
  44.5 1.1 collective-permute-done.1
  45.7 1.5 all-to-all-done.1
  47.1 1.3 shard_map.120
  48.5 3.9 %all-to-all-start.2 = ((bf16[32,8,896]{2,1,0:T(8,128)(2,1)}), bf16[32,8,896]{2,1,0:T(8,128)(2,1)S(1)}, u32[]{:S(2)}, u32[]{:S(2)}) async-start(bf16[32,8,896]{2,1,0:T(8,128)(2,1)} %bitcast.9), calls=%async_computation.2 | async-start | bytes 917504 | tf_op jit(solution)/shard_map/all_to_all | solution.py:190
  52.4 1.9 %collective-permute-start.2 = (bf16[448,576]{1,0:T(8,128)(2,1)S(1)}, bf16[448,576]{1,0:T(8,128)(2,1)S(1)}, u32[]{:S(2)}, u32[]{:S(2)}) collective-permute-start(bf16[448,576]{1,0:T(8,128)(2,1)S(1)} %copy-done), channel_id=1, source_target_pairs={{0,32},{32,0},{64,96},{96,64},{128,160},{160,128},{192,224},{224,1... | collective-permute-start | bytes 1548296 | tf_op jit(solution)/shard_map/ppermute | solution.py:291
  54.3 2.4 %collective-permute-start.3 = (bf16[448,576]{1,0:T(8,128)(2,1)S(1)}, bf16[448,576]{1,0:T(8,128)(2,1)S(1)}, u32[]{:S(2)}, u32[]{:S(2)}) collective-permute-start(bf16[448,576]{1,0:T(8,128)(2,1)S(1)} %copy-done.1), channel_id=1, source_target_pairs={{0,32},{32,0},{64,96},{96,64},{128,160},{160,128},{192,224},{224,1... | collective-permute-start | bytes 1548296 | tf_op jit(solution)/shard_map/ppermute | solution.py:292
  56.7 1.6 %collective-permute-done.3.u2_ref = bf16[448,576]{1,0:T(8,128)(2,1)S(1)} collective-permute-done((bf16[448,576]{1,0:T(8,128)(2,1)S(1)}, bf16[448,576]{1,0:T(8,128)(2,1)S(1)}, u32[]{:S(2)}, u32[]{:S(2)}) %collective-permute-start.3) | collective-permute-done | bytes 516128 | tf_op jit(solution)/shard_map/ppermute | solution.py:292
  58.3 9.2 %all-to-all-done.2 = bf16[32,8,896]{2,1,0:T(8,128)(2,1)S(1)} async-done(((bf16[32,8,896]{2,1,0:T(8,128)(2,1)}), bf16[32,8,896]{2,1,0:T(8,128)(2,1)S(1)}, u32[]{:S(2)}, u32[]{:S(2)}) %all-to-all-start.2) | async-done | bytes 458784 | tf_op jit(solution)/shard_map/all_to_all | solution.py:190
  68.4 4.7 %all-to-all-start.3 = ((bf16[32,8,896]{2,1,0:T(8,128)(2,1)}), bf16[32,8,896]{2,1,0:T(8,128)(2,1)S(1)}, u32[]{:S(2)}, u32[]{:S(2)}) async-start(bf16[32,8,896]{2,1,0:T(8,128)(2,1)} %shard_map.121), calls=%async_computation.3 | async-start | bytes 917504 | tf_op jit(solution)/shard_map/all_to_all | solution.py:190
  73.1 1.9 %collective-permute-start.4 = (bf16[448]{0:T(512)(128)(2,1)S(1)}, bf16[448]{0:T(512)(128)(2,1)S(1)}, u32[]{:S(2)}, u32[]{:S(2)}) collective-permute-start(bf16[448]{0:T(512)(128)(2,1)S(1)} %copy-done.6), channel_id=1, source_target_pairs={{0,32},{32,0},{64,96},{96,64},{128,160},{160,128},{192,224},{224,1... | collective-permute-start | bytes 2696 | tf_op jit(solution)/shard_map/ppermute | solution.py:239
  75.1 1.1 collective-permute-done.4
  76.2 12.6 %all-to-all-done.3 = bf16[32,8,896]{2,1,0:T(8,128)(2,1)S(1)} async-done(((bf16[32,8,896]{2,1,0:T(8,128)(2,1)}), bf16[32,8,896]{2,1,0:T(8,128)(2,1)S(1)}, u32[]{:S(2)}, u32[]{:S(2)}) %all-to-all-start.3) | async-done | bytes 458784 | tf_op jit(solution)/shard_map/all_to_all | solution.py:190
  89.0 1.9 %shard_map.122 = bf16[4,592,128]{2,1,0:T(8,128)(2,1)} custom-call(bf16[256,896]{1,0:T(8,128)(2,1)S(1)} %bitcast.28, bf16[1,896]{1,0:T(2,128)(2,1)S(1)} %broadcast_in_dim.2.gain_ref, bf16[448,576]{1,0:T(8,128)(2,1)S(1)} %copy-done, bf16[448,576]{1,0:T(8,128)(2,1)S(1)} %collective-permute-done.2.g2_ref, bf16[448,576]{1,0:T(8,128)(2,1)S(1)} %copy-done.1, ...), custom_call_target="tpu_custom_call" | custom-call | flops 528482304 | bytes 2097152 | tf_op jit(solution)/shard_map/pallas_call | solution.py:301
  90.8 4.8 %all-to-all-start.4 = ((bf16[4,592,128]{2,1,0:T(8,128)(2,1)}), bf16[4,592,128]{2,1,0:T(8,128)(2,1)S(1)}, u32[]{:S(2)}, u32[]{:S(2)}) async-start(bf16[4,592,128]{2,1,0:T(8,128)(2,1)} %shard_map.122), calls=%async_computation.4 | async-start | bytes 1212416 | tf_op jit(solution)/shard_map/all_to_all | solution.py:190
  95.6 2.0 %collective-permute-start.5 = (bf16[256,448]{1,0:T(8,128)(2,1)S(1)}, bf16[256,448]{1,0:T(8,128)(2,1)S(1)}, u32[]{:S(2)}, u32[]{:S(2)}) collective-permute-start(bf16[256,448]{1,0:T(8,128)(2,1)S(1)} %slice.16), channel_id=1, source_target_pairs={{0,32},{32,0},{64,96},{96,64},{128,160},{160,128},{192,224},{224,1... | collective-permute-start | bytes 688136 | tf_op jit(solution)/shard_map/ppermute | solution.py:309
  97.7 1.5 collective-permute-done.5
  99.2 2.9 %all-to-all-done.4 = bf16[4,592,128]{2,1,0:T(8,128)(2,1)S(1)} async-done(((bf16[4,592,128]{2,1,0:T(8,128)(2,1)}), bf16[4,592,128]{2,1,0:T(8,128)(2,1)S(1)}, u32[]{:S(2)}, u32[]{:S(2)}) %all-to-all-start.4) | async-done | bytes 606240 | tf_op jit(solution)/shard_map/all_to_all | solution.py:190
  102.2 4.3 %collective-permute-start.6 = (bf16[592,128]{1,0:T(8,128)(2,1)S(1)}, bf16[592,128]{1,0:T(8,128)(2,1)S(1)}, u32[]{:S(2)}, u32[]{:S(2)}) collective-permute-start(bf16[592,128]{1,0:T(8,128)(2,1)S(1)} %convert_element_type.22), channel_id=1, source_target_pairs={{0,256},{32,288},{64,320},{96,352},{128,384},{160,416},{192,448},{... | collective-permute-start | bytes 454664 | tf_op jit(solution)/shard_map/ppermute | solution.py:312
  106.5 8.0 %collective-permute-done.6.theirs_ref = bf16[592,128]{1,0:T(8,128)(2,1)S(1)} collective-permute-done((bf16[592,128]{1,0:T(8,128)(2,1)S(1)}, bf16[592,128]{1,0:T(8,128)(2,1)S(1)}, u32[]{:S(2)}, u32[]{:S(2)}) %collective-permute-start.6) | collective-permute-done | bytes 151584 | tf_op jit(solution)/shard_map/ppermute | solution.py:312
  114.5 1.2 shard_map.123
  115.7 6.0 %all-to-all-start.5 = ((bf16[8,288,128]{2,1,0:T(8,128)(2,1)}), bf16[8,288,128]{2,1,0:T(8,128)(2,1)S(1)}, u32[]{:S(2)}, u32[]{:S(2)}) async-start(bf16[8,288,128]{2,1,0:T(8,128)(2,1)} %shard_map.123), calls=%async_computation.5 | async-start | bytes 1179648 | tf_op jit(solution)/shard_map/all_to_all | solution.py:190
  122.1 8.6 %all-to-all-done.5.hidden_ref = bf16[8,288,128]{2,1,0:T(8,128)(2,1)S(1)} async-done(((bf16[8,288,128]{2,1,0:T(8,128)(2,1)}), bf16[8,288,128]{2,1,0:T(8,128)(2,1)S(1)}, u32[]{:S(2)}, u32[]{:S(2)}) %all-to-all-start.5) | async-done | bytes 589856 | tf_op jit(solution)/shard_map/all_to_all | solution.py:190
  130.7 1.8 %shard_map.124 = bf16[256,896]{1,0:T(8,128)(2,1)} custom-call(bf16[512,512]{1,0:T(8,128)(2,1)S(1)} %compare_convert_fusion.pick_ref, bf16[8,288,128]{2,1,0:T(8,128)(2,1)S(1)} %all-to-all-done.5.hidden_ref, bf16[448,576]{1,0:T(8,128)(2,1)S(1)} %bitcast.31), custom_call_target="tpu_custom_call" | custom-call | flops 566231040 | bytes 2097152 | tf_op jit(solution)/shard_map/pallas_call | solution.py:330
  132.5 5.6 %all-to-all-start.6 = ((bf16[32,8,896]{2,1,0:T(8,128)(2,1)}), bf16[32,8,896]{2,1,0:T(8,128)(2,1)S(1)}, u32[]{:S(2)}, u32[]{:S(2)}) async-start(bf16[32,8,896]{2,1,0:T(8,128)(2,1)} %bitcast.17), calls=%async_computation.6 | async-start | bytes 917504 | tf_op jit(solution)/shard_map/all_to_all | solution.py:190
  138.4 15.5 %all-to-all-done.6 = bf16[32,8,896]{2,1,0:T(8,128)(2,1)S(1)} async-done(((bf16[32,8,896]{2,1,0:T(8,128)(2,1)}), bf16[32,8,896]{2,1,0:T(8,128)(2,1)S(1)}, u32[]{:S(2)}, u32[]{:S(2)}) %all-to-all-start.6) | async-done | bytes 458784 | tf_op jit(solution)/shard_map/all_to_all | solution.py:190
  (36 shorter events, 4.0 us)
Async XLA Ops:
  4.8 37.7 %copy-start.4 = (bf16[16,448]{1,0:T(8,128)(2,1)S(1)}, bf16[16,448]{1,0:T(8,128)(2,1)}, u32[]{:S(2)}) copy-start(bf16[16,448]{1,0:T(8,128)(2,1)} %param.19) | copy-start | bytes 43012
  4.8 42.3 %copy-start.3 = (bf16[512,448]{0,1:T(8,128)(2,1)S(1)}, bf16[512,448]{0,1:T(8,128)(2,1)}, u32[]{:S(2)}) copy-start(bf16[512,448]{0,1:T(8,128)(2,1)} %param.18) | copy-start | bytes 1376260
  4.8 31.8 %all-to-all-start = ((bf16[64,4,512]{2,1,0:T(4,128)(2,1)}), bf16[64,4,512]{2,1,0:T(4,128)(2,1)S(1)}, u32[]{:S(2)}, u32[]{:S(2)}) async-start(bf16[64,4,512]{2,1,0:T(4,128)(2,1)} %shard_map.118), calls=%async_computation | async-start | bytes 524288 | tf_op jit(solution)/shard_map/all_to_all | solution.py:190
  21.5 24.1 %collective-permute-start = (bf16[512,448]{0,1:T(8,128)(2,1)}, bf16[512,448]{0,1:T(8,128)(2,1)S(1)}, u32[]{:S(2)}, u32[]{:S(2)}) collective-permute-start(bf16[512,448]{0,1:T(8,128)(2,1)} %param.18), channel_id=1, source_target_pairs={{0,32},{32,0},{64,96},{96,64},{128,160},{160,128},{192,224},{224,1... | collective-permute-start | bytes 1376264 | tf_op jit(solution)/shard_map/ppermute | solution.py:238
  24.6 27.8 %copy-start = (bf16[448,576]{1,0:T(8,128)(2,1)S(1)}, bf16[448,576]{1,0:T(8,128)(2,1)}, u32[]{:S(2)}) copy-start(bf16[448,576]{1,0:T(8,128)(2,1)} %g1_ref) | copy-start | bytes 1548292
  24.6 29.7 %copy-start.1 = (bf16[448,576]{1,0:T(8,128)(2,1)S(1)}, bf16[448,576]{1,0:T(8,128)(2,1)}, u32[]{:S(2)}) copy-start(bf16[448,576]{1,0:T(8,128)(2,1)} %u1_ref) | copy-start | bytes 1548292
  37.7 9.4 %all-to-all-start.1 = ((bf16[4,64,512]{2,1,0:T(8,128)(2,1)}), bf16[4,64,512]{2,1,0:T(8,128)(2,1)S(1)}, u32[]{:S(2)}, u32[]{:S(2)}) async-start(bf16[4,64,512]{2,1,0:T(8,128)(2,1)} %shard_map.119), calls=%async_computation.1 | async-start | bytes 524288 | tf_op jit(solution)/shard_map/all_to_all | solution.py:190
  42.5 3.1 %collective-permute-start.1 = (bf16[16,448]{1,0:T(8,128)(2,1)S(1)}, bf16[16,448]{1,0:T(8,128)(2,1)S(1)}, u32[]{:S(2)}, u32[]{:S(2)}) collective-permute-start(bf16[16,448]{1,0:T(8,128)(2,1)S(1)} %copy-done.4), channel_id=1, source_target_pairs={{0,32},{32,0},{64,96},{96,64},{128,160},{160,128},{192,224},{224,1... | collective-permute-start | bytes 43016 | tf_op jit(solution)/shard_map/ppermute | solution.py:240
  47.1 26.0 %copy-start.6 = (bf16[448]{0:T(512)(128)(2,1)S(1)}, bf16[448]{0:T(512)(128)(2,1)}, u32[]{:S(2)}) copy-start(bf16[448]{0:T(512)(128)(2,1)} %param.20) | copy-start | bytes 2692
  48.5 19.1 %all-to-all-start.2 = ((bf16[32,8,896]{2,1,0:T(8,128)(2,1)}), bf16[32,8,896]{2,1,0:T(8,128)(2,1)S(1)}, u32[]{:S(2)}, u32[]{:S(2)}) async-start(bf16[32,8,896]{2,1,0:T(8,128)(2,1)} %bitcast.9), calls=%async_computation.2 | async-start | bytes 917504 | tf_op jit(solution)/shard_map/all_to_all | solution.py:190
  52.4 4.4 %collective-permute-start.2 = (bf16[448,576]{1,0:T(8,128)(2,1)S(1)}, bf16[448,576]{1,0:T(8,128)(2,1)S(1)}, u32[]{:S(2)}, u32[]{:S(2)}) collective-permute-start(bf16[448,576]{1,0:T(8,128)(2,1)S(1)} %copy-done), channel_id=1, source_target_pairs={{0,32},{32,0},{64,96},{96,64},{128,160},{160,128},{192,224},{224,1... | collective-permute-start | bytes 1548296 | tf_op jit(solution)/shard_map/ppermute | solution.py:291
  54.3 4.0 %collective-permute-start.3 = (bf16[448,576]{1,0:T(8,128)(2,1)S(1)}, bf16[448,576]{1,0:T(8,128)(2,1)S(1)}, u32[]{:S(2)}, u32[]{:S(2)}) collective-permute-start(bf16[448,576]{1,0:T(8,128)(2,1)S(1)} %copy-done.1), channel_id=1, source_target_pairs={{0,32},{32,0},{64,96},{96,64},{128,160},{160,128},{192,224},{224,1... | collective-permute-start | bytes 1548296 | tf_op jit(solution)/shard_map/ppermute | solution.py:292
  68.4 20.5 %all-to-all-start.3 = ((bf16[32,8,896]{2,1,0:T(8,128)(2,1)}), bf16[32,8,896]{2,1,0:T(8,128)(2,1)S(1)}, u32[]{:S(2)}, u32[]{:S(2)}) async-start(bf16[32,8,896]{2,1,0:T(8,128)(2,1)} %shard_map.121), calls=%async_computation.3 | async-start | bytes 917504 | tf_op jit(solution)/shard_map/all_to_all | solution.py:190
  73.1 3.0 %collective-permute-start.4 = (bf16[448]{0:T(512)(128)(2,1)S(1)}, bf16[448]{0:T(512)(128)(2,1)S(1)}, u32[]{:S(2)}, u32[]{:S(2)}) collective-permute-start(bf16[448]{0:T(512)(128)(2,1)S(1)} %copy-done.6), channel_id=1, source_target_pairs={{0,32},{32,0},{64,96},{96,64},{128,160},{160,128},{192,224},{224,1... | collective-permute-start | bytes 2696 | tf_op jit(solution)/shard_map/ppermute | solution.py:239
  90.8 11.2 %all-to-all-start.4 = ((bf16[4,592,128]{2,1,0:T(8,128)(2,1)}), bf16[4,592,128]{2,1,0:T(8,128)(2,1)S(1)}, u32[]{:S(2)}, u32[]{:S(2)}) async-start(bf16[4,592,128]{2,1,0:T(8,128)(2,1)} %shard_map.122), calls=%async_computation.4 | async-start | bytes 1212416 | tf_op jit(solution)/shard_map/all_to_all | solution.py:190
  95.6 26.1 %copy-start.5 = (s32[512]{0:T(512)S(1)}, s32[512]{0:T(512)}, u32[]{:S(2)}) copy-start(s32[512]{0:T(512)} %param.16) | copy-start | bytes 6148
  95.6 3.5 %collective-permute-start.5 = (bf16[256,448]{1,0:T(8,128)(2,1)S(1)}, bf16[256,448]{1,0:T(8,128)(2,1)S(1)}, u32[]{:S(2)}, u32[]{:S(2)}) collective-permute-start(bf16[256,448]{1,0:T(8,128)(2,1)S(1)} %slice.16), channel_id=1, source_target_pairs={{0,32},{32,0},{64,96},{96,64},{128,160},{160,128},{192,224},{224,1... | collective-permute-start | bytes 688136 | tf_op jit(solution)/shard_map/ppermute | solution.py:309
  102.1 28.6 %copy-start.2 = (bf16[576,448]{0,1:T(8,128)(2,1)S(1)}, bf16[576,448]{0,1:T(8,128)(2,1)}, u32[]{:S(2)}) copy-start(bf16[576,448]{0,1:T(8,128)(2,1)} %param.23) | copy-start | bytes 1548292
  102.2 12.4 %collective-permute-start.6 = (bf16[592,128]{1,0:T(8,128)(2,1)S(1)}, bf16[592,128]{1,0:T(8,128)(2,1)S(1)}, u32[]{:S(2)}, u32[]{:S(2)}) collective-permute-start(bf16[592,128]{1,0:T(8,128)(2,1)S(1)} %convert_element_type.22), channel_id=1, source_target_pairs={{0,256},{32,288},{64,320},{96,352},{128,384},{160,416},{192,448},{... | collective-permute-start | bytes 454664 | tf_op jit(solution)/shard_map/ppermute | solution.py:312
  115.7 14.9 %all-to-all-start.5 = ((bf16[8,288,128]{2,1,0:T(8,128)(2,1)}), bf16[8,288,128]{2,1,0:T(8,128)(2,1)S(1)}, u32[]{:S(2)}, u32[]{:S(2)}) async-start(bf16[8,288,128]{2,1,0:T(8,128)(2,1)} %shard_map.123), calls=%async_computation.5 | async-start | bytes 1179648 | tf_op jit(solution)/shard_map/all_to_all | solution.py:190
  132.5 21.4 %all-to-all-start.6 = ((bf16[32,8,896]{2,1,0:T(8,128)(2,1)}), bf16[32,8,896]{2,1,0:T(8,128)(2,1)S(1)}, u32[]{:S(2)}, u32[]{:S(2)}) async-start(bf16[32,8,896]{2,1,0:T(8,128)(2,1)} %bitcast.17), calls=%async_computation.6 | async-start | bytes 917504 | tf_op jit(solution)/shard_map/all_to_all | solution.py:190

commit v5 on v4

--- a/solution.py
+++ b/solution.py
@@ -99,11 +99,11 @@
         rest = jnp.concatenate([rest[:, : LANES // 2], rest[:, LANES // 2 :]], axis=0)
         blocks.append(jnp.concatenate(tiles + [rest], axis=1))
     hidden = jnp.concatenate(blocks, axis=0)
-    parts = []
-    for k in range(2):
-        pick = pick_ref[k * half : (k + 1) * half]
-        rows = jnp.dot(pick, hidden, preferred_element_type=F32).astype(BF)
-        parts.append(lax.dot_general(rows, w_ref[...], NT, preferred_element_type=F32))
+    terms = lax.dot_general(hidden, w_ref[...], NT, preferred_element_type=F32).astype(BF)
+    parts = [
+        jnp.dot(pick_ref[k * half : (k + 1) * half], terms, preferred_element_type=F32)
+        for k in range(2)
+    ]
     out_ref[...] = jnp.concatenate(parts, axis=1).astype(BF)
 
 
@@ -178,8 +178,8 @@
     share = 1.0 / total
     own = (jnp.exp(own - highest) * share).astype(BF).astype(F32)
     probs = jnp.concatenate([(expo * share).astype(BF) for expo in expos], axis=1)
-    latent = lax.dot_general(probs, held[:LAT, :], NT, preferred_element_type=F32)
-    latent = latent + own * new[:, :LAT]
+    latent = lax.dot_general(held[:LAT, :], probs, NT, preferred_element_type=F32)
+    latent = latent.T + own * new[:, :LAT]
     count, heads = out_ref.shape[0] // 2, out_ref.shape[1]
     latent = latent.reshape(count, heads, LAT).astype(BF)
     out_ref[:count] = latent
@@ -333,14 +333,16 @@
         [VMEM] * 3,
         2 * rows * ff * (rows + width),
     )(pick, hidden, down_weight.T)
-    ffn_own = sum_scatter(ffn_terms, "tp", n_tp)
-    ffn_own = jnp.concatenate([ffn_own[:, :width], ffn_own[:, width:]], axis=0)
     wanted = lax.dynamic_slice_in_dim(order, tp * own_count, own_count)
     pick1 = (wanted[:, None] == (set_rows + core * n_tp)[None, :]).astype(BF)
     pick2 = (wanted[:, None] == (set_rows + (1 - core) * n_tp)[None, :]).astype(BF)
     mid_rows = jnp.dot(pick1, mid_here, preferred_element_type=F32) + jnp.dot(
         pick2, mid_rest, preferred_element_type=F32
     )
+    got = exchange(ffn_terms, "tp", None)
+    got, mid_rows = lax.optimization_barrier((got, mid_rows))
+    ffn_own = add_blocks(got, n_tp)
+    ffn_own = jnp.concatenate([ffn_own[:, :width], ffn_own[:, width:]], axis=0)
     return (mid_rows + ffn_own).astype(BF)
 
 

time: 157 us -> 157 us (level)
  no operation moved by 1% of the time
where the time goes in v5:
time: 157 us; the launch traced here: 155 us
  waiting for transfers between devices  75.4 us (48%)
  starting transfers between devices  62.9 us (40%)
  Pallas kernels  12.4 us (8%)
  local copies, waits for them, and re-layouts  1.64 us (1%)
    all_to_all x7, waiting for transfers between devices, exchange(): lax.all_to_all(array, axis, split_axis=0, concat_axis=0, axis_index_group...  62 us
    all_to_all x7, starting transfers between devices, exchange(): lax.all_to_all(array, axis, split_axis=0, concat_axis=0, axis_index_group...  46.5 us
    ppermute x1, waiting for transfers between devices, local(): theirs = lax.ppermute(sums.astype(BF), 'dp', across_y)  8.05 us
    ppermute x1, starting transfers between devices, local(): theirs = lax.ppermute(sums.astype(BF), 'dp', across_y)  4.3 us
    pallas_call x1, Pallas kernels, local(): pl.pallas_call(attend_kernel, out_shape=jax.ShapeDtypeStruct((2 * n_tp, q...  4.21 us
  transfers between devices with their start and end apart: 14, of which 12 were waited for; matrix products, arithmetic and copies ran while one was open for 1% of the time, Pallas kernels for 1%

profile of v5, /device:TPU:6, one launch (start us, length us, event | category | flops | bytes accessed | tf_op | source)
XLA Modules:
  0.0 154.7 jit_solution(12300741640279715590)
XLA Ops:
  0.7 4.2 %shard_map.118 = bf16[64,4,512]{2,1,0:T(4,128)(2,1)} custom-call(s32[1]{0:T(128)S(6)} %copy.18.length_ref, bf16[576,128]{1,0:T(8,128)(2,1)} %bitcast.40, bf16[1,576]{1,0:T(2,128)(2,1)} %new_hbm.1, bf16[576,1792]{1,0:T(8,128)(2,1)} %bitcast.38), custom_call_target="tpu_custom_call" | custom-call | tf_op jit(solution)/shard_map/pallas_call | solution.py:242
  4.9 16.7 %all-to-all-start = ((bf16[64,4,512]{2,1,0:T(4,128)(2,1)}), bf16[64,4,512]{2,1,0:T(4,128)(2,1)S(1)}, u32[]{:S(2)}, u32[]{:S(2)}) async-start(bf16[64,4,512]{2,1,0:T(4,128)(2,1)} %shard_map.118), calls=%async_computation | async-start | bytes 524288 | tf_op jit(solution)/shard_map/all_to_all | solution.py:190
  21.6 1.9 %collective-permute-start = (bf16[512,448]{0,1:T(8,128)(2,1)}, bf16[512,448]{0,1:T(8,128)(2,1)S(1)}, u32[]{:S(2)}, u32[]{:S(2)}) collective-permute-start(bf16[512,448]{0,1:T(8,128)(2,1)} %param.18), channel_id=1, source_target_pairs={{0,32},{32,0},{64,96},{96,64},{128,160},{160,128},{192,224},{224,1... | collective-permute-start | bytes 1376264 | tf_op jit(solution)/shard_map/ppermute | solution.py:238
  24.7 12.0 %all-to-all-done.owned_ref = bf16[64,4,512]{2,1,0:T(4,128)(2,1)S(1)} async-done(((bf16[64,4,512]{2,1,0:T(4,128)(2,1)}), bf16[64,4,512]{2,1,0:T(4,128)(2,1)S(1)}, u32[]{:S(2)}, u32[]{:S(2)}) %all-to-all-start) | async-done | bytes 262176 | tf_op jit(solution)/shard_map/all_to_all | solution.py:190
  36.7 1.1 shard_map.119
  37.8 4.8 %all-to-all-start.1 = ((bf16[4,64,512]{2,1,0:T(8,128)(2,1)}), bf16[4,64,512]{2,1,0:T(8,128)(2,1)S(1)}, u32[]{:S(2)}, u32[]{:S(2)}) async-start(bf16[4,64,512]{2,1,0:T(8,128)(2,1)} %shard_map.119), calls=%async_computation.1 | async-start | bytes 524288 | tf_op jit(solution)/shard_map/all_to_all | solution.py:190
  42.6 1.9 %collective-permute-start.1 = (bf16[16,448]{1,0:T(8,128)(2,1)S(1)}, bf16[16,448]{1,0:T(8,128)(2,1)S(1)}, u32[]{:S(2)}, u32[]{:S(2)}) collective-permute-start(bf16[16,448]{1,0:T(8,128)(2,1)S(1)} %copy-done.4), channel_id=1, source_target_pairs={{0,32},{32,0},{64,96},{96,64},{128,160},{160,128},{192,224},{224,1... | collective-permute-start | bytes 43016 | tf_op jit(solution)/shard_map/ppermute | solution.py:240
  44.5 1.1 collective-permute-done.1
  45.7 1.5 all-to-all-done.1
  47.2 1.3 shard_map.120
  48.5 3.9 %all-to-all-start.2 = ((bf16[32,8,896]{2,1,0:T(8,128)(2,1)}), bf16[32,8,896]{2,1,0:T(8,128)(2,1)S(1)}, u32[]{:S(2)}, u32[]{:S(2)}) async-start(bf16[32,8,896]{2,1,0:T(8,128)(2,1)} %bitcast.9), calls=%async_computation.2 | async-start | bytes 917504 | tf_op jit(solution)/shard_map/all_to_all | solution.py:190
  52.4 1.9 %collective-permute-start.2 = (bf16[448,576]{1,0:T(8,128)(2,1)S(1)}, bf16[448,576]{1,0:T(8,128)(2,1)S(1)}, u32[]{:S(2)}, u32[]{:S(2)}) collective-permute-start(bf16[448,576]{1,0:T(8,128)(2,1)S(1)} %copy-done), channel_id=1, source_target_pairs={{0,32},{32,0},{64,96},{96,64},{128,160},{160,128},{192,224},{224,1... | collective-permute-start | bytes 1548296 | tf_op jit(solution)/shard_map/ppermute | solution.py:291
  54.4 2.4 %collective-permute-start.3 = (bf16[448,576]{1,0:T(8,128)(2,1)S(1)}, bf16[448,576]{1,0:T(8,128)(2,1)S(1)}, u32[]{:S(2)}, u32[]{:S(2)}) collective-permute-start(bf16[448,576]{1,0:T(8,128)(2,1)S(1)} %copy-done.1), channel_id=1, source_target_pairs={{0,32},{32,0},{64,96},{96,64},{128,160},{160,128},{192,224},{224,1... | collective-permute-start | bytes 1548296 | tf_op jit(solution)/shard_map/ppermute | solution.py:292
  56.8 1.6 %collective-permute-done.3.u2_ref = bf16[448,576]{1,0:T(8,128)(2,1)S(1)} collective-permute-done((bf16[448,576]{1,0:T(8,128)(2,1)S(1)}, bf16[448,576]{1,0:T(8,128)(2,1)S(1)}, u32[]{:S(2)}, u32[]{:S(2)}) %collective-permute-start.3) | collective-permute-done | bytes 516128 | tf_op jit(solution)/shard_map/ppermute | solution.py:292
  58.4 9.2 %all-to-all-done.2 = bf16[32,8,896]{2,1,0:T(8,128)(2,1)S(1)} async-done(((bf16[32,8,896]{2,1,0:T(8,128)(2,1)}), bf16[32,8,896]{2,1,0:T(8,128)(2,1)S(1)}, u32[]{:S(2)}, u32[]{:S(2)}) %all-to-all-start.2) | async-done | bytes 458784 | tf_op jit(solution)/shard_map/all_to_all | solution.py:190
  68.4 4.7 %all-to-all-start.3 = ((bf16[32,8,896]{2,1,0:T(8,128)(2,1)}), bf16[32,8,896]{2,1,0:T(8,128)(2,1)S(1)}, u32[]{:S(2)}, u32[]{:S(2)}) async-start(bf16[32,8,896]{2,1,0:T(8,128)(2,1)} %shard_map.121), calls=%async_computation.3 | async-start | bytes 917504 | tf_op jit(solution)/shard_map/all_to_all | solution.py:190
  73.2 1.9 %collective-permute-start.4 = (bf16[448]{0:T(512)(128)(2,1)S(1)}, bf16[448]{0:T(512)(128)(2,1)S(1)}, u32[]{:S(2)}, u32[]{:S(2)}) collective-permute-start(bf16[448]{0:T(512)(128)(2,1)S(1)} %copy-done.6), channel_id=1, source_target_pairs={{0,32},{32,0},{64,96},{96,64},{128,160},{160,128},{192,224},{224,1... | collective-permute-start | bytes 2696 | tf_op jit(solution)/shard_map/ppermute | solution.py:239
  75.1 1.1 collective-permute-done.4
  76.3 12.6 %all-to-all-done.3 = bf16[32,8,896]{2,1,0:T(8,128)(2,1)S(1)} async-done(((bf16[32,8,896]{2,1,0:T(8,128)(2,1)}), bf16[32,8,896]{2,1,0:T(8,128)(2,1)S(1)}, u32[]{:S(2)}, u32[]{:S(2)}) %all-to-all-start.3) | async-done | bytes 458784 | tf_op jit(solution)/shard_map/all_to_all | solution.py:190
  89.0 1.9 %shard_map.122 = bf16[4,592,128]{2,1,0:T(8,128)(2,1)} custom-call(bf16[256,896]{1,0:T(8,128)(2,1)S(1)} %bitcast.32, bf16[1,896]{1,0:T(2,128)(2,1)S(1)} %broadcast_in_dim.2.gain_ref, bf16[448,576]{1,0:T(8,128)(2,1)S(1)} %copy-done, bf16[448,576]{1,0:T(8,128)(2,1)S(1)} %collective-permute-done.2.g2_ref, bf16[448,576]{1,0:T(8,128)(2,1)S(1)} %copy-done.1, ...), custom_call_target="tpu_custom_call" | custom-call | flops 528482304 | bytes 2097152 | tf_op jit(solution)/shard_map/pallas_call | solution.py:301
  90.9 4.8 %all-to-all-start.4 = ((bf16[4,592,128]{2,1,0:T(8,128)(2,1)}), bf16[4,592,128]{2,1,0:T(8,128)(2,1)S(1)}, u32[]{:S(2)}, u32[]{:S(2)}) async-start(bf16[4,592,128]{2,1,0:T(8,128)(2,1)} %shard_map.122), calls=%async_computation.4 | async-start | bytes 1212416 | tf_op jit(solution)/shard_map/all_to_all | solution.py:190
  95.7 2.0 %collective-permute-start.5 = (bf16[256,448]{1,0:T(8,128)(2,1)S(1)}, bf16[256,448]{1,0:T(8,128)(2,1)S(1)}, u32[]{:S(2)}, u32[]{:S(2)}) collective-permute-start(bf16[256,448]{1,0:T(8,128)(2,1)S(1)} %slice.16), channel_id=1, source_target_pairs={{0,32},{32,0},{64,96},{96,64},{128,160},{160,128},{192,224},{224,1... | collective-permute-start | bytes 688136 | tf_op jit(solution)/shard_map/ppermute | solution.py:309
  97.7 1.5 collective-permute-done.5
  99.2 2.9 %all-to-all-done.4 = bf16[4,592,128]{2,1,0:T(8,128)(2,1)S(1)} async-done(((bf16[4,592,128]{2,1,0:T(8,128)(2,1)}), bf16[4,592,128]{2,1,0:T(8,128)(2,1)S(1)}, u32[]{:S(2)}, u32[]{:S(2)}) %all-to-all-start.4) | async-done | bytes 606240 | tf_op jit(solution)/shard_map/all_to_all | solution.py:190
  102.2 4.3 %collective-permute-start.6 = (bf16[592,128]{1,0:T(8,128)(2,1)S(1)}, bf16[592,128]{1,0:T(8,128)(2,1)S(1)}, u32[]{:S(2)}, u32[]{:S(2)}) collective-permute-start(bf16[592,128]{1,0:T(8,128)(2,1)S(1)} %convert_element_type.25), channel_id=1, source_target_pairs={{0,256},{32,288},{64,320},{96,352},{128,384},{160,416},{192,448},{... | collective-permute-start | bytes 454664 | tf_op jit(solution)/shard_map/ppermute | solution.py:312
  106.6 8.0 %collective-permute-done.6.theirs_ref = bf16[592,128]{1,0:T(8,128)(2,1)S(1)} collective-permute-done((bf16[592,128]{1,0:T(8,128)(2,1)S(1)}, bf16[592,128]{1,0:T(8,128)(2,1)S(1)}, u32[]{:S(2)}, u32[]{:S(2)}) %collective-permute-start.6) | collective-permute-done | bytes 151584 | tf_op jit(solution)/shard_map/ppermute | solution.py:312
  114.6 1.2 shard_map.123
  115.8 6.0 %all-to-all-start.5 = ((bf16[8,288,128]{2,1,0:T(8,128)(2,1)}), bf16[8,288,128]{2,1,0:T(8,128)(2,1)S(1)}, u32[]{:S(2)}, u32[]{:S(2)}) async-start(bf16[8,288,128]{2,1,0:T(8,128)(2,1)} %shard_map.123), calls=%async_computation.5 | async-start | bytes 1179648 | tf_op jit(solution)/shard_map/all_to_all | solution.py:190
  122.2 8.6 %all-to-all-done.5.hidden_ref = bf16[8,288,128]{2,1,0:T(8,128)(2,1)S(1)} async-done(((bf16[8,288,128]{2,1,0:T(8,128)(2,1)}), bf16[8,288,128]{2,1,0:T(8,128)(2,1)S(1)}, u32[]{:S(2)}, u32[]{:S(2)}) %all-to-all-start.5) | async-done | bytes 589856 | tf_op jit(solution)/shard_map/all_to_all | solution.py:190
  130.7 1.8 %shard_map.124 = bf16[256,896]{1,0:T(8,128)(2,1)} custom-call(bf16[512,512]{1,0:T(8,128)(2,1)S(1)} %compare_convert_fusion.pick_ref, bf16[8,288,128]{2,1,0:T(8,128)(2,1)S(1)} %all-to-all-done.5.hidden_ref, bf16[448,576]{1,0:T(8,128)(2,1)S(1)} %bitcast.35), custom_call_target="tpu_custom_call" | custom-call | flops 566231040 | bytes 2097152 | tf_op jit(solution)/shard_map/pallas_call | solution.py:330
  132.5 5.6 %all-to-all-start.6 = ((bf16[32,8,896]{2,1,0:T(8,128)(2,1)}), bf16[32,8,896]{2,1,0:T(8,128)(2,1)S(1)}, u32[]{:S(2)}, u32[]{:S(2)}) async-start(bf16[32,8,896]{2,1,0:T(8,128)(2,1)} %bitcast.17), calls=%async_computation.6 | async-start | bytes 917504 | tf_op jit(solution)/shard_map/all_to_all | solution.py:190
  138.6 15.3 %all-to-all-done.6 = bf16[32,8,896]{2,1,0:T(8,128)(2,1)S(1)} async-done(((bf16[32,8,896]{2,1,0:T(8,128)(2,1)}), bf16[32,8,896]{2,1,0:T(8,128)(2,1)S(1)}, u32[]{:S(2)}, u32[]{:S(2)}) %all-to-all-start.6) | async-done | bytes 458784 | tf_op jit(solution)/shard_map/all_to_all | solution.py:190
  (37 shorter events, 4.0 us)
Async XLA Ops:
  4.9 37.7 %copy-start.4 = (bf16[16,448]{1,0:T(8,128)(2,1)S(1)}, bf16[16,448]{1,0:T(8,128)(2,1)}, u32[]{:S(2)}) copy-start(bf16[16,448]{1,0:T(8,128)(2,1)} %param.19) | copy-start | bytes 43012
  4.9 42.3 %copy-start.3 = (bf16[512,448]{0,1:T(8,128)(2,1)S(1)}, bf16[512,448]{0,1:T(8,128)(2,1)}, u32[]{:S(2)}) copy-start(bf16[512,448]{0,1:T(8,128)(2,1)} %param.18) | copy-start | bytes 1376260
  4.9 31.8 %all-to-all-start = ((bf16[64,4,512]{2,1,0:T(4,128)(2,1)}), bf16[64,4,512]{2,1,0:T(4,128)(2,1)S(1)}, u32[]{:S(2)}, u32[]{:S(2)}) async-start(bf16[64,4,512]{2,1,0:T(4,128)(2,1)} %shard_map.118), calls=%async_computation | async-start | bytes 524288 | tf_op jit(solution)/shard_map/all_to_all | solution.py:190
  21.6 24.1 %collective-permute-start = (bf16[512,448]{0,1:T(8,128)(2,1)}, bf16[512,448]{0,1:T(8,128)(2,1)S(1)}, u32[]{:S(2)}, u32[]{:S(2)}) collective-permute-start(bf16[512,448]{0,1:T(8,128)(2,1)} %param.18), channel_id=1, source_target_pairs={{0,32},{32,0},{64,96},{96,64},{128,160},{160,128},{192,224},{224,1... | collective-permute-start | bytes 1376264 | tf_op jit(solution)/shard_map/ppermute | solution.py:238
  24.7 27.8 %copy-start = (bf16[448,576]{1,0:T(8,128)(2,1)S(1)}, bf16[448,576]{1,0:T(8,128)(2,1)}, u32[]{:S(2)}) copy-start(bf16[448,576]{1,0:T(8,128)(2,1)} %g1_ref) | copy-start | bytes 1548292
  24.7 29.7 %copy-start.1 = (bf16[448,576]{1,0:T(8,128)(2,1)S(1)}, bf16[448,576]{1,0:T(8,128)(2,1)}, u32[]{:S(2)}) copy-start(bf16[448,576]{1,0:T(8,128)(2,1)} %u1_ref) | copy-start | bytes 1548292
  37.8 9.4 %all-to-all-start.1 = ((bf16[4,64,512]{2,1,0:T(8,128)(2,1)}), bf16[4,64,512]{2,1,0:T(8,128)(2,1)S(1)}, u32[]{:S(2)}, u32[]{:S(2)}) async-start(bf16[4,64,512]{2,1,0:T(8,128)(2,1)} %shard_map.119), calls=%async_computation.1 | async-start | bytes 524288 | tf_op jit(solution)/shard_map/all_to_all | solution.py:190
  42.6 3.1 %collective-permute-start.1 = (bf16[16,448]{1,0:T(8,128)(2,1)S(1)}, bf16[16,448]{1,0:T(8,128)(2,1)S(1)}, u32[]{:S(2)}, u32[]{:S(2)}) collective-permute-start(bf16[16,448]{1,0:T(8,128)(2,1)S(1)} %copy-done.4), channel_id=1, source_target_pairs={{0,32},{32,0},{64,96},{96,64},{128,160},{160,128},{192,224},{224,1... | collective-permute-start | bytes 43016 | tf_op jit(solution)/shard_map/ppermute | solution.py:240
  47.2 26.0 %copy-start.6 = (bf16[448]{0:T(512)(128)(2,1)S(1)}, bf16[448]{0:T(512)(128)(2,1)}, u32[]{:S(2)}) copy-start(bf16[448]{0:T(512)(128)(2,1)} %param.20) | copy-start | bytes 2692
  48.5 19.0 %all-to-all-start.2 = ((bf16[32,8,896]{2,1,0:T(8,128)(2,1)}), bf16[32,8,896]{2,1,0:T(8,128)(2,1)S(1)}, u32[]{:S(2)}, u32[]{:S(2)}) async-start(bf16[32,8,896]{2,1,0:T(8,128)(2,1)} %bitcast.9), calls=%async_computation.2 | async-start | bytes 917504 | tf_op jit(solution)/shard_map/all_to_all | solution.py:190
  52.4 4.4 %collective-permute-start.2 = (bf16[448,576]{1,0:T(8,128)(2,1)S(1)}, bf16[448,576]{1,0:T(8,128)(2,1)S(1)}, u32[]{:S(2)}, u32[]{:S(2)}) collective-permute-start(bf16[448,576]{1,0:T(8,128)(2,1)S(1)} %copy-done), channel_id=1, source_target_pairs={{0,32},{32,0},{64,96},{96,64},{128,160},{160,128},{192,224},{224,1... | collective-permute-start | bytes 1548296 | tf_op jit(solution)/shard_map/ppermute | solution.py:291
  54.4 4.0 %collective-permute-start.3 = (bf16[448,576]{1,0:T(8,128)(2,1)S(1)}, bf16[448,576]{1,0:T(8,128)(2,1)S(1)}, u32[]{:S(2)}, u32[]{:S(2)}) collective-permute-start(bf16[448,576]{1,0:T(8,128)(2,1)S(1)} %copy-done.1), channel_id=1, source_target_pairs={{0,32},{32,0},{64,96},{96,64},{128,160},{160,128},{192,224},{224,1... | collective-permute-start | bytes 1548296 | tf_op jit(solution)/shard_map/ppermute | solution.py:292
  68.4 20.5 %all-to-all-start.3 = ((bf16[32,8,896]{2,1,0:T(8,128)(2,1)}), bf16[32,8,896]{2,1,0:T(8,128)(2,1)S(1)}, u32[]{:S(2)}, u32[]{:S(2)}) async-start(bf16[32,8,896]{2,1,0:T(8,128)(2,1)} %shard_map.121), calls=%async_computation.3 | async-start | bytes 917504 | tf_op jit(solution)/shard_map/all_to_all | solution.py:190
  73.2 3.0 %collective-permute-start.4 = (bf16[448]{0:T(512)(128)(2,1)S(1)}, bf16[448]{0:T(512)(128)(2,1)S(1)}, u32[]{:S(2)}, u32[]{:S(2)}) collective-permute-start(bf16[448]{0:T(512)(128)(2,1)S(1)} %copy-done.6), channel_id=1, source_target_pairs={{0,32},{32,0},{64,96},{96,64},{128,160},{160,128},{192,224},{224,1... | collective-permute-start | bytes 2696 | tf_op jit(solution)/shard_map/ppermute | solution.py:239
  90.9 11.2 %all-to-all-start.4 = ((bf16[4,592,128]{2,1,0:T(8,128)(2,1)}), bf16[4,592,128]{2,1,0:T(8,128)(2,1)S(1)}, u32[]{:S(2)}, u32[]{:S(2)}) async-start(bf16[4,592,128]{2,1,0:T(8,128)(2,1)} %shard_map.122), calls=%async_computation.4 | async-start | bytes 1212416 | tf_op jit(solution)/shard_map/all_to_all | solution.py:190
  95.7 26.1 %copy-start.5 = (s32[512]{0:T(512)S(1)}, s32[512]{0:T(512)}, u32[]{:S(2)}) copy-start(s32[512]{0:T(512)} %param.16) | copy-start | bytes 6148
  95.7 3.5 %collective-permute-start.5 = (bf16[256,448]{1,0:T(8,128)(2,1)S(1)}, bf16[256,448]{1,0:T(8,128)(2,1)S(1)}, u32[]{:S(2)}, u32[]{:S(2)}) collective-permute-start(bf16[256,448]{1,0:T(8,128)(2,1)S(1)} %slice.16), channel_id=1, source_target_pairs={{0,32},{32,0},{64,96},{96,64},{128,160},{160,128},{192,224},{224,1... | collective-permute-start | bytes 688136 | tf_op jit(solution)/shard_map/ppermute | solution.py:309
  102.1 28.6 %copy-start.2 = (bf16[576,448]{0,1:T(8,128)(2,1)S(1)}, bf16[576,448]{0,1:T(8,128)(2,1)}, u32[]{:S(2)}) copy-start(bf16[576,448]{0,1:T(8,128)(2,1)} %param.23) | copy-start | bytes 1548292
  102.2 12.4 %collective-permute-start.6 = (bf16[592,128]{1,0:T(8,128)(2,1)S(1)}, bf16[592,128]{1,0:T(8,128)(2,1)S(1)}, u32[]{:S(2)}, u32[]{:S(2)}) collective-permute-start(bf16[592,128]{1,0:T(8,128)(2,1)S(1)} %convert_element_type.25), channel_id=1, source_target_pairs={{0,256},{32,288},{64,320},{96,352},{128,384},{160,416},{192,448},{... | collective-permute-start | bytes 454664 | tf_op jit(solution)/shard_map/ppermute | solution.py:312
  115.8 14.9 %all-to-all-start.5 = ((bf16[8,288,128]{2,1,0:T(8,128)(2,1)}), bf16[8,288,128]{2,1,0:T(8,128)(2,1)S(1)}, u32[]{:S(2)}, u32[]{:S(2)}) async-start(bf16[8,288,128]{2,1,0:T(8,128)(2,1)} %shard_map.123), calls=%async_computation.5 | async-start | bytes 1179648 | tf_op jit(solution)/shard_map/all_to_all | solution.py:190
  132.5 21.4 %all-to-all-start.6 = ((bf16[32,8,896]{2,1,0:T(8,128)(2,1)}), bf16[32,8,896]{2,1,0:T(8,128)(2,1)S(1)}, u32[]{:S(2)}, u32[]{:S(2)}) async-start(bf16[32,8,896]{2,1,0:T(8,128)(2,1)} %bitcast.17), calls=%async_computation.6 | async-start | bytes 917504 | tf_op jit(solution)/shard_map/all_to_all | solution.py:190

commit v6 on v5

--- a/solution.py
+++ b/solution.py
@@ -116,8 +116,8 @@
         out_ref[k] = total
 
 
-def hidden_kernel(mine_ref, theirs_ref, out_ref):
-    sums = mine_ref[...] + theirs_ref[...].astype(F32)
+def hidden_kernel(sums_ref, out_ref):
+    sums = sums_ref[0].astype(F32) + sums_ref[1].astype(F32)
     tiles = sums.shape[0] // 64
     rows = 64
     extra = sums[tiles * rows :]
@@ -234,7 +234,7 @@
     xs, two = range(n_x), range(2)
     along_x = [[at(y, x, c) for x in xs] for y in two for c in two]
     same_y = [[at(y, x, c) for x in xs for c in two] for y in two]
-    across_y = [(i, (i + n_dp // 2) % n_dp) for i in range(n_dp)]
+    along_y = [[at(y, x, c) for y in two] for x in xs for c in two]
     out_proj2 = lax.ppermute(out_proj, "dp", swap)
     norm_gain2 = lax.ppermute(norm_gain, "dp", swap)
     residual2 = lax.ppermute(residual, "dp", swap)
@@ -308,24 +308,31 @@
     got = exchange(terms, "dp", along_x).reshape(-1, LANES)
     mid_rest = lax.ppermute(mid_there, "dp", swap)
     got, mid_rest = lax.optimization_barrier((got, mid_rest))
-    sums = add_blocks(got, n_x)
-    theirs = lax.ppermute(sums.astype(BF), "dp", across_y)
+    sums = add_blocks(got, n_x).astype(BF)
+    sums = jnp.broadcast_to(sums, (2,) + sums.shape)
+    sums, order = lax.optimization_barrier((sums, order))
+    sums = exchange(sums, "dp", along_y)
+    rows = n_dp * n_tp
+    own_count = rows // n_tp
+    spots = jnp.arange(rows)
+    spot_dp = at(spots // n_tp % 2, spots // (4 * n_tp), spots // (2 * n_tp) % 2)
+    spot_rows = spot_dp * n_tp + spots % n_tp
+    listed = order.reshape(n_tp, 2, own_count // 2).swapaxes(0, 1).reshape(rows)
+    pick = (listed[:, None] == spot_rows[None, :]).astype(BF)
+    sums, pick = lax.optimization_barrier((sums, pick))
     copies = call(
         hidden_kernel,
         jax.ShapeDtypeStruct((n_x * 2, 2 * n_tp * ff // LANES, LANES), BF),
-        [VMEM] * 2,
+        [VMEM],
         8 * sums.size,
-    )(sums, theirs)
-    copies, order = lax.optimization_barrier((copies, order))
+    )(sums)
+    wanted = lax.dynamic_slice_in_dim(order, tp * own_count, own_count)
+    pick1 = (wanted[:, None] == (set_rows + core * n_tp)[None, :]).astype(BF)
+    pick2 = (wanted[:, None] == (set_rows + (1 - core) * n_tp)[None, :]).astype(BF)
+    copies, mid_here = lax.optimization_barrier((copies, mid_here))
     hidden = exchange(copies, "dp", same_y)
-    rows = n_dp * n_tp
-    spots = jnp.arange(rows)
-    spot_dp = at(spots // n_tp % 2, spots // (4 * n_tp), spots // (2 * n_tp) % 2)
-    spot_rows = spot_dp * n_tp + spots % n_tp
-    own_count = rows // n_tp
-    listed = order.reshape(n_tp, 2, own_count // 2).swapaxes(0, 1).reshape(rows)
-    pick = (listed[:, None] == spot_rows[None, :]).astype(BF)
-    hidden, pick = lax.optimization_barrier((hidden, pick))
+    mid_rows = jnp.dot(pick1, mid_here, preferred_element_type=F32)
+    hidden, mid_rows = lax.optimization_barrier((hidden, mid_rows))
     width = down_weight.shape[1]
     ffn_terms = call(
         down_kernel,
@@ -333,12 +340,8 @@
         [VMEM] * 3,
         2 * rows * ff * (rows + width),
     )(pick, hidden, down_weight.T)
-    wanted = lax.dynamic_slice_in_dim(order, tp * own_count, own_count)
-    pick1 = (wanted[:, None] == (set_rows + core * n_tp)[None, :]).astype(BF)
-    pick2 = (wanted[:, None] == (set_rows + (1 - core) * n_tp)[None, :]).astype(BF)
-    mid_rows = jnp.dot(pick1, mid_here, preferred_element_type=F32) + jnp.dot(
-        pick2, mid_rest, preferred_element_type=F32
-    )
+    ffn_terms, mid_rest = lax.optimization_barrier((ffn_terms, mid_rest))
+    mid_rows = mid_rows + jnp.dot(pick2, mid_rest, preferred_element_type=F32)
     got = exchange(ffn_terms, "tp", None)
     got, mid_rows = lax.optimization_barrier((got, mid_rows))
     ffn_own = add_blocks(got, n_tp)

time: 157 us -> 159 us (1.013)
  waiting for transfers between devices: 75.4 us -> 78.2 us
    all_to_all x7 -> x8, waiting for transfers between devices: 62 us -> 72.9 us  [exchange(): lax.all_to_all(array, axis, split_axis=0, concat_axis=0, axis_index_group...]
    ppermute x1 -> x0, waiting for transfers between devices: 8.05 us -> none  [local(): theirs = lax.ppermute(sums.astype(BF), 'dp', across_y)]
    ppermute x1 -> x0, starting transfers between devices: 4.3 us -> none  [local(): theirs = lax.ppermute(sums.astype(BF), 'dp', across_y)]
    all_to_all x7 -> x8, starting transfers between devices: 46.5 us -> 49.5 us  [exchange(): lax.all_to_all(array, axis, split_axis=0, concat_axis=0, axis_index_group...]
where the time goes in v6:
time: 159 us; the launch traced here: 157 us
  waiting for transfers between devices  78.2 us (49%)
  starting transfers between devices  61.5 us (39%)
  Pallas kernels  12.4 us (8%)
  local copies, waits for them, and re-layouts  2.36 us (1%)
    all_to_all x8, waiting for transfers between devices, exchange(): lax.all_to_all(array, axis, split_axis=0, concat_axis=0, axis_index_group...  72.9 us
    all_to_all x8, starting transfers between devices, exchange(): lax.all_to_all(array, axis, split_axis=0, concat_axis=0, axis_index_group...  49.5 us
    pallas_call x1, Pallas kernels, local(): pl.pallas_call(attend_kernel, out_shape=jax.ShapeDtypeStruct((2 * n_tp, q...  4.21 us
  transfers between devices with their start and end apart: 14, of which 12 were waited for; matrix products, arithmetic and copies ran while one was open for 1% of the time, Pallas kernels for 1%

profile of v6, /device:TPU:6, one launch (start us, length us, event | category | flops | bytes accessed | tf_op | source)
XLA Modules:
  0.0 156.9 jit_solution(10248454926794295960)
XLA Ops:
  0.7 4.2 %shard_map.118 = bf16[64,4,512]{2,1,0:T(4,128)(2,1)} custom-call(s32[1]{0:T(128)S(6)} %copy.18.length_ref, bf16[576,128]{1,0:T(8,128)(2,1)} %bitcast.39, bf16[1,576]{1,0:T(2,128)(2,1)} %new_hbm.1, bf16[576,1792]{1,0:T(8,128)(2,1)} %bitcast.37), custom_call_target="tpu_custom_call" | custom-call | tf_op jit(solution)/shard_map/pallas_call | solution.py:242
  4.9 16.7 %all-to-all-start = ((bf16[64,4,512]{2,1,0:T(4,128)(2,1)}), bf16[64,4,512]{2,1,0:T(4,128)(2,1)S(1)}, u32[]{:S(2)}, u32[]{:S(2)}) async-start(bf16[64,4,512]{2,1,0:T(4,128)(2,1)} %shard_map.118), calls=%async_computation | async-start | bytes 524288 | tf_op jit(solution)/shard_map/all_to_all | solution.py:190
  21.6 1.9 %collective-permute-start = (bf16[512,448]{0,1:T(8,128)(2,1)}, bf16[512,448]{0,1:T(8,128)(2,1)S(1)}, u32[]{:S(2)}, u32[]{:S(2)}) collective-permute-start(bf16[512,448]{0,1:T(8,128)(2,1)} %param.18), channel_id=1, source_target_pairs={{0,32},{32,0},{64,96},{96,64},{128,160},{160,128},{192,224},{224,1... | collective-permute-start | bytes 1376264 | tf_op jit(solution)/shard_map/ppermute | solution.py:238
  24.7 12.0 %all-to-all-done.owned_ref = bf16[64,4,512]{2,1,0:T(4,128)(2,1)S(1)} async-done(((bf16[64,4,512]{2,1,0:T(4,128)(2,1)}), bf16[64,4,512]{2,1,0:T(4,128)(2,1)S(1)}, u32[]{:S(2)}, u32[]{:S(2)}) %all-to-all-start) | async-done | bytes 262176 | tf_op jit(solution)/shard_map/all_to_all | solution.py:190
  36.7 1.1 shard_map.119
  37.8 4.8 %all-to-all-start.1 = ((bf16[4,64,512]{2,1,0:T(8,128)(2,1)}), bf16[4,64,512]{2,1,0:T(8,128)(2,1)S(1)}, u32[]{:S(2)}, u32[]{:S(2)}) async-start(bf16[4,64,512]{2,1,0:T(8,128)(2,1)} %shard_map.119), calls=%async_computation.1 | async-start | bytes 524288 | tf_op jit(solution)/shard_map/all_to_all | solution.py:190
  42.6 1.9 %collective-permute-start.1 = (bf16[16,448]{1,0:T(8,128)(2,1)S(1)}, bf16[16,448]{1,0:T(8,128)(2,1)S(1)}, u32[]{:S(2)}, u32[]{:S(2)}) collective-permute-start(bf16[16,448]{1,0:T(8,128)(2,1)S(1)} %copy-done.4), channel_id=1, source_target_pairs={{0,32},{32,0},{64,96},{96,64},{128,160},{160,128},{192,224},{224,1... | collective-permute-start | bytes 43016 | tf_op jit(solution)/shard_map/ppermute | solution.py:240
  44.6 1.1 collective-permute-done.1
  45.7 1.5 all-to-all-done.1
  47.2 1.3 shard_map.120
  48.5 3.9 %all-to-all-start.2 = ((bf16[32,8,896]{2,1,0:T(8,128)(2,1)}), bf16[32,8,896]{2,1,0:T(8,128)(2,1)S(1)}, u32[]{:S(2)}, u32[]{:S(2)}) async-start(bf16[32,8,896]{2,1,0:T(8,128)(2,1)} %bitcast.9), calls=%async_computation.2 | async-start | bytes 917504 | tf_op jit(solution)/shard_map/all_to_all | solution.py:190
  52.4 1.9 %collective-permute-start.2 = (bf16[448,576]{1,0:T(8,128)(2,1)S(1)}, bf16[448,576]{1,0:T(8,128)(2,1)S(1)}, u32[]{:S(2)}, u32[]{:S(2)}) collective-permute-start(bf16[448,576]{1,0:T(8,128)(2,1)S(1)} %copy-done), channel_id=1, source_target_pairs={{0,32},{32,0},{64,96},{96,64},{128,160},{160,128},{192,224},{224,1... | collective-permute-start | bytes 1548296 | tf_op jit(solution)/shard_map/ppermute | solution.py:291
  54.4 2.4 %collective-permute-start.3 = (bf16[448,576]{1,0:T(8,128)(2,1)S(1)}, bf16[448,576]{1,0:T(8,128)(2,1)S(1)}, u32[]{:S(2)}, u32[]{:S(2)}) collective-permute-start(bf16[448,576]{1,0:T(8,128)(2,1)S(1)} %copy-done.1), channel_id=1, source_target_pairs={{0,32},{32,0},{64,96},{96,64},{128,160},{160,128},{192,224},{224,1... | collective-permute-start | bytes 1548296 | tf_op jit(solution)/shard_map/ppermute | solution.py:292
  56.8 1.6 %collective-permute-done.3.u2_ref = bf16[448,576]{1,0:T(8,128)(2,1)S(1)} collective-permute-done((bf16[448,576]{1,0:T(8,128)(2,1)S(1)}, bf16[448,576]{1,0:T(8,128)(2,1)S(1)}, u32[]{:S(2)}, u32[]{:S(2)}) %collective-permute-start.3) | collective-permute-done | bytes 516128 | tf_op jit(solution)/shard_map/ppermute | solution.py:292
  58.4 9.2 %all-to-all-done.2 = bf16[32,8,896]{2,1,0:T(8,128)(2,1)S(1)} async-done(((bf16[32,8,896]{2,1,0:T(8,128)(2,1)}), bf16[32,8,896]{2,1,0:T(8,128)(2,1)S(1)}, u32[]{:S(2)}, u32[]{:S(2)}) %all-to-all-start.2) | async-done | bytes 458784 | tf_op jit(solution)/shard_map/all_to_all | solution.py:190
  68.4 4.7 %all-to-all-start.3 = ((bf16[32,8,896]{2,1,0:T(8,128)(2,1)}), bf16[32,8,896]{2,1,0:T(8,128)(2,1)S(1)}, u32[]{:S(2)}, u32[]{:S(2)}) async-start(bf16[32,8,896]{2,1,0:T(8,128)(2,1)} %shard_map.121), calls=%async_computation.3 | async-start | bytes 917504 | tf_op jit(solution)/shard_map/all_to_all | solution.py:190
  73.2 1.9 %collective-permute-start.4 = (bf16[448]{0:T(512)(128)(2,1)S(1)}, bf16[448]{0:T(512)(128)(2,1)S(1)}, u32[]{:S(2)}, u32[]{:S(2)}) collective-permute-start(bf16[448]{0:T(512)(128)(2,1)S(1)} %copy-done.6), channel_id=1, source_target_pairs={{0,32},{32,0},{64,96},{96,64},{128,160},{160,128},{192,224},{224,1... | collective-permute-start | bytes 2696 | tf_op jit(solution)/shard_map/ppermute | solution.py:239
  75.1 1.1 collective-permute-done.4
  76.3 12.6 %all-to-all-done.3 = bf16[32,8,896]{2,1,0:T(8,128)(2,1)S(1)} async-done(((bf16[32,8,896]{2,1,0:T(8,128)(2,1)}), bf16[32,8,896]{2,1,0:T(8,128)(2,1)S(1)}, u32[]{:S(2)}, u32[]{:S(2)}) %all-to-all-start.3) | async-done | bytes 458784 | tf_op jit(solution)/shard_map/all_to_all | solution.py:190
  89.0 1.9 %shard_map.122 = bf16[4,592,128]{2,1,0:T(8,128)(2,1)} custom-call(bf16[256,896]{1,0:T(8,128)(2,1)S(1)} %bitcast.32, bf16[1,896]{1,0:T(2,128)(2,1)S(1)} %broadcast_in_dim.4.gain_ref, bf16[448,576]{1,0:T(8,128)(2,1)S(1)} %copy-done, bf16[448,576]{1,0:T(8,128)(2,1)S(1)} %collective-permute-done.2.g2_ref, bf16[448,576]{1,0:T(8,128)(2,1)S(1)} %copy-done.1, ...), custom_call_target="tpu_custom_call" | custom-call | flops 528482304 | bytes 2097152 | tf_op jit(solution)/shard_map/pallas_call | solution.py:301
  90.9 4.9 %all-to-all-start.4 = ((bf16[4,592,128]{2,1,0:T(8,128)(2,1)}), bf16[4,592,128]{2,1,0:T(8,128)(2,1)S(1)}, u32[]{:S(2)}, u32[]{:S(2)}) async-start(bf16[4,592,128]{2,1,0:T(8,128)(2,1)} %shard_map.122), calls=%async_computation.4 | async-start | bytes 1212416 | tf_op jit(solution)/shard_map/all_to_all | solution.py:190
  95.9 1.9 %collective-permute-start.5 = (bf16[256,448]{1,0:T(8,128)(2,1)S(1)}, bf16[256,448]{1,0:T(8,128)(2,1)S(1)}, u32[]{:S(2)}, u32[]{:S(2)}) collective-permute-start(bf16[256,448]{1,0:T(8,128)(2,1)S(1)} %get-tuple-element.42), channel_id=1, source_target_pairs={{0,32},{32,0},{64,96},{96,64},{128,160},{160,128},{192,224},{224,1... | collective-permute-start | bytes 688136 | tf_op jit(solution)/shard_map/ppermute | solution.py:309
  97.8 1.5 collective-permute-done.5
  99.3 3.0 %all-to-all-done.4 = bf16[4,592,128]{2,1,0:T(8,128)(2,1)S(1)} async-done(((bf16[4,592,128]{2,1,0:T(8,128)(2,1)}), bf16[4,592,128]{2,1,0:T(8,128)(2,1)S(1)}, u32[]{:S(2)}, u32[]{:S(2)}) %all-to-all-start.4) | async-done | bytes 606240 | tf_op jit(solution)/shard_map/all_to_all | solution.py:190
  103.2 3.5 %all-to-all-start.5 = ((bf16[2,592,128]{2,1,0:T(8,128)(2,1)}), bf16[2,592,128]{2,1,0:T(8,128)(2,1)S(1)}, u32[]{:S(2)}, u32[]{:S(2)}) async-start(bf16[2,592,128]{2,1,0:T(8,128)(2,1)} %broadcast_in_dim.5), calls=%async_computation.5 | async-start | bytes 606208 | tf_op jit(solution)/shard_map/all_to_all | solution.py:190
  107.1 10.3 %all-to-all-done.5.sums_ref = bf16[2,592,128]{2,1,0:T(8,128)(2,1)S(1)} async-done(((bf16[2,592,128]{2,1,0:T(8,128)(2,1)}), bf16[2,592,128]{2,1,0:T(8,128)(2,1)S(1)}, u32[]{:S(2)}, u32[]{:S(2)}) %all-to-all-start.5) | async-done | bytes 303136 | tf_op jit(solution)/shard_map/all_to_all | solution.py:190
  117.4 1.2 shard_map.123
  118.6 5.5 %all-to-all-start.6 = ((bf16[8,288,128]{2,1,0:T(8,128)(2,1)}), bf16[8,288,128]{2,1,0:T(8,128)(2,1)S(1)}, u32[]{:S(2)}, u32[]{:S(2)}) async-start(bf16[8,288,128]{2,1,0:T(8,128)(2,1)} %shard_map.123), calls=%async_computation.6 | async-start | bytes 1179648 | tf_op jit(solution)/shard_map/all_to_all | solution.py:190
  124.4 8.7 %all-to-all-done.6.hidden_ref = bf16[8,288,128]{2,1,0:T(8,128)(2,1)S(1)} async-done(((bf16[8,288,128]{2,1,0:T(8,128)(2,1)}), bf16[8,288,128]{2,1,0:T(8,128)(2,1)S(1)}, u32[]{:S(2)}, u32[]{:S(2)}) %all-to-all-start.6) | async-done | bytes 589856 | tf_op jit(solution)/shard_map/all_to_all | solution.py:190
  133.1 1.8 %shard_map.124 = bf16[256,896]{1,0:T(8,128)(2,1)} custom-call(bf16[512,512]{1,0:T(8,128)(2,1)S(1)} %compare_convert_fusion.pick_ref, bf16[8,288,128]{2,1,0:T(8,128)(2,1)S(1)} %all-to-all-done.6.hidden_ref, bf16[448,576]{1,0:T(8,128)(2,1)S(1)} %bitcast.34), custom_call_target="tpu_custom_call" | custom-call | flops 566231040 | bytes 2097152 | tf_op jit(solution)/shard_map/pallas_call | solution.py:337
  134.9 5.5 %all-to-all-start.7 = ((bf16[32,8,896]{2,1,0:T(8,128)(2,1)}), bf16[32,8,896]{2,1,0:T(8,128)(2,1)S(1)}, u32[]{:S(2)}, u32[]{:S(2)}) async-start(bf16[32,8,896]{2,1,0:T(8,128)(2,1)} %bitcast.17), calls=%async_computation.7 | async-start | bytes 917504 | tf_op jit(solution)/shard_map/all_to_all | solution.py:190
  140.6 15.6 %all-to-all-done.7 = bf16[32,8,896]{2,1,0:T(8,128)(2,1)S(1)} async-done(((bf16[32,8,896]{2,1,0:T(8,128)(2,1)}), bf16[32,8,896]{2,1,0:T(8,128)(2,1)S(1)}, u32[]{:S(2)}, u32[]{:S(2)}) %all-to-all-start.7) | async-done | bytes 458784 | tf_op jit(solution)/shard_map/all_to_all | solution.py:190
  (37 shorter events, 4.7 us)
Async XLA Ops:
  4.9 37.7 %copy-start.4 = (bf16[16,448]{1,0:T(8,128)(2,1)S(1)}, bf16[16,448]{1,0:T(8,128)(2,1)}, u32[]{:S(2)}) copy-start(bf16[16,448]{1,0:T(8,128)(2,1)} %param.19) | copy-start | bytes 43012
  4.9 42.3 %copy-start.3 = (bf16[512,448]{0,1:T(8,128)(2,1)S(1)}, bf16[512,448]{0,1:T(8,128)(2,1)}, u32[]{:S(2)}) copy-start(bf16[512,448]{0,1:T(8,128)(2,1)} %param.18) | copy-start | bytes 1376260
  4.9 31.8 %all-to-all-start = ((bf16[64,4,512]{2,1,0:T(4,128)(2,1)}), bf16[64,4,512]{2,1,0:T(4,128)(2,1)S(1)}, u32[]{:S(2)}, u32[]{:S(2)}) async-start(bf16[64,4,512]{2,1,0:T(4,128)(2,1)} %shard_map.118), calls=%async_computation | async-start | bytes 524288 | tf_op jit(solution)/shard_map/all_to_all | solution.py:190
  21.6 24.1 %collective-permute-start = (bf16[512,448]{0,1:T(8,128)(2,1)}, bf16[512,448]{0,1:T(8,128)(2,1)S(1)}, u32[]{:S(2)}, u32[]{:S(2)}) collective-permute-start(bf16[512,448]{0,1:T(8,128)(2,1)} %param.18), channel_id=1, source_target_pairs={{0,32},{32,0},{64,96},{96,64},{128,160},{160,128},{192,224},{224,1... | collective-permute-start | bytes 1376264 | tf_op jit(solution)/shard_map/ppermute | solution.py:238
  24.7 27.8 %copy-start = (bf16[448,576]{1,0:T(8,128)(2,1)S(1)}, bf16[448,576]{1,0:T(8,128)(2,1)}, u32[]{:S(2)}) copy-start(bf16[448,576]{1,0:T(8,128)(2,1)} %g1_ref) | copy-start | bytes 1548292
  24.7 29.7 %copy-start.1 = (bf16[448,576]{1,0:T(8,128)(2,1)S(1)}, bf16[448,576]{1,0:T(8,128)(2,1)}, u32[]{:S(2)}) copy-start(bf16[448,576]{1,0:T(8,128)(2,1)} %u1_ref) | copy-start | bytes 1548292
  37.8 9.4 %all-to-all-start.1 = ((bf16[4,64,512]{2,1,0:T(8,128)(2,1)}), bf16[4,64,512]{2,1,0:T(8,128)(2,1)S(1)}, u32[]{:S(2)}, u32[]{:S(2)}) async-start(bf16[4,64,512]{2,1,0:T(8,128)(2,1)} %shard_map.119), calls=%async_computation.1 | async-start | bytes 524288 | tf_op jit(solution)/shard_map/all_to_all | solution.py:190
  42.6 3.1 %collective-permute-start.1 = (bf16[16,448]{1,0:T(8,128)(2,1)S(1)}, bf16[16,448]{1,0:T(8,128)(2,1)S(1)}, u32[]{:S(2)}, u32[]{:S(2)}) collective-permute-start(bf16[16,448]{1,0:T(8,128)(2,1)S(1)} %copy-done.4), channel_id=1, source_target_pairs={{0,32},{32,0},{64,96},{96,64},{128,160},{160,128},{192,224},{224,1... | collective-permute-start | bytes 43016 | tf_op jit(solution)/shard_map/ppermute | solution.py:240
  47.2 26.0 %copy-start.6 = (bf16[448]{0:T(512)(128)(2,1)S(1)}, bf16[448]{0:T(512)(128)(2,1)}, u32[]{:S(2)}) copy-start(bf16[448]{0:T(512)(128)(2,1)} %param.20) | copy-start | bytes 2692
  48.5 19.0 %all-to-all-start.2 = ((bf16[32,8,896]{2,1,0:T(8,128)(2,1)}), bf16[32,8,896]{2,1,0:T(8,128)(2,1)S(1)}, u32[]{:S(2)}, u32[]{:S(2)}) async-start(bf16[32,8,896]{2,1,0:T(8,128)(2,1)} %bitcast.9), calls=%async_computation.2 | async-start | bytes 917504 | tf_op jit(solution)/shard_map/all_to_all | solution.py:190
  52.4 4.4 %collective-permute-start.2 = (bf16[448,576]{1,0:T(8,128)(2,1)S(1)}, bf16[448,576]{1,0:T(8,128)(2,1)S(1)}, u32[]{:S(2)}, u32[]{:S(2)}) collective-permute-start(bf16[448,576]{1,0:T(8,128)(2,1)S(1)} %copy-done), channel_id=1, source_target_pairs={{0,32},{32,0},{64,96},{96,64},{128,160},{160,128},{192,224},{224,1... | collective-permute-start | bytes 1548296 | tf_op jit(solution)/shard_map/ppermute | solution.py:291
  54.4 4.0 %collective-permute-start.3 = (bf16[448,576]{1,0:T(8,128)(2,1)S(1)}, bf16[448,576]{1,0:T(8,128)(2,1)S(1)}, u32[]{:S(2)}, u32[]{:S(2)}) collective-permute-start(bf16[448,576]{1,0:T(8,128)(2,1)S(1)} %copy-done.1), channel_id=1, source_target_pairs={{0,32},{32,0},{64,96},{96,64},{128,160},{160,128},{192,224},{224,1... | collective-permute-start | bytes 1548296 | tf_op jit(solution)/shard_map/ppermute | solution.py:292
  68.4 20.5 %all-to-all-start.3 = ((bf16[32,8,896]{2,1,0:T(8,128)(2,1)}), bf16[32,8,896]{2,1,0:T(8,128)(2,1)S(1)}, u32[]{:S(2)}, u32[]{:S(2)}) async-start(bf16[32,8,896]{2,1,0:T(8,128)(2,1)} %shard_map.121), calls=%async_computation.3 | async-start | bytes 917504 | tf_op jit(solution)/shard_map/all_to_all | solution.py:190
  73.2 3.0 %collective-permute-start.4 = (bf16[448]{0:T(512)(128)(2,1)S(1)}, bf16[448]{0:T(512)(128)(2,1)S(1)}, u32[]{:S(2)}, u32[]{:S(2)}) collective-permute-start(bf16[448]{0:T(512)(128)(2,1)S(1)} %copy-done.6), channel_id=1, source_target_pairs={{0,32},{32,0},{64,96},{96,64},{128,160},{160,128},{192,224},{224,1... | collective-permute-start | bytes 2696 | tf_op jit(solution)/shard_map/ppermute | solution.py:239
  90.9 15.8 %copy-start.5 = (s32[512]{0:T(512)S(1)}, s32[512]{0:T(512)}, u32[]{:S(2)}) copy-start(s32[512]{0:T(512)} %param.16) | copy-start | bytes 6148
  90.9 11.4 %all-to-all-start.4 = ((bf16[4,592,128]{2,1,0:T(8,128)(2,1)}), bf16[4,592,128]{2,1,0:T(8,128)(2,1)S(1)}, u32[]{:S(2)}, u32[]{:S(2)}) async-start(bf16[4,592,128]{2,1,0:T(8,128)(2,1)} %shard_map.122), calls=%async_computation.4 | async-start | bytes 1212416 | tf_op jit(solution)/shard_map/all_to_all | solution.py:190
  95.9 3.4 %collective-permute-start.5 = (bf16[256,448]{1,0:T(8,128)(2,1)S(1)}, bf16[256,448]{1,0:T(8,128)(2,1)S(1)}, u32[]{:S(2)}, u32[]{:S(2)}) collective-permute-start(bf16[256,448]{1,0:T(8,128)(2,1)S(1)} %get-tuple-element.42), channel_id=1, source_target_pairs={{0,32},{32,0},{64,96},{96,64},{128,160},{160,128},{192,224},{224,1... | collective-permute-start | bytes 688136 | tf_op jit(solution)/shard_map/ppermute | solution.py:309
  102.4 30.7 %copy-start.2 = (bf16[576,448]{0,1:T(8,128)(2,1)S(1)}, bf16[576,448]{0,1:T(8,128)(2,1)}, u32[]{:S(2)}) copy-start(bf16[576,448]{0,1:T(8,128)(2,1)} %param.23) | copy-start | bytes 1548292
  103.2 14.3 %all-to-all-start.5 = ((bf16[2,592,128]{2,1,0:T(8,128)(2,1)}), bf16[2,592,128]{2,1,0:T(8,128)(2,1)S(1)}, u32[]{:S(2)}, u32[]{:S(2)}) async-start(bf16[2,592,128]{2,1,0:T(8,128)(2,1)} %broadcast_in_dim.5), calls=%async_computation.5 | async-start | bytes 606208 | tf_op jit(solution)/shard_map/all_to_all | solution.py:190
  118.6 14.5 %all-to-all-start.6 = ((bf16[8,288,128]{2,1,0:T(8,128)(2,1)}), bf16[8,288,128]{2,1,0:T(8,128)(2,1)S(1)}, u32[]{:S(2)}, u32[]{:S(2)}) async-start(bf16[8,288,128]{2,1,0:T(8,128)(2,1)} %shard_map.123), calls=%async_computation.6 | async-start | bytes 1179648 | tf_op jit(solution)/shard_map/all_to_all | solution.py:190
  134.9 21.3 %all-to-all-start.7 = ((bf16[32,8,896]{2,1,0:T(8,128)(2,1)}), bf16[32,8,896]{2,1,0:T(8,128)(2,1)S(1)}, u32[]{:S(2)}, u32[]{:S(2)}) async-start(bf16[32,8,896]{2,1,0:T(8,128)(2,1)} %bitcast.17), calls=%async_computation.7 | async-start | bytes 917504 | tf_op jit(solution)/shard_map/all_to_all | solution.py:190

commit v7 on v5

--- a/solution.py
+++ b/solution.py
@@ -237,7 +237,6 @@
     across_y = [(i, (i + n_dp // 2) % n_dp) for i in range(n_dp)]
     out_proj2 = lax.ppermute(out_proj, "dp", swap)
     norm_gain2 = lax.ppermute(norm_gain, "dp", swap)
-    residual2 = lax.ppermute(residual, "dp", swap)
     positions = latent_cache.shape[1]
     copies = pl.pallas_call(
         attend_kernel,
@@ -256,10 +255,11 @@
         [at(y, x, c) * n_tp + j for y in two for j in range(n_tp)] for x in xs for c in two
     ]
     heads, _, size = value_up.shape
-    copies, value_up = lax.optimization_barrier((copies, value_up))
+    copies, value_up, residual = lax.optimization_barrier((copies, value_up, residual))
     owned = exchange(copies, ("dp", "tp"), both_y)
     maps = value_up.transpose(1, 0, 2).reshape(LAT, heads * size)
-    owned, maps = lax.optimization_barrier((owned, maps))
+    residual2 = lax.ppermute(residual, "dp", swap)
+    owned, maps, residual2 = lax.optimization_barrier((owned, maps, residual2))
     copies = call(
         value_kernel,
         jax.ShapeDtypeStruct((n_x, owned.shape[0], heads * size), BF),
@@ -304,10 +304,7 @@
         [VMEM] * 6,
         4 * mid_set.size * ff,
     )(mid_set, gain, gate_weight, gate_weight2, up_weight, up_weight2)
-    terms, mid_there = lax.optimization_barrier((terms, mid_there))
     got = exchange(terms, "dp", along_x).reshape(-1, LANES)
-    mid_rest = lax.ppermute(mid_there, "dp", swap)
-    got, mid_rest = lax.optimization_barrier((got, mid_rest))
     sums = add_blocks(got, n_x)
     theirs = lax.ppermute(sums.astype(BF), "dp", across_y)
     copies = call(
@@ -316,7 +313,8 @@
         [VMEM] * 2,
         8 * sums.size,
     )(sums, theirs)
-    copies, order = lax.optimization_barrier((copies, order))
+    copies, order, mid_there = lax.optimization_barrier((copies, order, mid_there))
+    mid_rest = lax.ppermute(mid_there, "dp", swap)
     hidden = exchange(copies, "dp", same_y)
     rows = n_dp * n_tp
     spots = jnp.arange(rows)
@@ -325,7 +323,7 @@
     own_count = rows // n_tp
     listed = order.reshape(n_tp, 2, own_count // 2).swapaxes(0, 1).reshape(rows)
     pick = (listed[:, None] == spot_rows[None, :]).astype(BF)
-    hidden, pick = lax.optimization_barrier((hidden, pick))
+    hidden, pick, mid_rest = lax.optimization_barrier((hidden, pick, mid_rest))
     width = down_weight.shape[1]
     ffn_terms = call(
         down_kernel,

time: 157 us -> 153 us (0.975)
  blocking collectives: 0 us -> 10.8 us
  waiting for transfers between devices: 75.4 us -> 65.2 us
  starting transfers between devices: 62.9 us -> 59.3 us
    all_to_all x0 -> x1, blocking collectives: none -> 10.8 us  [exchange(): lax.all_to_all(array, axis, split_axis=0, concat_axis=0, axis_index_group...]
    all_to_all x7 -> x6, waiting for transfers between devices: 62 us -> 54.2 us  [exchange(): lax.all_to_all(array, axis, split_axis=0, concat_axis=0, axis_index_group...]
    all_to_all x7 -> x6, starting transfers between devices: 46.5 us -> 41.2 us  [exchange(): lax.all_to_all(array, axis, split_axis=0, concat_axis=0, axis_index_group...]
  transfers between devices with their start and end apart: 14 -> 13, of which waited for: 12 -> 10; matrix products, arithmetic and copies ran while one was open for 1% -> 1% of each run, Pallas kernels for 1% -> 1%
where the time goes in v7:
time: 153 us; the launch traced here: 151 us
  waiting for transfers between devices  65.2 us (43%)
  starting transfers between devices  59.3 us (39%)
  Pallas kernels  11.5 us (8%)
  blocking collectives  10.8 us (7%)
  local copies, waits for them, and re-layouts  1.64 us (1%)
    all_to_all x6, waiting for transfers between devices, exchange(): lax.all_to_all(array, axis, split_axis=0, concat_axis=0, axis_index_group...  54.2 us
    all_to_all x6, starting transfers between devices, exchange(): lax.all_to_all(array, axis, split_axis=0, concat_axis=0, axis_index_group...  41.2 us
    all_to_all x1, blocking collectives, exchange(): lax.all_to_all(array, axis, split_axis=0, concat_axis=0, axis_index_group...  10.8 us
    ppermute x1, waiting for transfers between devices, local(): theirs = lax.ppermute(sums.astype(BF), 'dp', across_y)  7.12 us
    ppermute x1, starting transfers between devices, local(): theirs = lax.ppermute(sums.astype(BF), 'dp', across_y)  5.43 us
    pallas_call x1, Pallas kernels, local(): pl.pallas_call(attend_kernel, out_shape=jax.ShapeDtypeStruct((2 * n_tp, q...  4.2 us
  transfers between devices with their start and end apart: 13, of which 10 were waited for; matrix products, arithmetic and copies ran while one was open for 1% of the time, Pallas kernels for 1%

profile of v7, /device:TPU:6, one launch (start us, length us, event | category | flops | bytes accessed | tf_op | source)
XLA Modules:
  0.0 150.9 jit_solution(6859411734149084958)
XLA Ops:
  0.7 4.2 %shard_map.118 = bf16[64,4,512]{2,1,0:T(4,128)(2,1)} custom-call(s32[1]{0:T(128)S(6)} %copy.18.length_ref, bf16[576,128]{1,0:T(8,128)(2,1)} %bitcast.37, bf16[1,576]{1,0:T(2,128)(2,1)} %new_hbm.1, bf16[576,1792]{1,0:T(8,128)(2,1)} %bitcast.35), custom_call_target="tpu_custom_call" | custom-call | tf_op jit(solution)/shard_map/pallas_call | solution.py:241
  4.9 16.7 %all-to-all-start = ((bf16[64,4,512]{2,1,0:T(4,128)(2,1)}), bf16[64,4,512]{2,1,0:T(4,128)(2,1)S(1)}, u32[]{:S(2)}, u32[]{:S(2)}) async-start(bf16[64,4,512]{2,1,0:T(4,128)(2,1)} %shard_map.118), calls=%async_computation | async-start | bytes 524288 | tf_op jit(solution)/shard_map/all_to_all | solution.py:190
  21.6 1.9 %collective-permute-start = (bf16[16,448]{1,0:T(8,128)(2,1)}, bf16[16,448]{1,0:T(8,128)(2,1)S(1)}, u32[]{:S(2)}, u32[]{:S(2)}) collective-permute-start(bf16[16,448]{1,0:T(8,128)(2,1)} %param.19), channel_id=1, source_target_pairs={{0,32},{32,0},{64,96},{96,64},{128,160},{160,128},{192,224},{224,1... | collective-permute-start | bytes 43016 | tf_op jit(solution)/shard_map/ppermute | solution.py:261
  23.6 2.4 %collective-permute-start.1 = (bf16[512,448]{0,1:T(8,128)(2,1)}, bf16[512,448]{0,1:T(8,128)(2,1)S(1)}, u32[]{:S(2)}, u32[]{:S(2)}) collective-permute-start(bf16[512,448]{0,1:T(8,128)(2,1)} %param.18), channel_id=1, source_target_pairs={{0,32},{32,0},{64,96},{96,64},{128,160},{160,128},{192,224},{224,1... | collective-permute-start | bytes 1376264 | tf_op jit(solution)/shard_map/ppermute | solution.py:238
  26.0 1.1 copy_bitcast_fusion.w_ref
  27.1 9.6 %all-to-all-done.owned_ref = bf16[64,4,512]{2,1,0:T(4,128)(2,1)S(1)} async-done(((bf16[64,4,512]{2,1,0:T(4,128)(2,1)}), bf16[64,4,512]{2,1,0:T(4,128)(2,1)S(1)}, u32[]{:S(2)}, u32[]{:S(2)}) %all-to-all-start) | async-done | bytes 262176 | tf_op jit(solution)/shard_map/all_to_all | solution.py:190
  36.7 1.1 shard_map.119
  37.8 4.8 %all-to-all-start.1 = ((bf16[4,64,512]{2,1,0:T(8,128)(2,1)}), bf16[4,64,512]{2,1,0:T(8,128)(2,1)S(1)}, u32[]{:S(2)}, u32[]{:S(2)}) async-start(bf16[4,64,512]{2,1,0:T(8,128)(2,1)} %shard_map.119), calls=%async_computation.1 | async-start | bytes 524288 | tf_op jit(solution)/shard_map/all_to_all | solution.py:190
  42.7 4.5 %all-to-all-done.1 = bf16[4,64,512]{2,1,0:T(8,128)(2,1)S(1)} async-done(((bf16[4,64,512]{2,1,0:T(8,128)(2,1)}), bf16[4,64,512]{2,1,0:T(8,128)(2,1)S(1)}, u32[]{:S(2)}, u32[]{:S(2)}) %all-to-all-start.1) | async-done | bytes 262176 | tf_op jit(solution)/shard_map/all_to_all | solution.py:190
  47.2 1.3 shard_map.120
  48.5 3.9 %all-to-all-start.2 = ((bf16[32,8,896]{2,1,0:T(8,128)(2,1)}), bf16[32,8,896]{2,1,0:T(8,128)(2,1)S(1)}, u32[]{:S(2)}, u32[]{:S(2)}) async-start(bf16[32,8,896]{2,1,0:T(8,128)(2,1)} %bitcast.9), calls=%async_computation.2 | async-start | bytes 917504 | tf_op jit(solution)/shard_map/all_to_all | solution.py:190
  52.4 1.9 %collective-permute-start.2 = (bf16[448,576]{1,0:T(8,128)(2,1)S(1)}, bf16[448,576]{1,0:T(8,128)(2,1)S(1)}, u32[]{:S(2)}, u32[]{:S(2)}) collective-permute-start(bf16[448,576]{1,0:T(8,128)(2,1)S(1)} %copy-done), channel_id=1, source_target_pairs={{0,32},{32,0},{64,96},{96,64},{128,160},{160,128},{192,224},{224,1... | collective-permute-start | bytes 1548296 | tf_op jit(solution)/shard_map/ppermute | solution.py:291
  54.4 2.4 %collective-permute-start.3 = (bf16[448,576]{1,0:T(8,128)(2,1)S(1)}, bf16[448,576]{1,0:T(8,128)(2,1)S(1)}, u32[]{:S(2)}, u32[]{:S(2)}) collective-permute-start(bf16[448,576]{1,0:T(8,128)(2,1)S(1)} %copy-done.1), channel_id=1, source_target_pairs={{0,32},{32,0},{64,96},{96,64},{128,160},{160,128},{192,224},{224,1... | collective-permute-start | bytes 1548296 | tf_op jit(solution)/shard_map/ppermute | solution.py:292
  56.8 1.6 %collective-permute-done.3.u2_ref = bf16[448,576]{1,0:T(8,128)(2,1)S(1)} collective-permute-done((bf16[448,576]{1,0:T(8,128)(2,1)S(1)}, bf16[448,576]{1,0:T(8,128)(2,1)S(1)}, u32[]{:S(2)}, u32[]{:S(2)}) %collective-permute-start.3) | collective-permute-done | bytes 516128 | tf_op jit(solution)/shard_map/ppermute | solution.py:292
  58.4 7.4 %all-to-all-done.2 = bf16[32,8,896]{2,1,0:T(8,128)(2,1)S(1)} async-done(((bf16[32,8,896]{2,1,0:T(8,128)(2,1)}), bf16[32,8,896]{2,1,0:T(8,128)(2,1)S(1)}, u32[]{:S(2)}, u32[]{:S(2)}) %all-to-all-start.2) | async-done | bytes 458784 | tf_op jit(solution)/shard_map/all_to_all | solution.py:190
  65.8 0.9 shard_map.121
  66.6 4.4 %all-to-all-start.3 = ((bf16[32,8,896]{2,1,0:T(8,128)(2,1)}), bf16[32,8,896]{2,1,0:T(8,128)(2,1)S(1)}, u32[]{:S(2)}, u32[]{:S(2)}) async-start(bf16[32,8,896]{2,1,0:T(8,128)(2,1)} %shard_map.121), calls=%async_computation.3 | async-start | bytes 917504 | tf_op jit(solution)/shard_map/all_to_all | solution.py:190
  71.1 1.9 %collective-permute-start.4 = (bf16[448]{0:T(512)(128)(2,1)S(1)}, bf16[448]{0:T(512)(128)(2,1)S(1)}, u32[]{:S(2)}, u32[]{:S(2)}) collective-permute-start(bf16[448]{0:T(512)(128)(2,1)S(1)} %copy-done.6), channel_id=1, source_target_pairs={{0,32},{32,0},{64,96},{96,64},{128,160},{160,128},{192,224},{224,1... | collective-permute-start | bytes 2696 | tf_op jit(solution)/shard_map/ppermute | solution.py:239
  73.0 1.1 collective-permute-done.4
  74.2 12.1 %all-to-all-done.3 = bf16[32,8,896]{2,1,0:T(8,128)(2,1)S(1)} async-done(((bf16[32,8,896]{2,1,0:T(8,128)(2,1)}), bf16[32,8,896]{2,1,0:T(8,128)(2,1)S(1)}, u32[]{:S(2)}, u32[]{:S(2)}) %all-to-all-start.3) | async-done | bytes 458784 | tf_op jit(solution)/shard_map/all_to_all | solution.py:190
  86.3 1.0 shard_map.122
  87.3 10.8 %all_to_all.49 = bf16[4,592,128]{2,1,0:T(8,128)(2,1)S(1)} all-to-all(bf16[4,592,128]{2,1,0:T(8,128)(2,1)S(1)} %shard_map.122), channel_id=1, replica_groups={{0,64,128,192},{32,96,160,224},{256,320,384,448},{288,352,416,480},{1,6..., dimensions={0} | all-to-all | bytes 1212416 | tf_op jit(solution)/shard_map/all_to_all | solution.py:190
  98.2 5.4 %collective-permute-start.5 = (bf16[592,128]{1,0:T(8,128)(2,1)S(1)}, bf16[592,128]{1,0:T(8,128)(2,1)S(1)}, u32[]{:S(2)}, u32[]{:S(2)}) collective-permute-start(bf16[592,128]{1,0:T(8,128)(2,1)S(1)} %convert_element_type.21), channel_id=1, source_target_pairs={{0,256},{32,288},{64,320},{96,352},{128,384},{160,416},{192,448},{... | collective-permute-start | bytes 454664 | tf_op jit(solution)/shard_map/ppermute | solution.py:309
  103.8 7.1 %collective-permute-done.5.theirs_ref = bf16[592,128]{1,0:T(8,128)(2,1)S(1)} collective-permute-done((bf16[592,128]{1,0:T(8,128)(2,1)S(1)}, bf16[592,128]{1,0:T(8,128)(2,1)S(1)}, u32[]{:S(2)}, u32[]{:S(2)}) %collective-permute-start.5) | collective-permute-done | bytes 151584 | tf_op jit(solution)/shard_map/ppermute | solution.py:309
  111.0 1.2 shard_map.123
  112.1 5.5 %all-to-all-start.5 = ((bf16[8,288,128]{2,1,0:T(8,128)(2,1)}), bf16[8,288,128]{2,1,0:T(8,128)(2,1)S(1)}, u32[]{:S(2)}, u32[]{:S(2)}) async-start(bf16[8,288,128]{2,1,0:T(8,128)(2,1)} %shard_map.123), calls=%async_computation.5 | async-start | bytes 1179648 | tf_op jit(solution)/shard_map/all_to_all | solution.py:190
  117.9 2.1 %collective-permute-start.6 = (bf16[256,448]{1,0:T(8,128)(2,1)S(1)}, bf16[256,448]{1,0:T(8,128)(2,1)S(1)}, u32[]{:S(2)}, u32[]{:S(2)}) collective-permute-start(bf16[256,448]{1,0:T(8,128)(2,1)S(1)} %slice.16), channel_id=1, source_target_pairs={{0,32},{32,0},{64,96},{96,64},{128,160},{160,128},{192,224},{224,1... | collective-permute-start | bytes 688136 | tf_op jit(solution)/shard_map/ppermute | solution.py:317
  120.1 1.2 collective-permute-done.6
  121.3 5.3 %all-to-all-done.5.hidden_ref = bf16[8,288,128]{2,1,0:T(8,128)(2,1)S(1)} async-done(((bf16[8,288,128]{2,1,0:T(8,128)(2,1)}), bf16[8,288,128]{2,1,0:T(8,128)(2,1)S(1)}, u32[]{:S(2)}, u32[]{:S(2)}) %all-to-all-start.5) | async-done | bytes 589856 | tf_op jit(solution)/shard_map/all_to_all | solution.py:190
  126.6 1.8 %shard_map.124 = bf16[256,896]{1,0:T(8,128)(2,1)} custom-call(bf16[512,512]{1,0:T(8,128)(2,1)S(1)} %compare_convert_fusion.pick_ref, bf16[8,288,128]{2,1,0:T(8,128)(2,1)S(1)} %all-to-all-done.5.hidden_ref, bf16[448,576]{1,0:T(8,128)(2,1)S(1)} %bitcast.32), custom_call_target="tpu_custom_call" | custom-call | flops 566231040 | bytes 2097152 | tf_op jit(solution)/shard_map/pallas_call | solution.py:328
  128.4 5.9 %all-to-all-start.6 = ((bf16[32,8,896]{2,1,0:T(8,128)(2,1)}), bf16[32,8,896]{2,1,0:T(8,128)(2,1)S(1)}, u32[]{:S(2)}, u32[]{:S(2)}) async-start(bf16[32,8,896]{2,1,0:T(8,128)(2,1)} %bitcast.15), calls=%async_computation.6 | async-start | bytes 917504 | tf_op jit(solution)/shard_map/all_to_all | solution.py:190
  134.8 15.3 %all-to-all-done.6 = bf16[32,8,896]{2,1,0:T(8,128)(2,1)S(1)} async-done(((bf16[32,8,896]{2,1,0:T(8,128)(2,1)}), bf16[32,8,896]{2,1,0:T(8,128)(2,1)S(1)}, u32[]{:S(2)}, u32[]{:S(2)}) %all-to-all-start.6) | async-done | bytes 458784 | tf_op jit(solution)/shard_map/all_to_all | solution.py:190
  (36 shorter events, 2.0 us)
Async XLA Ops:
  4.9 37.7 %copy-start.4 = (bf16[16,448]{1,0:T(8,128)(2,1)S(1)}, bf16[16,448]{1,0:T(8,128)(2,1)}, u32[]{:S(2)}) copy-start(bf16[16,448]{1,0:T(8,128)(2,1)} %param.19) | copy-start | bytes 43012
  4.9 42.3 %copy-start.3 = (bf16[512,448]{0,1:T(8,128)(2,1)S(1)}, bf16[512,448]{0,1:T(8,128)(2,1)}, u32[]{:S(2)}) copy-start(bf16[512,448]{0,1:T(8,128)(2,1)} %param.18) | copy-start | bytes 1376260
  4.9 31.8 %all-to-all-start = ((bf16[64,4,512]{2,1,0:T(4,128)(2,1)}), bf16[64,4,512]{2,1,0:T(4,128)(2,1)S(1)}, u32[]{:S(2)}, u32[]{:S(2)}) async-start(bf16[64,4,512]{2,1,0:T(4,128)(2,1)} %shard_map.118), calls=%async_computation | async-start | bytes 524288 | tf_op jit(solution)/shard_map/all_to_all | solution.py:190
  21.6 5.5 %collective-permute-start = (bf16[16,448]{1,0:T(8,128)(2,1)}, bf16[16,448]{1,0:T(8,128)(2,1)S(1)}, u32[]{:S(2)}, u32[]{:S(2)}) collective-permute-start(bf16[16,448]{1,0:T(8,128)(2,1)} %param.19), channel_id=1, source_target_pairs={{0,32},{32,0},{64,96},{96,64},{128,160},{160,128},{192,224},{224,1... | collective-permute-start | bytes 43016 | tf_op jit(solution)/shard_map/ppermute | solution.py:261
  23.6 19.1 %collective-permute-start.1 = (bf16[512,448]{0,1:T(8,128)(2,1)}, bf16[512,448]{0,1:T(8,128)(2,1)S(1)}, u32[]{:S(2)}, u32[]{:S(2)}) collective-permute-start(bf16[512,448]{0,1:T(8,128)(2,1)} %param.18), channel_id=1, source_target_pairs={{0,32},{32,0},{64,96},{96,64},{128,160},{160,128},{192,224},{224,1... | collective-permute-start | bytes 1376264 | tf_op jit(solution)/shard_map/ppermute | solution.py:238
  27.1 25.3 %copy-start = (bf16[448,576]{1,0:T(8,128)(2,1)S(1)}, bf16[448,576]{1,0:T(8,128)(2,1)}, u32[]{:S(2)}) copy-start(bf16[448,576]{1,0:T(8,128)(2,1)} %g1_ref) | copy-start | bytes 1548292
  27.1 27.3 %copy-start.1 = (bf16[448,576]{1,0:T(8,128)(2,1)S(1)}, bf16[448,576]{1,0:T(8,128)(2,1)}, u32[]{:S(2)}) copy-start(bf16[448,576]{1,0:T(8,128)(2,1)} %u1_ref) | copy-start | bytes 1548292
  37.8 9.4 %all-to-all-start.1 = ((bf16[4,64,512]{2,1,0:T(8,128)(2,1)}), bf16[4,64,512]{2,1,0:T(8,128)(2,1)S(1)}, u32[]{:S(2)}, u32[]{:S(2)}) async-start(bf16[4,64,512]{2,1,0:T(8,128)(2,1)} %shard_map.119), calls=%async_computation.1 | async-start | bytes 524288 | tf_op jit(solution)/shard_map/all_to_all | solution.py:190
  47.2 23.9 %copy-start.6 = (bf16[448]{0:T(512)(128)(2,1)S(1)}, bf16[448]{0:T(512)(128)(2,1)}, u32[]{:S(2)}) copy-start(bf16[448]{0:T(512)(128)(2,1)} %param.20) | copy-start | bytes 2692
  48.5 17.3 %all-to-all-start.2 = ((bf16[32,8,896]{2,1,0:T(8,128)(2,1)}), bf16[32,8,896]{2,1,0:T(8,128)(2,1)S(1)}, u32[]{:S(2)}, u32[]{:S(2)}) async-start(bf16[32,8,896]{2,1,0:T(8,128)(2,1)} %bitcast.9), calls=%async_computation.2 | async-start | bytes 917504 | tf_op jit(solution)/shard_map/all_to_all | solution.py:190
  52.4 4.4 %collective-permute-start.2 = (bf16[448,576]{1,0:T(8,128)(2,1)S(1)}, bf16[448,576]{1,0:T(8,128)(2,1)S(1)}, u32[]{:S(2)}, u32[]{:S(2)}) collective-permute-start(bf16[448,576]{1,0:T(8,128)(2,1)S(1)} %copy-done), channel_id=1, source_target_pairs={{0,32},{32,0},{64,96},{96,64},{128,160},{160,128},{192,224},{224,1... | collective-permute-start | bytes 1548296 | tf_op jit(solution)/shard_map/ppermute | solution.py:291
  54.4 4.0 %collective-permute-start.3 = (bf16[448,576]{1,0:T(8,128)(2,1)S(1)}, bf16[448,576]{1,0:T(8,128)(2,1)S(1)}, u32[]{:S(2)}, u32[]{:S(2)}) collective-permute-start(bf16[448,576]{1,0:T(8,128)(2,1)S(1)} %copy-done.1), channel_id=1, source_target_pairs={{0,32},{32,0},{64,96},{96,64},{128,160},{160,128},{192,224},{224,1... | collective-permute-start | bytes 1548296 | tf_op jit(solution)/shard_map/ppermute | solution.py:292
  66.6 19.7 %all-to-all-start.3 = ((bf16[32,8,896]{2,1,0:T(8,128)(2,1)}), bf16[32,8,896]{2,1,0:T(8,128)(2,1)S(1)}, u32[]{:S(2)}, u32[]{:S(2)}) async-start(bf16[32,8,896]{2,1,0:T(8,128)(2,1)} %shard_map.121), calls=%async_computation.3 | async-start | bytes 917504 | tf_op jit(solution)/shard_map/all_to_all | solution.py:190
  71.1 3.0 %collective-permute-start.4 = (bf16[448]{0:T(512)(128)(2,1)S(1)}, bf16[448]{0:T(512)(128)(2,1)S(1)}, u32[]{:S(2)}, u32[]{:S(2)}) collective-permute-start(bf16[448]{0:T(512)(128)(2,1)S(1)} %copy-done.6), channel_id=1, source_target_pairs={{0,32},{32,0},{64,96},{96,64},{128,160},{160,128},{192,224},{224,1... | collective-permute-start | bytes 2696 | tf_op jit(solution)/shard_map/ppermute | solution.py:239
  98.1 19.5 %copy-start.5 = (s32[512]{0:T(512)S(1)}, s32[512]{0:T(512)}, u32[]{:S(2)}) copy-start(s32[512]{0:T(512)} %param.16) | copy-start | bytes 6148
  98.2 28.4 %copy-start.2 = (bf16[576,448]{0,1:T(8,128)(2,1)S(1)}, bf16[576,448]{0,1:T(8,128)(2,1)}, u32[]{:S(2)}) copy-start(bf16[576,448]{0,1:T(8,128)(2,1)} %param.23) | copy-start | bytes 1548292
  98.2 12.7 %collective-permute-start.5 = (bf16[592,128]{1,0:T(8,128)(2,1)S(1)}, bf16[592,128]{1,0:T(8,128)(2,1)S(1)}, u32[]{:S(2)}, u32[]{:S(2)}) collective-permute-start(bf16[592,128]{1,0:T(8,128)(2,1)S(1)} %convert_element_type.21), channel_id=1, source_target_pairs={{0,256},{32,288},{64,320},{96,352},{128,384},{160,416},{192,448},{... | collective-permute-start | bytes 454664 | tf_op jit(solution)/shard_map/ppermute | solution.py:309
  112.1 14.5 %all-to-all-start.5 = ((bf16[8,288,128]{2,1,0:T(8,128)(2,1)}), bf16[8,288,128]{2,1,0:T(8,128)(2,1)S(1)}, u32[]{:S(2)}, u32[]{:S(2)}) async-start(bf16[8,288,128]{2,1,0:T(8,128)(2,1)} %shard_map.123), calls=%async_computation.5 | async-start | bytes 1179648 | tf_op jit(solution)/shard_map/all_to_all | solution.py:190
  117.9 3.4 %collective-permute-start.6 = (bf16[256,448]{1,0:T(8,128)(2,1)S(1)}, bf16[256,448]{1,0:T(8,128)(2,1)S(1)}, u32[]{:S(2)}, u32[]{:S(2)}) collective-permute-start(bf16[256,448]{1,0:T(8,128)(2,1)S(1)} %slice.16), channel_id=1, source_target_pairs={{0,32},{32,0},{64,96},{96,64},{128,160},{160,128},{192,224},{224,1... | collective-permute-start | bytes 688136 | tf_op jit(solution)/shard_map/ppermute | solution.py:317
  128.4 21.7 %all-to-all-start.6 = ((bf16[32,8,896]{2,1,0:T(8,128)(2,1)}), bf16[32,8,896]{2,1,0:T(8,128)(2,1)S(1)}, u32[]{:S(2)}, u32[]{:S(2)}) async-start(bf16[32,8,896]{2,1,0:T(8,128)(2,1)} %bitcast.15), calls=%async_computation.6 | async-start | bytes 917504 | tf_op jit(solution)/shard_map/all_to_all | solution.py:190
